TPU v7x, 32 devices: a whole 2x2x4 slice. The times are simulated.
32 devices in a mesh: tm: 8 (over z, y), space: 4 (over x, core).
Axes of the slice: x: 2, y: 2, z: 4, core: 2. Of those that a mesh axis runs over, the one named last changes fastest.
Arguments:
- forcing: float32 [32, 128, 128, 128], P('tm', 'space'), may hold values from -6 to 6
- coarse_guess: float32 [8, 128, 128, 128], P('tm', 'space'), may hold values from -6 to 6
- initial: float32 [128, 128, 128], P('space'), may hold values from -6 to 6
Outputs:
- solution: float32 [32, 128, 128, 128], P('tm', 'space')
- residual: float32 [8, 128, 128, 128], P('tm', None, 'space')
All inputs are finite; a program needn't handle non-finite values.
Results may differ from a plain program's by a relative error of at most 0.00007.
Values sent between devices are 32-bit elements; how exact they have to be, the bound alone decides.
No kernel may reach another device: no remote copies, remote signals or barrier semaphores. Data moves between devices by JAX's collectives and lax.ppermute only.
A program may use at most 192 MiB of HBM per device.

v0:
```python
import jax
import jax.numpy as jnp
from jax import lax
from jax.sharding import PartitionSpec as P

time_step = 0.5
highest = lax.Precision.HIGHEST


def from_behind(shard, axis, by):
    devices = lax.axis_size(axis)
    return lax.ppermute(shard, axis, [(i, (i + by) % devices) for i in range(devices)])


def passed_along(value, axis, steps):
    count = lax.axis_size(axis)
    first, last = (max(0, -steps), min(count, count - steps))
    return lax.ppermute(value, axis, [(source, source + steps) for source in range(first, last)])


def prefix_2(part, axis, combine, identity):
    place = lax.axis_index(axis)
    gathered = jax.tree.map(lambda a: lax.all_gather(a, axis), part)
    state = jax.tree.map(lambda a, e: jnp.zeros_like(a) + jnp.asarray(e, a.dtype), part, identity)

    def one(step, state):
        return combine(
            state, jax.tree.map(lambda a: lax.dynamic_index_in_dim(a, step, 0, False), gathered)
        )

    return lax.fori_loop(0, place, one, state)


def sine_table(length):
    ladder = jnp.arange(1, length + 1, dtype=jnp.float32)
    return jnp.sqrt(2.0 / (length + 1)) * jnp.sin(
        jnp.pi * ladder[:, None] * ladder[None, :] / (length + 1)
    )


def eigen_values(length):
    ladder = jnp.arange(1, length + 1, dtype=jnp.float32)
    return -4.0 * jnp.sin(jnp.pi * ladder / (2 * (length + 1))) ** 2


def per_device(forcing, coarse_guess, initial):
    steps = forcing.shape[0]
    width_x = initial.shape[0] * lax.axis_size("space")
    width_y = initial.shape[1]
    width_z = initial.shape[2]
    slice_y = width_y // lax.axis_size("space")
    table_x = sine_table(width_x)
    table_y = sine_table(width_y)
    table_z = sine_table(width_z)
    offset = lax.axis_index("space") * slice_y
    local_y = lax.dynamic_slice_in_dim(eigen_values(width_y), offset, slice_y)
    spectrum = (
        eigen_values(width_x)[:, None, None]
        + local_y[None, :, None]
        + eigen_values(width_z)[None, None, :]
    )
    implicit = 1.0 - 0.5 * time_step * spectrum
    fine_rate = (1.0 + 0.5 * time_step * spectrum) / implicit
    wide_step = 0.5 * steps * time_step
    coarse_rate = (1.0 + wide_step * spectrum) / (1.0 - wide_step * spectrum)
    leading = (lax.axis_index("tm") == 0).astype(jnp.float32)
    fields = jnp.concatenate([forcing, coarse_guess, initial[None]], axis=0)
    fields = jnp.einsum("bxyz,zr->bxyr", fields, table_z, precision=highest)
    fields = jnp.einsum("bxyr,yq->bxqr", fields, table_y, precision=highest)
    spectra = jnp.einsum(
        "bxqr,xp->bpqr",
        lax.all_to_all(fields, "space", split_axis=2, concat_axis=1, tiled=True),
        table_x,
        precision=highest,
    )
    anchor = leading * spectra[steps + 1]
    begin = from_behind(spectra[steps], "tm", 1)
    source = spectra[:steps] * (time_step / implicit)

    def relax_steps(starting):
        current = starting
        values = []
        for number in range(steps - 1):
            current = fine_rate * current + source[number]
            values.append(current)
        return values

    coarse_value = fine_rate * relax_steps(begin)[-1] + source[steps - 1]
    second = passed_along(coarse_value, "tm", 1) + anchor
    residual = fine_rate * relax_steps(second)[-1] + source[steps - 1] - coarse_value

    def combine(earlier, later):
        return (earlier[0] * later[0], later[0] * earlier[1] + later[1])

    identity = (jnp.ones_like(residual), jnp.zeros_like(residual))
    powers, prefix = prefix_2((coarse_rate, residual), "tm", combine, identity)
    corrected = coarse_value + (coarse_rate * prefix + residual)
    third = second + prefix
    points = relax_steps(third) + [corrected]
    fields = jnp.stack(points, axis=0)
    fields = jnp.einsum("bpqr,px->bxqr", fields, table_x, precision=highest)
    pieces = lax.all_to_all(fields, "space", split_axis=1, concat_axis=2, tiled=True)
    pieces = jnp.einsum("bxqr,qy->bxyr", pieces, table_y, precision=highest)
    return (jnp.einsum("bxyr,rz->bxyz", pieces, table_z, precision=highest), residual[None])


def solution(mesh):
    placed = (P("tm", "space", None, None), P("tm", "space", None, None), P("space", None, None))
    return jax.shard_map(
        per_device,
        mesh=mesh,
        in_specs=placed,
        out_specs=(P("tm", "space", None, None), P("tm", None, "space", None)),
        check_vma=False,
    )
```

profile of v0, /device:TPU:25, one launch (start us, length us, event | category | flops | bytes accessed | tf_op | source)
XLA Modules:
  0.0 753.1 jit_solution(15380561479222114512)
XLA Ops:
  7.2 0.0 all-gather.4.cloned.1.call-start
  7.3 0.1 dynamic_slice.12
  7.3 0.1 broadcast_add_fusion
  7.4 0.1 copy.40
  7.5 0.0 copy-start.4
  7.5 1.7 fusion.24
  9.2 0.0 all-gather.4.cloned.1.call-update
  9.2 0.0 all-gather.6.cloned.1.call-start
  9.3 0.4 copy-done.4
  9.7 13.4 %fusion.1 = f32[6,32,128,128]{3,2,1,0:T(8,128)S(1)} fusion(f32[1,32,128,128]{3,2,1,0:T(8,128)S(1)} %bitcast.113, f32[1,32,128,128]{3,2,1,0:T(8,128)} %param.6, f32[4,32,128,128]{3,2,1,0:T(8,128)} %param.5, f32[128]{0:T(128)S(1)} %get-tuple-element.88, f32[128]{0:T(128)S(1)} %get-tuple-element.89), kind=kOutput, calls=%fused_computation.4 | convolution fusion | flops 4838178816 | bytes 25166848 | tf_op jit(solution)/shard_map/bxyz,zr->bxyr/dot_general | solution.py:68
  23.2 14.7 %convolution_bitcast_fusion.1 = f32[6,32,128,128]{3,2,1,0:T(8,128)} fusion(f32[6,32,128,128]{3,2,1,0:T(8,128)S(1)} %fusion.1, f32[128]{0:T(128)S(1)} %get-tuple-element.88, f32[128]{0:T(128)S(1)} %get-tuple-element.89), kind=kOutput, calls=%fused_computation.22 | convolution fusion | flops 4831887360 | bytes 25166848 | tf_op jit(solution)/shard_map/bxyr,yq->bxqr/dot_general | solution.py:69
  37.8 16.4 %copy.37 = f32[6,32,128,128]{3,1,0,2:T(8,128)} copy(f32[6,32,128,128]{3,2,1,0:T(8,128)} %convolution_bitcast_fusion.1) | data formatting | bytes 25165824 | tf_op jit(solution)/shard_map/bxyr,yq->bxqr/transpose | solution.py:69
  54.2 147.5 %all_to_all.36 = f32[6,32,128,128]{3,1,0,2:T(8,128)} all-to-all(f32[6,32,128,128]{3,1,0,2:T(8,128)} %copy.37), channel_id=1, replica_groups=mesh['tm'=8,'space'=4] {'space'}, dimensions={2} | all-to-all | bytes 25165824 | tf_op jit(solution)/shard_map/all_to_all | solution.py:72
  201.7 11.4 %copy.38 = f32[6,32,4,32,128]{4,1,2,3,0:T(8,128)} copy(f32[6,32,4,32,128]{4,1,0,3,2:T(8,128)} %bitcast.107) | data formatting | bytes 25165824 | tf_op jit(solution)/shard_map/all_to_all | solution.py:72
  213.1 14.4 %convolution_bitcast_fusion = f32[6,128,32,128]{3,1,2,0:T(8,128)S(1)} fusion(f32[6,128,32,128]{3,1,2,0:T(8,128)} %bitcast.108, f32[128]{0:T(128)S(1)} %get-tuple-element.88, f32[128]{0:T(128)S(1)} %get-tuple-element.89), kind=kOutput, calls=%fused_computation.21 | convolution fusion | flops 4831887360 | bytes 25166848 | tf_op jit(solution)/shard_map/bxqr,xp->bpqr/dot_general | solution.py:70
  227.4 0.0 copy-start.1
  227.5 0.1 slice_bitcast_fusion.4
  227.6 1.3 collective-permute-start
  228.9 3.0 copy-done.1
  231.9 0.6 fusion.22
  232.5 4.7 slice_multiply_fusion
  237.2 0.0 copy-start
  237.2 44.4 %collective-permute-done = f32[128,32,128]{2,0,1:T(8,128)S(1)} collective-permute-done((f32[128,32,128]{2,0,1:T(8,128)S(1)}, f32[128,32,128]{2,0,1:T(8,128)S(1)}, u32[]{:S(2)}, u32[]{:S(2)}) %collective-permute-start) | collective-permute-done | bytes 2097184 | tf_op jit(solution)/shard_map/ppermute | solution.py:12
  281.6 1.4 multiply_add_fusion.2
  283.1 0.0 copy-done
  283.1 0.0 copy-start.3
  283.1 1.9 collective-permute-start.1
  285.0 47.4 %collective-permute-done.1 = f32[128,32,128]{2,0,1:T(8,128)} collective-permute-done((f32[128,32,128]{2,0,1:T(8,128)S(1)}, f32[128,32,128]{2,0,1:T(8,128)}, u32[]{:S(2)}, u32[]{:S(2)}) %collective-permute-start.1) | collective-permute-done | bytes 2097184 | tf_op jit(solution)/shard_map/ppermute | solution.py:18
  332.4 6.5 add_subtract_fusion.2
  339.0 0.0 copy-done.3
  339.0 0.0 all-gather.6.cloned.1.call-update
  339.0 0.0 all-gather.4.cloned.1.call-done
  339.0 227.0 %all-gather.6.cloned.1.call-done = f32[1024,32,128]{2,0,1:T(8,128)} async-done(((f32[128,32,128]{2,0,1:T(8,128)}), f32[1024,32,128]{2,0,1:T(8,128)}) %all-gather.6.cloned.1.call-update) | async-done | bytes 16777232 | tf_op jit(solution)/shard_map/all_gather | solution.py:23
  566.0 0.2 broadcast_in_dim.5
  566.3 31.5 %while.12 = (s32[]{:T(128)}, f32[128,32,128]{2,1,0:T(8,128)S(1)}, s32[]{:T(128)}, f32[8,128,32,128]{3,2,1,0:T(8,128)}, f32[8,128,32,128]{3,1,0,2:T(8,128)}, /*index=5*/s32[]{:T(128)}, s32[]{:T(128)}, s32[]{:T(128)}) while((s32[]{:T(128)}, f32[128,32,128]{2,1,0:T(8,128)S(1)}, s32[]{:T(128)}, f32[8,128,32,128]{3,2,1,0:T(8,128)}, ...), condition=%wide.region_1.2_spmd, body=%wide.region_0.1_spmd.sunk | while | flops 1048581 | bytes 12583047 | solution.py:31
  566.3 1.7 constant_dynamic-slice_fusion.2
  568.1 3.5 fusion.82
  571.6 1.7 constant_dynamic-slice_fusion.2
  573.3 3.5 fusion.82
  576.8 1.7 constant_dynamic-slice_fusion.2
  578.6 3.5 fusion.82
  582.1 1.7 constant_dynamic-slice_fusion.2
  583.8 3.5 fusion.82
  587.3 1.7 constant_dynamic-slice_fusion.2
  589.0 3.5 fusion.82
  592.5 1.7 constant_dynamic-slice_fusion.2
  594.3 3.5 fusion.82
  597.8 6.5 fusion.32
  604.3 3.1 add_bitcast_fusion
  607.3 8.8 %fusion.17 = f32[4,128,32,128]{3,1,2,0:T(8,128)S(1)} fusion(f32[1,128,32,128]{3,1,2,0:T(8,128)S(1)} %get-tuple-element.87, f32[1,128,32,128]{3,1,2,0:T(8,128)S(1)} %add_bitcast_fusion, f32[1,128,32,128]{3,1,2,0:T(8,128)S(1)} %get-tuple-element.85, f32[1,128,32,128]{3,1,2,0:T(8,128)S(1)} %bitcast.111, f32[128]{0:T(128)S(1)} %get-tuple-element.88, ...), kind=kOutput, calls=%fused_computation.26 | convolution fusion | flops 3227566080 | bytes 16778240 | tf_op jit(solution)/shard_map/bpqr,px->bxqr/dot_general | solution.py:101
  616.1 8.4 %copy.45 = f32[4,128,32,128]{3,2,0,1:T(8,128)} copy(f32[4,128,32,128]{3,1,2,0:T(8,128)S(1)} %fusion.17) | data formatting | bytes 16777216 | tf_op jit(solution)/shard_map/bpqr,px->bxqr/transpose | solution.py:101
  624.6 0.0 copy-start.2
  624.6 6.2 all-to-all-start.1
  630.8 0.0 copy-done.2
  630.8 2.5 copy.49
  633.3 89.8 %all-to-all-done.1 = f32[4,128,32,128]{3,2,0,1:T(8,128)} async-done(((f32[4,128,32,128]{3,2,0,1:T(8,128)}), f32[4,128,32,128]{3,2,0,1:T(8,128)}, u32[]{:S(2)}, u32[]{:S(2)}) %all-to-all-start.1) | async-done | bytes 8388640 | tf_op jit(solution)/shard_map/all_to_all | solution.py:102
  723.1 4.4 copy.47
  727.5 8.8 %fusion.38 = f32[128,4,32,128]{3,0,2,1:T(8,128)S(1)} fusion(f32[4,32,128,128]{3,2,1,0:T(8,128)S(1)} %bitcast.110, f32[128]{0:T(128)S(1)} %get-tuple-element.88, f32[128]{0:T(128)S(1)} %get-tuple-element.89), kind=kOutput, calls=%fused_computation.58 | convolution fusion | flops 3221274624 | bytes 16778240 | tf_op jit(solution)/shard_map/bxqr,qy->bxyr/dot_general | solution.py:103
  736.3 9.7 %fusion.15 = f32[4,32,128,128]{3,2,1,0:T(8,128)} fusion(f32[128,4,32,128]{3,0,2,1:T(8,128)S(1)} %fusion.38, f32[128]{0:T(128)S(1)} %get-tuple-element.88, f32[128]{0:T(128)S(1)} %get-tuple-element.89), kind=kOutput, calls=%fused_computation.19 | convolution fusion | flops 3221274624 | bytes 16778240 | tf_op jit(solution)/shard_map/bxyr,rz->bxyz/dot_general | solution.py:104
  (2 shorter events, 0.1 us)
Async XLA Ops:
  7.2 331.9 %all-gather.4.cloned.1.call-start = ((), (), s32[]{:S(2)}) async-start(), calls=%async_computation.2 | async-start | bytes 18874368 | tf_op jit(solution)/shard_map/all_gather | solution.py:23
  7.5 2.2 copy-start.4
  9.2 556.8 %all-gather.6.cloned.1.call-start = ((), (), s32[]{:S(2)}) async-start(), calls=%async_computation.3 | async-start | bytes 18874368 | tf_op jit(solution)/shard_map/all_gather | solution.py:23
  227.4 4.4 copy-start.1
  227.6 54.0 %collective-permute-start = (f32[128,32,128]{2,0,1:T(8,128)S(1)}, f32[128,32,128]{2,0,1:T(8,128)S(1)}, u32[]{:S(2)}, u32[]{:S(2)}) collective-permute-start(f32[128,32,128]{2,0,1:T(8,128)S(1)} %slice_bitcast_fusion.4), channel_id=1, source_target_pairs={{0,4},{4,8},{8,12},{12,16},{16,20},{20,24},{24,28},{28,0},{1,5},{5... | collective-permute-start | bytes 6291464 | tf_op jit(solution)/shard_map/ppermute | solution.py:12
  237.2 45.9 %copy-start = (f32[4,128,32,128]{3,1,2,0:T(8,128)}, f32[4,128,32,128]{3,1,2,0:T(8,128)S(1)}, u32[]{:S(2)}) copy-start(f32[4,128,32,128]{3,1,2,0:T(8,128)S(1)} %slice_multiply_fusion) | copy-start | bytes 25165828
  283.1 55.9 %copy-start.3 = (f32[128,32,128]{2,0,1:T(8,128)}, f32[128,32,128]{2,0,1:T(8,128)S(1)}, u32[]{:S(2)}) copy-start(f32[128,32,128]{2,0,1:T(8,128)S(1)} %multiply_add_fusion.2) | copy-start | bytes 6291460
  283.1 49.3 %collective-permute-start.1 = (f32[128,32,128]{2,0,1:T(8,128)S(1)}, f32[128,32,128]{2,0,1:T(8,128)}, u32[]{:S(2)}, u32[]{:S(2)}) collective-permute-start(f32[128,32,128]{2,0,1:T(8,128)S(1)} %multiply_add_fusion.2), channel_id=1, source_target_pairs={{0,4},{4,8},{8,12},{12,16},{16,20},{20,24},{24,28},{1,5},{5,9},{9,... | collective-permute-start | bytes 6291464 | tf_op jit(solution)/shard_map/ppermute | solution.py:18
  624.6 6.2 copy-start.2
  624.6 98.5 %all-to-all-start.1 = ((f32[4,128,32,128]{3,2,0,1:T(8,128)}), f32[4,128,32,128]{3,2,0,1:T(8,128)}, u32[]{:S(2)}, u32[]{:S(2)}) async-start(f32[4,128,32,128]{3,2,0,1:T(8,128)} %copy.45), calls=%async_computation.1 | async-start | bytes 16777216 | tf_op jit(solution)/shard_map/all_to_all | solution.py:102
Sparse Core Ops, SparseCore 0:
  10.7 226.8 all-gather.3
  339.1 226.8 all-gather.5
where the time goes:
time: 764 us; the launch traced here: 753 us
  waiting for transfers between devices  409 us (54%)
  blocking collectives  147 us (19%)
  matrix products  69.8 us (9%)
  local copies, waits for them, and re-layouts  57.5 us (8%)
  other arithmetic  45.5 us (6%)
  between operations  14.5 us (2%)
  starting transfers between devices  9.52 us (1%)
    all_gather x2, waiting for transfers between devices, prefix_2(): gathered = jax.tree.map(lambda a: lax.all_gather(a, axis), part)  227 us
    all_to_all x1, blocking collectives, per_device(): lax.all_to_all(fields, 'space', split_axis=2, concat_axis=1, tiled=True)  147 us
    all_to_all x1, waiting for transfers between devices, per_device(): lax.all_to_all(fields, 'space', split_axis=1, concat_axis=2, tiled=True)  89.8 us
    ppermute x1, waiting for transfers between devices, passed_along(): lax.ppermute(value, axis, [(source, source + steps) for source in range(f...  47.4 us
    ppermute x1, waiting for transfers between devices, from_behind(): lax.ppermute(shard, axis, [(i, (i + by) % devices) for i in range(devices)])  44.4 us
    add x6, other arithmetic, combine(): return (earlier[0] * later[0], later[0] * earlier[1] + later[1])  20.9 us
    transpose x1, local copies, waits for them, and re-layouts, per_device(): fields = jnp.einsum('bxyr,yq->bxqr', fields, table_y, precision=highest)  16.4 us
  transfers between devices with their start and end apart: 5, of which 4 were waited for; matrix products, arithmetic and copies ran while one was open for 11% of the time, Pallas kernels for 0%

commit v1 on v0

v1 whole, which is shorter than its diff:
```python
import jax
import jax.numpy as jnp
import ml_dtypes
import numpy as np
from jax import lax
from jax.experimental import pallas as pl
from jax.experimental.pallas import tpu as pltpu
from jax.sharding import Mesh
from jax.sharding import PartitionSpec as P

time_step = 0.5
half = 0.5 * time_step
high = lax.Precision.HIGH


def room(mebibytes):
    return pltpu.CompilerParams(vmem_limit_bytes=mebibytes << 20)


def cost(*arrays):
    moved = sum(int(np.prod(a.shape)) * 4 for a in arrays)
    return pl.CostEstimate(flops=moved * 400, bytes_accessed=2 * moved, transcendentals=0)


def sine_table(length):
    ladder = np.arange(1, length + 1, dtype=np.float64)
    table = np.sqrt(2.0 / (length + 1)) * np.sin(
        np.pi * ladder[:, None] * ladder[None, :] / (length + 1)
    )
    return table.astype(np.float32)


def eigen_values(length):
    ladder = np.arange(1, length + 1, dtype=np.float64)
    return -4.0 * np.sin(np.pi * ladder / (2 * (length + 1))) ** 2


def two_parts(table):
    upper = table.astype(ml_dtypes.bfloat16)
    return upper, (table - upper.astype(np.float32)).astype(ml_dtypes.bfloat16)


def right_table(table):
    upper, lower = two_parts(table)
    return np.block([[upper, lower], [upper, np.zeros_like(lower)]])


def left_table(table):
    upper, lower = two_parts(table)
    return np.block([[upper, upper], [lower, np.zeros_like(lower)]])


def pivot_table(planes, width_y, width_z, weight):
    cross = eigen_values(width_y)[:, None] + eigen_values(width_z)[None, :]
    diagonal = (1.0 + 2.0 * weight - weight * cross) / weight
    pivots = [1.0 / diagonal]
    for _ in range(planes // 2 - 1):
        pivots.append(1.0 / (diagonal - pivots[-1]))
    pivots.append(1.0 / (1.0 - pivots[-1] ** 2))
    return np.stack(pivots).astype(np.float32)


def split(values):
    upper = values.astype(jnp.bfloat16)
    return upper, (values - upper.astype(jnp.float32)).astype(jnp.bfloat16)


def times_right(values, table):
    width = values.shape[-1]
    both = jnp.dot(
        jnp.concatenate(split(values), axis=1), table, preferred_element_type=jnp.float32
    )
    return both[:, :width] + both[:, width:]


def times_left(table, values):
    both = jnp.dot(
        table, jnp.concatenate(split(values), axis=0), preferred_element_type=jnp.float32
    )
    width = values.shape[0]
    return both[:width] + both[width:]


def solve(planes, right, pivot, work, left_ghost, right_ghost, finish):
    middle = planes // 2
    lower, upper = left_ghost, right_ghost
    for k in range(middle):
        low, top = right(k), right(planes - 1 - k)
        low = low if lower is None else low + lower
        top = top if upper is None else top + upper
        factor = pivot(k)
        lower, upper = low * factor, top * factor
        if k < middle - 1:
            work[k] = lower
            work[planes - 1 - k] = upper
    factor, joint = pivot(middle - 1), pivot(middle)
    lower, upper = (lower + factor * upper) * joint, (upper + factor * lower) * joint
    finish(middle - 1, lower)
    finish(planes - middle, upper)
    for k in range(middle - 2, -1, -1):
        factor = pivot(k)
        lower = work[k] + factor * lower
        upper = work[planes - 1 - k] + factor * upper
        finish(k, lower)
        finish(planes - 1 - k, upper)


def transformed(block, z_ref, y_ref):
    count, width_y, width_z = block.shape
    lines = times_right(block.reshape(count * width_y, width_z), z_ref[...])
    step = 2 if count % 2 == 0 else 1
    out = []
    for i in range(0, count, step):
        wide = [lines[(i + j) * width_y : (i + j + 1) * width_y] for j in range(step)]
        wide = times_left(y_ref[...], jnp.concatenate(wide, axis=1))
        out += [wide[:, j * width_z : (j + 1) * width_z] for j in range(step)]
    return out


def front_kernel(x_steps, forcing_ref, z_ref, y_ref, pivot_ref, pushed_ref, out_ref, kept, work):
    steps, count, width_y, width_z = forcing_ref.shape
    planes, parts, own = kept.shape[1:4]
    some = out_ref.shape[0]
    turn = pl.program_id(0)

    @pl.when(turn < x_steps)
    def _():
        for n in range(steps):
            for i, plane in enumerate(transformed(forcing_ref[n], z_ref, y_ref)):
                pushed_ref[n, i] = plane
                kept[n, turn * count + i] = plane.reshape(parts, own, width_z)

    @pl.when(turn >= x_steps)
    def _():
        place = pl.ds((turn - x_steps) * some, some)
        for n in range(steps):

            def right(k):
                pushed = kept[n, k, place]
                return pushed if n == 0 else pushed + (2.0 / half) * out_ref[:, k]

            def finish(k, solved):
                if k == 0:
                    out_ref[:, planes + 2 * n] = solved
                if k == planes - 1:
                    out_ref[:, planes + 2 * n + 1] = solved
                out_ref[:, k] = solved if n == 0 else solved - out_ref[:, k]

            solve(planes, right, lambda k: pivot_ref[k], work, None, None, finish)


def front(forcing, z_right, y_left, pivots, parts):
    steps, planes, width_y, width_z = forcing.shape
    own = width_y // parts
    count = 4 if planes % 4 == 0 else 1
    some = 2 if parts % 2 == 0 else 1
    x_steps, q_steps = planes // count, parts // some
    early = lambda i: jnp.minimum(i, x_steps - 1)
    late = lambda i: jnp.maximum(i - x_steps, 0)
    total = planes + 2 * steps
    return pl.pallas_call(
        lambda *refs: front_kernel(x_steps, *refs),
        grid=(x_steps + q_steps,),
        out_shape=(
            jax.ShapeDtypeStruct(forcing.shape, jnp.float32),
            jax.ShapeDtypeStruct((parts, total, own, width_z), jnp.float32),
        ),
        in_specs=[
            pl.BlockSpec((steps, count, width_y, width_z), lambda i: (0, early(i), 0, 0)),
            pl.BlockSpec(z_right.shape, lambda i: (0, 0)),
            pl.BlockSpec(y_left.shape, lambda i: (0, 0)),
            pl.BlockSpec((planes // 2 + 1, some, own, width_z), lambda i: (0, late(i), 0, 0)),
        ],
        out_specs=(
            pl.BlockSpec((steps, count, width_y, width_z), lambda i: (0, early(i), 0, 0)),
            pl.BlockSpec((some, total, own, width_z), lambda i: (late(i), 0, 0, 0)),
        ),
        scratch_shapes=[
            pltpu.VMEM((steps, planes, parts, own, width_z), jnp.float32),
            pltpu.VMEM((planes, some, own, width_z), jnp.float32),
        ],
        cost_estimate=cost(forcing),
        compiler_params=room(24),
    )(forcing, z_right, y_left, pivots)


def opening_kernel(g_steps, pair_ref, guess_ref, initial_ref, z_ref, y_ref, out_ref):
    parts, count, own, width_z = out_ref.shape
    block = jnp.where(pl.program_id(0) < g_steps, guess_ref[...], initial_ref[...])
    for i, plane in enumerate(transformed(block, z_ref, y_ref)):
        out_ref[:, i] = plane.reshape(parts, own, width_z)


def opening_fields(guess, initial, z_right, y_left, pair, parts):
    planes, width_y, width_z = guess.shape
    share = planes // 2
    count = 8 if share % 8 == 0 else 1
    g_steps, a_steps = planes // count, share // count
    own = width_y // parts
    block = (count, width_y, width_z)
    whole = lambda a: pl.BlockSpec(a.shape, lambda i, p: (0, 0))
    return pl.pallas_call(
        lambda *refs: opening_kernel(g_steps, *refs),
        grid_spec=pltpu.PrefetchScalarGridSpec(
            num_scalar_prefetch=1,
            grid=(g_steps + a_steps,),
            in_specs=[
                pl.BlockSpec(block, lambda i, p: (jnp.minimum(i, g_steps - 1), 0, 0)),
                pl.BlockSpec(
                    block, lambda i, p: (p[0] * a_steps + jnp.maximum(i - g_steps, 0), 0, 0)
                ),
                whole(z_right),
                whole(y_left),
            ],
            out_specs=pl.BlockSpec((parts, count, own, width_z), lambda i, p: (0, i, 0, 0)),
        ),
        out_shape=jax.ShapeDtypeStruct((parts, planes + share, own, width_z), jnp.float32),
        cost_estimate=cost(guess),
        compiler_params=room(60),
    )(pair[None], guess, initial, z_right, y_left)


def relax_kernel(pushed_ref, early_ref, fine_ref, out_ref, work):
    steps, planes = out_ref.shape[:2]
    for n in range(steps):

        def old(k):
            return early_ref[:, k] if n == 0 else out_ref[n - 1, k]

        def right(k):
            return pushed_ref[n, k] + (2.0 / half) * old(k)

        def keep(k, solved):
            out_ref[n, k] = solved - old(k)

        ghosts = [early_ref[:, planes + 2 * n + i] for i in (0, 1)]
        solve(planes, right, lambda k: fine_ref[k], work, *ghosts, keep)


def relax(pushed, early, fine_pivots):
    steps, planes, parts, own, width_z = pushed.shape
    step = 2 if parts % 2 == 0 else 1
    block = pl.BlockSpec((steps, planes, step, own, width_z), lambda i: (0, 0, i, 0, 0))
    return pl.pallas_call(
        relax_kernel,
        grid=(parts // step,),
        out_shape=jax.ShapeDtypeStruct(pushed.shape, jnp.float32),
        in_specs=[
            block,
            pl.BlockSpec((step, early.shape[1], own, width_z), lambda i: (i, 0, 0, 0)),
            pl.BlockSpec((planes // 2 + 1, step, own, width_z), lambda i: (0, i, 0, 0)),
        ],
        out_specs=block,
        scratch_shapes=[pltpu.VMEM((planes, step, own, width_z), jnp.float32)],
        cost_estimate=cost(early),
        compiler_params=room(24),
    )(pushed, early, fine_pivots)


def finish_kernel(q_steps, relaxed_ref, *refs):
    *late_refs, fine_ref, wide_ref, y_ref, z_ref, out_ref, points, state, work = refs
    steps, count, width_y, width_z = out_ref.shape
    planes = points.shape[1]
    some = state.shape[1]
    wide = steps * half
    turn = pl.program_id(0)

    def late(k):
        return jnp.concatenate([ref[:, k] for ref in late_refs], axis=1)

    @pl.when(turn < q_steps)
    def _():
        place = pl.ds(turn * some, some)

        def sent(k, solved):
            points[steps - 1, k, place] = relaxed_ref[steps - 1, k] + (solved - late(k))

        ghosts = [late(planes + 2 * (steps - 1) + i) for i in (0, 1)]
        solve(planes, lambda k: (2.0 / wide) * late(k), lambda k: wide_ref[k], work, *ghosts, sent)
        for n in range(steps - 1):

            def old(k):
                return late(k) if n == 0 else state[k]

            def right(k):
                return (2.0 / half) * old(k)

            def keep(k, solved):
                fresh = solved - old(k)
                state[k] = fresh
                points[n, k, place] = relaxed_ref[n, k] + fresh

            ghosts = [late(planes + 2 * n + i) for i in (0, 1)]
            solve(planes, right, lambda k: fine_ref[k], work, *ghosts, keep)

    @pl.when(turn >= q_steps)
    def _():
        first = (turn - q_steps) * count
        step = 2 if count % 2 == 0 else 1
        for n in range(steps):
            lines = []
            for i in range(0, count, step):
                wide = [points[n, first + i + j].reshape(width_y, width_z) for j in range(step)]
                wide = times_left(y_ref[...], jnp.concatenate(wide, axis=1))
                lines += [wide[:, j * width_z : (j + 1) * width_z] for j in range(step)]
            block = times_right(jnp.concatenate(lines, axis=0), z_ref[...])
            out_ref[n] = block.reshape(count, width_y, width_z)


def finish(relaxed, lates, fine_pivots, wide_pivots, y_left, z_right):
    steps, planes, parts, own, width_z = relaxed.shape
    width_y = parts * own
    some = 2 if parts % 2 == 0 else 1
    count = 4 if planes % 4 == 0 else 1
    q_steps, x_steps = parts // some, planes // count
    ahead = lambda i: jnp.minimum(i, q_steps - 1)
    after = lambda i: jnp.maximum(i - q_steps, 0)
    pivots = pl.BlockSpec((planes // 2 + 1, some, own, width_z), lambda i: (0, ahead(i), 0, 0))
    return pl.pallas_call(
        lambda *refs: finish_kernel(q_steps, *refs),
        grid=(q_steps + x_steps,),
        out_shape=jax.ShapeDtypeStruct((steps, planes, width_y, width_z), jnp.float32),
        in_specs=[
            pl.BlockSpec((steps, planes, some, own, width_z), lambda i: (0, 0, ahead(i), 0, 0)),
            *(
                pl.BlockSpec((some, *late.shape[1:]), lambda i: (ahead(i), 0, 0, 0))
                for late in lates
            ),
            pivots,
            pivots,
            pl.BlockSpec(y_left.shape, lambda i: (0, 0)),
            pl.BlockSpec(z_right.shape, lambda i: (0, 0)),
        ],
        out_specs=pl.BlockSpec((steps, count, width_y, width_z), lambda i: (0, after(i), 0, 0)),
        scratch_shapes=[
            pltpu.VMEM(relaxed.shape, jnp.float32),
            pltpu.VMEM((planes, some, own, width_z), jnp.float32),
            pltpu.VMEM((planes, some, own, width_z), jnp.float32),
        ],
        cost_estimate=cost(relaxed),
        compiler_params=room(28),
    )(relaxed, *lates, fine_pivots, wide_pivots, y_left, z_right)


def per_device(forcing, coarse_guess, initial):
    steps, planes, width_y, width_z = forcing.shape
    n_space = lax.axis_size("space")
    n_plane = lax.axis_size("plane")
    width_x = planes * n_space
    parts = 2 * n_space
    own = width_y // parts
    chunks = 2 if own % 16 == 0 else 1
    rows = own // chunks
    table_x = jnp.asarray(sine_table(width_x))
    z_right = jnp.asarray(right_table(sine_table(width_z)))
    y_left = jnp.asarray(left_table(sine_table(width_y)))
    y_scaled = jnp.asarray(left_table((time_step / half) * sine_table(width_y)))
    fine_pivots = pivot_table(planes, width_y, width_z, half)
    wide_pivots = pivot_table(planes, width_y, width_z, steps * half)
    pair = lax.axis_index("pair")
    level = lax.axis_index("plane")
    offset = (lax.axis_index("space") * 2 + pair) * own
    e_x, e_y, e_z = (
        jnp.asarray(eigen_values(n).astype(np.float32)) for n in (width_x, width_y, width_z)
    )
    spectrum = (
        e_x[:, None, None]
        + lax.dynamic_slice_in_dim(e_y, offset, own)[None, :, None]
        + e_z[None, None, :]
    )
    implicit = 1.0 - half * spectrum
    fine = (1.0 + half * spectrum) / implicit
    wide = steps * half
    coarse = (1.0 + wide * spectrum) / (1.0 - wide * spectrum)
    power = [jnp.ones_like(fine)]
    for _ in range(steps):
        power.append(power[-1] * fine)
    leap = power[steps]

    def swap(fields):
        return lax.all_to_all(fields, ("space", "pair"), split_axis=0, concat_axis=0, tiled=True)

    def spread(fields):
        return swap(fields).reshape(n_space, 2, *fields.shape[1:])

    by_device = table_x.reshape(n_space, planes, width_x)

    def modes(cells):
        return jnp.einsum("sbmqr,smp->bpqr", cells, by_device, precision=high)

    share = planes // 2
    opened = opening_fields(coarse_guess[0], initial, z_right, y_left, pair, parts)
    opened, forcing = lax.optimization_barrier((opened, forcing))
    opened = spread(opened)
    pushed, relaxed = front(
        forcing, z_right, y_scaled, jnp.asarray(fine_pivots.reshape(-1, parts, own, width_z)), parts
    )
    opened, relaxed = lax.optimization_barrier((opened, relaxed))
    arrived = spread(relaxed)

    guess = modes(opened[:, :, :planes])
    before = lax.ppermute(guess[1], "plane", [(i, (i + 1) % n_plane) for i in range(n_plane)])
    anchor = jnp.einsum(
        "sbmqr,sbmp->pqr",
        opened[:, :, planes:],
        table_x.reshape(n_space, 2, share, width_x),
        precision=high,
    )

    edges = arrived[:, :, planes:].reshape(n_space, 2, steps, 2, own, width_z)
    full = np.concatenate([np.zeros((1, width_x)), sine_table(width_x), np.zeros((1, width_x))])
    across = np.stack([full[0 : width_x : planes], full[planes + 1 :: planes]], axis=1)
    border = np.stack([full[1 : width_x + 1 : planes], full[planes : width_x + 1 : planes]], axis=1)
    across = jnp.asarray(across.astype(np.float32))
    border = jnp.asarray(border.astype(np.float32))
    kicks = jnp.einsum("sbnkqr,skp->nbpqr", edges, across, precision=high) * (half / implicit)
    drift = [kicks[0]]
    for n in range(1, steps):
        drift.append(fine * drift[-1] + kicks[n])
    gathered = modes(arrived[:, :, :planes]) + drift[-1]

    value = jnp.stack([leap * before + gathered[0], leap * guess[0] + gathered[1]])
    second_residual = leap * (value[0] - guess[0])

    def chunk_of(array, c):
        return lax.slice_in_dim(array, c * rows, (c + 1) * rows, axis=array.ndim - 2)

    shifted = [
        lax.ppermute(chunk_of(value[1], c), "plane", [(i, i + 1) for i in range(n_plane - 1)])
        for c in range(chunks)
    ]
    rate = [chunk_of(coarse, c) for c in range(chunks)]
    second = [chunk_of(second_residual, c) for c in range(chunks)]
    start = [chunk_of(before, c) for c in range(chunks)]
    carries = [jnp.zeros_like(start[0])] * chunks
    lasts, firsts, sent = [], [], []

    def onward(c, carried):
        return rate[c] * (rate[c] * carried + firsts[c]) + second[c]

    def hop(c, sent, place):
        return lax.ppermute(sent, "plane", [(place, place + 1)])

    for c in range(chunks):
        if c > 0:
            sent[c - 1], start[c] = lax.optimization_barrier((sent[c - 1], start[c]))
        lasts.append(jnp.where(level == 0, chunk_of(anchor, c), shifted[c]))
        firsts.append(chunk_of(leap, c) * (lasts[c] - start[c]))
        sent.append(onward(c, carries[c]))
    sent[-1], lasts, firsts = lax.optimization_barrier((sent[-1], lasts, firsts))
    last = jnp.concatenate(lasts, axis=1)
    first_residual = jnp.concatenate(firsts, axis=1)

    def cells(spectra):
        return jnp.einsum("bpqr,smp->sbmqr", spectra, by_device, precision=high)

    def ghosts(spectra, own_planes=None):
        rim = jnp.einsum("nbpqr,skp->sbnkqr", spectra, border, precision=high)
        if own_planes is not None:
            rim = rim + own_planes
        blank = jnp.zeros_like(rim[:1, :, :, :1])
        left = jnp.concatenate([blank, rim[:-1, :, :, 1:]], axis=0)
        right = jnp.concatenate([rim[1:, :, :, :1], blank], axis=0)
        both = jnp.concatenate([left, right], axis=3)
        return both.reshape(n_space, 2, -1, *both.shape[4:])

    def sums(begin, count, c=None):
        pick = (lambda a: a) if c is None else (lambda a: chunk_of(a, c))
        return [pick(power[n] + power[n - 1]) * begin for n in range(1, count + 1)]

    def packed(*pieces):
        joined = jnp.concatenate(pieces, axis=2)
        return joined.reshape(parts, *joined.shape[2:])

    begin = jnp.stack([last, value[0]])
    both = sums(begin, steps)
    for n in range(steps):
        both[n] = both[n] + drift[n] + (drift[n - 1] if n > 0 else 0.0)
    early = packed(cells(begin), ghosts(jnp.stack(both), edges))
    mine = jnp.where(pair == 0, first_residual, second_residual)
    other = jnp.where(pair == 0, second_residual, first_residual)
    early, second, other = lax.optimization_barrier((early, second, other))
    other = lax.ppermute(other, "pair", [(0, 1), (1, 0)])
    early = swap(early)
    for place in range(n_plane - 1):
        for c in range(chunks):
            if place > 0:
                sent[c] = onward(c, carries[c])
        if place == n_plane - 2:
            sent, pushed = lax.optimization_barrier((sent, pushed))
        for c in range(chunks):
            carries[c] = carries[c] + hop(c, sent[c], place)
    fine_pivots, wide_pivots = (
        jnp.asarray(a.reshape(-1, parts, own, width_z)) for a in (fine_pivots, wide_pivots)
    )
    relaxed = relax(pushed.reshape(steps, planes, parts, own, width_z), early, fine_pivots)
    lates = []
    for c in range(chunks):
        error = jnp.stack([carries[c], rate[c] * carries[c] + firsts[c]])
        spectra = jnp.stack(sums(error, steps - 1, c) + [(rate[c] + 1.0) * error])
        late = packed(cells(error), ghosts(spectra))
        late, relaxed, mine = lax.optimization_barrier((late, relaxed, mine))
        lates.append(swap(late))
    residual = jnp.concatenate(
        [jnp.where(pair == 0, mine, other), jnp.where(pair == 0, other, mine)], axis=1
    )
    points = finish(relaxed, lates, fine_pivots, wide_pivots, y_left, z_right)
    return (points, residual[None])


def solution(mesh):
    whole = mesh.devices
    cut = Mesh(whole.reshape(whole.shape[0] // 2, 2, whole.shape[1]), ("plane", "pair", "space"))
    both = ("plane", "pair")
    placed = (P(both, "space", None, None), P(both, "space", None, None), P("space", None, None))
    return jax.shard_map(
        per_device,
        mesh=cut,
        in_specs=placed,
        out_specs=(P(both, "space", None, None), P(both, None, "space", None)),
        check_vma=False,
    )
```

time: 764 us -> 280 us (0.37)
  waiting for transfers between devices: 409 us -> 117 us
  blocking collectives: 147 us -> 0 us
  matrix products: 69.8 us -> 14.5 us
  Pallas kernels: 0 us -> 32.7 us
  starting transfers between devices: 9.52 us -> 39.6 us
  other arithmetic: 45.5 us -> 24.3 us
  between operations: 14.5 us -> 1.44 us
  local copies, waits for them, and re-layouts: 57.5 us -> 45 us
    all_gather x2 -> x0, waiting for transfers between devices: 227 us -> none  [prefix_2(): gathered = jax.tree.map(lambda a: lax.all_gather(a, axis), part)]
    all_to_all x1 -> x0, blocking collectives: 147 us -> none  [per_device(): lax.all_to_all(fields, 'space', split_axis=2, concat_axis=1, tiled=True)]
    dot_general x6 -> x10, matrix products: 69.8 us -> 14.5 us  [the longest x3 4.32 us: ghosts(): rim = jnp.einsum('nbpqr,skp->sbnkqr', spectra, border, precision=high)]
    ppermute x2 -> x10, waiting for transfers between devices: 91.8 us -> 50.7 us  [the longest x6 32.9 us: hop(): return lax.ppermute(sent, 'plane', [(place, place + 1)])]
    pallas_call x0 -> x4, Pallas kernels: none -> 32.7 us  [the longest x1 11.4 us: finish(): pl.pallas_call(lambda *refs: finish_kernel(q_steps, *refs), grid=(q_steps...]
    unnamed x11 -> x105, local copies, waits for them, and re-layouts: 5.94 us -> 29.8 us
    all_to_all x1 -> x5, waiting for transfers between devices: 89.8 us -> 66.6 us  [swap(): lax.all_to_all(fields, ('space', 'pair'), split_axis=0, concat_axis=0, ti...]
    all_to_all x1 -> x5, starting transfers between devices: 6.19 us -> 28.8 us  [swap(): lax.all_to_all(fields, ('space', 'pair'), split_axis=0, concat_axis=0, ti...]
  transfers between devices with their start and end apart: 5 -> 15, of which waited for: 4 -> 8; matrix products, arithmetic and copies ran while one was open for 11% -> 16% of each run, Pallas kernels for 0% -> 5%
where the time goes in v1:
time: 280 us; the launch traced here: 275 us
  waiting for transfers between devices  117 us (42%)
  local copies, waits for them, and re-layouts  45 us (16%)
  starting transfers between devices  39.6 us (14%)
  Pallas kernels  32.7 us (12%)
  other arithmetic  24.3 us (9%)
  matrix products  14.5 us (5%)
    all_to_all x5, waiting for transfers between devices, swap(): lax.all_to_all(fields, ('space', 'pair'), split_axis=0, concat_axis=0, ti...  66.6 us
    ppermute x6, waiting for transfers between devices, hop(): return lax.ppermute(sent, 'plane', [(place, place + 1)])  32.9 us
    unnamed x105, local copies, waits for them, and re-layouts  29.8 us
    all_to_all x5, starting transfers between devices, swap(): lax.all_to_all(fields, ('space', 'pair'), split_axis=0, concat_axis=0, ti...  28.8 us
    ppermute x2, waiting for transfers between devices, per_device(): lax.ppermute(chunk_of(value[1], c), 'plane', [(i, i + 1) for i in range(n...  17.8 us
    pallas_call x1, Pallas kernels, finish(): pl.pallas_call(lambda *refs: finish_kernel(q_steps, *refs), grid=(q_steps...  11.4 us
    pallas_call x1, Pallas kernels, front(): pl.pallas_call(lambda *refs: front_kernel(x_steps, *refs), grid=(x_steps...  10.7 us
    pallas_call x1, Pallas kernels, opening_fields(): pl.pallas_call(lambda *refs: opening_kernel(g_steps, *refs), grid_spec=pl...  7.16 us
  transfers between devices with their start and end apart: 15, of which 8 were waited for; matrix products, arithmetic and copies ran while one was open for 16% of the time, Pallas kernels for 5%

profile of v1, /device:TPU:25, one launch (start us, length us, event | category | flops | bytes accessed | tf_op | source)
XLA Modules:
  0.0 274.8 jit_solution(16652059007672364624)
XLA Ops:
  0.6 7.2 %shard_map.158 = f32[8,48,16,128]{3,2,1,0:T(8,128)} custom-call(s32[1]{0:T(128)} %bitcast.2.refs_0_, f32[32,128,128]{2,1,0:T(8,128)} %bitcast.182, f32[32,128,128]{2,1,0:T(8,128)} %refs_2_.2, bf16[256,256]{1,0:T(8,128)(2,1)} %constant.48.clone.refs_3_.refs_1_.refs_6_, bf16[256,256]{1,0:T(8,128)(2,1)} %constant.49.clone.refs_4_.refs_5_), custom_call_target="tpu_custom_call" | custom-call | flops 838860800 | bytes 4194304 | tf_op jit(solution)/shard_map/pallas_call | solution.py:202
  7.8 5.1 %all-to-all-start = ((f32[8,48,16,128]{3,2,1,0:T(8,128)}), f32[8,48,16,128]{3,2,1,0:T(8,128)}, u32[]{:S(2)}, u32[]{:S(2)}) async-start(f32[8,48,16,128]{3,2,1,0:T(8,128)} %shard_map.158), calls=%async_computation | async-start | bytes 6291456 | tf_op jit(solution)/shard_map/all_to_all | solution.py:381
  13.0 3.4 %copy-done.11 = f32[4,32,128,128]{3,2,1,0:T(8,128)S(1)} copy-done((f32[4,32,128,128]{3,2,1,0:T(8,128)S(1)}, f32[4,32,128,128]{3,2,1,0:T(8,128)}, u32[]{:S(2)}) %copy-start.11) | copy-done | bytes 8388632
  16.4 10.7 %shard_map.159 = (f32[4,32,128,128]{3,2,1,0:T(8,128)S(1)}, f32[8,40,16,128]{3,2,1,0:T(8,128)S(1)}) custom-call(f32[4,32,128,128]{3,2,1,0:T(8,128)S(1)} %copy-done.11, bf16[256,256]{1,0:T(8,128)(2,1)S(1)} %copy-done.9, bf16[256,256]{1,0:T(8,128)(2,1)S(1)} %copy-done.12, f32[17,8,16,128]{3,2,1,0:T(8,128)S(1)} %copy-done.4), custom_call_target="tpu_custom_call" | custom-call | flops 3355443200 | bytes 16777216 | tf_op jit(solution)/shard_map/pallas_call | solution.py:161
  27.1 3.4 %copy-done.2 = f32[4,32,128,128]{3,2,1,0:T(8,128)} copy-done((f32[4,32,128,128]{3,2,1,0:T(8,128)}, f32[4,32,128,128]{3,2,1,0:T(8,128)S(1)}, u32[]{:S(2)}) %copy-start.2) | copy-done | bytes 8388632
  30.5 1.5 copy-done.7
  32.0 17.6 %all-to-all-done = f32[8,48,16,128]{3,2,1,0:T(8,128)} async-done(((f32[8,48,16,128]{3,2,1,0:T(8,128)}), f32[8,48,16,128]{3,2,1,0:T(8,128)}, u32[]{:S(2)}, u32[]{:S(2)}) %all-to-all-start) | async-done | bytes 3145760 | tf_op jit(solution)/shard_map/all_to_all | solution.py:381
  49.6 4.9 %all-to-all-start.1 = ((f32[8,40,16,128]{3,2,1,0:T(8,128)}), f32[8,40,16,128]{3,2,1,0:T(8,128)}, u32[]{:S(2)}, u32[]{:S(2)}) async-start(f32[8,40,16,128]{3,2,1,0:T(8,128)} %copy-done.7), calls=%async_computation.1 | async-start | bytes 5242880 | tf_op jit(solution)/shard_map/all_to_all | solution.py:381
  54.7 2.9 %copy.32 = f32[4,2,48,16,128]{4,2,0,3,1:T(8,128)S(1)} copy(f32[4,2,48,16,128]{4,3,2,1,0:T(8,128)} %bitcast.4) | data formatting | bytes 6291456 | tf_op jit(solution)/shard_map/optimization_barrier | solution.py:398
  57.5 1.0 fusion.35
  58.7 1.2 copy-done.27
  60.3 25.2 %all-to-all-done.1 = f32[8,40,16,128]{3,2,1,0:T(8,128)} async-done(((f32[8,40,16,128]{3,2,1,0:T(8,128)}), f32[8,40,16,128]{3,2,1,0:T(8,128)}, u32[]{:S(2)}, u32[]{:S(2)}) %all-to-all-start.1) | async-done | bytes 2621472 | tf_op jit(solution)/shard_map/all_to_all | solution.py:381
  85.5 1.1 slice.152
  86.7 2.0 slice.151
  88.7 3.8 %bitcast_multiply_fusion = f32[4,2,128,16,128]{4,2,3,1,0:T(8,128)S(1)} fusion(f32[128,16,128]{2,0,1:T(8,128)S(1)} %get-tuple-element.119, f32[4,2,128,1,1,1]{2,0,1,5,3,4:T(4,128)S(1)} %copy-done.47, f32[4,2,4,2,16,128]{5,4,3,2,1,0:T(8,128)S(1)} %bitcast.177), kind=kOutput, calls=%fused_computation.8 | convolution fusion | flops 102760448 | bytes 9965568 | tf_op jit(solution)/shard_map/sbnkqr,skp->nbpqr/dot_general | solution.py:416
  92.6 2.5 bitcast_add_fusion
  95.1 1.0 copy-done.13
  96.1 4.5 %subtract_multiply_fusion = (f32[128,16,128]{2,0,1:T(8,128)}, f32[128,16,128]{2,0,1:T(8,128)S(1)}, f32[128,16,128]{2,0,1:T(8,128)S(1)}, f32[128,16,128]{2,0,1:T(...) fusion(f32[2,128,16,128]{3,1,2,0:T(8,128)S(1)} %copy-done.28, ...), kind=kLoop, calls=%fused_computation.88 | loop fusion | flops 5505024 | bytes 13640192 | tf_op jit(solution)/shard_map/mul | solution.py:423
  100.6 1.1 fusion.68
  101.7 1.3 collective-permute-start.1
  103.1 3.0 %copy.31 = f32[4,2,48,16,128]{4,2,0,1,3:T(8,128)S(1)} copy(f32[4,2,48,16,128]{4,3,2,1,0:T(8,128)} %bitcast.4) | data formatting | bytes 6291456 | tf_op jit(solution)/shard_map/optimization_barrier | solution.py:398
  106.0 1.6 collective-permute-start
  108.3 8.6 %collective-permute-done.1 = f32[128,8,128]{2,0,1:T(8,128)} collective-permute-done((f32[128,8,128]{2,0,1:T(8,128)}, f32[128,8,128]{2,0,1:T(8,128)}, u32[]{:S(2)}, u32[]{:S(2)}) %collective-permute-start.1) | collective-permute-done | bytes 524320 | tf_op jit(solution)/shard_map/ppermute | solution.py:429
  116.9 1.9 multiply_add_fusion.12
  118.8 9.2 %collective-permute-done = f32[128,8,128]{2,0,1:T(8,128)S(1)} collective-permute-done((f32[128,8,128]{2,0,1:T(8,128)S(1)}, f32[128,8,128]{2,0,1:T(8,128)S(1)}, u32[]{:S(2)}, u32[]{:S(2)}) %collective-permute-start) | collective-permute-done | bytes 524320 | tf_op jit(solution)/shard_map/ppermute | solution.py:429
  128.5 1.2 copy-done.23
  130.2 0.8 copy-done.21
  131.6 2.0 add_add_fusion.2
  133.6 2.1 fusion.43
  136.6 1.0 fusion.34
  137.8 1.2 copy.38
  139.0 1.6 pad_maximum_fusion
  140.7 1.5 broadcast_select_fusion.2
  143.8 1.3 multiply_add_fusion.8
  145.1 1.6 collective-permute-start.4
  146.7 4.9 %all-to-all-start.2 = ((f32[8,40,16,128]{3,2,1,0:T(8,128)}), f32[8,40,16,128]{3,2,1,0:T(8,128)S(1)}, u32[]{:S(2)}, u32[]{:S(2)}) async-start(f32[8,40,16,128]{3,2,1,0:T(8,128)} %pad_maximum_fusion), calls=%async_computation.2 | async-start | bytes 5242880 | tf_op jit(solution)/shard_map/all_to_all | solution.py:381
  151.6 1.8 multiply_add_fusion.7
  153.5 1.3 collective-permute-start.8
  154.8 1.5 collective-permute-start.7
  156.3 0.9 fusion.67
  157.2 1.2 fusion.65
  158.4 1.4 collective-permute-start.9
  159.8 21.9 %collective-permute-done.8 = f32[128,8,128]{2,0,1:T(8,128)S(1)} collective-permute-done((f32[128,8,128]{2,0,1:T(8,128)S(1)}, f32[128,8,128]{2,0,1:T(8,128)S(1)}, u32[]{:S(2)}, u32[]{:S(2)}) %collective-permute-start.8) | collective-permute-done | bytes 524320 | tf_op jit(solution)/shard_map/ppermute | solution.py:442
  181.7 11.0 %collective-permute-done.7 = f32[128,8,128]{2,0,1:T(8,128)S(1)} collective-permute-done((f32[128,8,128]{2,0,1:T(8,128)S(1)}, f32[128,8,128]{2,0,1:T(8,128)S(1)}, u32[]{:S(2)}, u32[]{:S(2)}) %collective-permute-start.7) | collective-permute-done | bytes 524320 | tf_op jit(solution)/shard_map/ppermute | solution.py:442
  192.7 1.5 add_bitcast_fusion.1
  194.8 1.1 fusion.44
  197.3 1.2 pad_maximum_fusion.3
  198.5 3.4 %copy-done.3 = f32[4,32,128,128]{3,2,1,0:T(8,128)S(1)} copy-done((f32[4,32,128,128]{3,2,1,0:T(8,128)S(1)}, f32[4,32,128,128]{3,2,1,0:T(8,128)}, u32[]{:S(2)}) %copy-start.3) | copy-done | bytes 8388632
  201.9 1.2 copy-done.5
  203.1 3.4 %shard_map.160.refs_0_ = f32[4,32,8,16,128]{4,3,2,1,0:T(8,128)S(1)} custom-call(f32[4,32,8,16,128]{4,3,2,1,0:T(8,128)S(1)} %bitcast.163, f32[8,40,16,128]{3,2,1,0:T(8,128)S(1)} %all-to-all-done.2.early_ref, f32[17,8,16,128]{3,2,1,0:T(8,128)S(1)} %copy-done.5), custom_call_target="tpu_custom_call" | custom-call | flops 1048576000 | bytes 5242880 | tf_op jit(solution)/shard_map/pallas_call | solution.py:244
  206.5 3.4 %copy-done = f32[4,32,8,16,128]{4,3,2,1,0:T(8,128)} copy-done((f32[4,32,8,16,128]{4,3,2,1,0:T(8,128)}, f32[4,32,8,16,128]{4,3,2,1,0:T(8,128)S(1)}, u32[]{:S(2)}) %copy-start) | copy-done | bytes 8388632
  209.9 9.9 %all-to-all-start.3 = ((f32[8,40,8,128]{3,2,1,0:T(8,128)}), f32[8,40,8,128]{3,2,1,0:T(8,128)S(1)}, u32[]{:S(2)}, u32[]{:S(2)}) async-start(f32[8,40,8,128]{3,2,1,0:T(8,128)} %pad_maximum_fusion.3), calls=%async_computation.3 | async-start | bytes 2621440 | tf_op jit(solution)/shard_map/all_to_all | solution.py:381
  219.8 1.8 broadcast_multiply_fusion.7
  221.7 1.1 fusion.45
  224.2 1.2 pad_maximum_fusion.2
  225.3 11.3 %all-to-all-done.3.refs_1_ = f32[8,40,8,128]{3,2,1,0:T(8,128)S(1)} async-done(((f32[8,40,8,128]{3,2,1,0:T(8,128)}), f32[8,40,8,128]{3,2,1,0:T(8,128)S(1)}, u32[]{:S(2)}, u32[]{:S(2)}) %all-to-all-start.3) | async-done | bytes 1310752 | tf_op jit(solution)/shard_map/all_to_all | solution.py:381
  236.7 4.0 %all-to-all-start.4 = ((f32[8,40,8,128]{3,2,1,0:T(8,128)}), f32[8,40,8,128]{3,2,1,0:T(8,128)S(1)}, u32[]{:S(2)}, u32[]{:S(2)}) async-start(f32[8,40,8,128]{3,2,1,0:T(8,128)} %pad_maximum_fusion.2), calls=%async_computation.4 | async-start | bytes 2621440 | tf_op jit(solution)/shard_map/all_to_all | solution.py:381
  240.7 1.7 broadcast_select_fusion.1
  242.6 2.5 copy.45
  245.1 12.4 %all-to-all-done.4.refs_2_ = f32[8,40,8,128]{3,2,1,0:T(8,128)S(1)} async-done(((f32[8,40,8,128]{3,2,1,0:T(8,128)}), f32[8,40,8,128]{3,2,1,0:T(8,128)S(1)}, u32[]{:S(2)}, u32[]{:S(2)}) %all-to-all-start.4) | async-done | bytes 1310752 | tf_op jit(solution)/shard_map/all_to_all | solution.py:381
  257.5 3.4 %copy-done.1 = f32[4,32,8,16,128]{4,3,2,1,0:T(8,128)S(1)} copy-done((f32[4,32,8,16,128]{4,3,2,1,0:T(8,128)S(1)}, f32[4,32,8,16,128]{4,3,2,1,0:T(8,128)}, u32[]{:S(2)}) %copy-start.1) | copy-done | bytes 8388632
  260.9 1.2 copy-done.6
  262.2 1.2 copy-done.8
  263.4 11.4 %shard_map.161 = f32[4,32,128,128]{3,2,1,0:T(8,128)} custom-call(f32[4,32,8,16,128]{4,3,2,1,0:T(8,128)S(1)} %copy-done.1, f32[8,40,8,128]{3,2,1,0:T(8,128)S(1)} %all-to-all-done.3.refs_1_, f32[8,40,8,128]{3,2,1,0:T(8,128)S(1)} %all-to-all-done.4.refs_2_, f32[17,8,16,128]{3,2,1,0:T(8,128)S(1)} %copy-done.6, f32[17,8,16,128]{3,2,1,0:T(8,128)S(1)} %copy-done.8, ...), custom_call_target="tpu_custom_call" | custom-call | flops 3355443200 | bytes 16777216 | tf_op jit(solution)/shard_map/pallas_call | solution.py:319
  (127 shorter events, 9.1 us)
Async XLA Ops:
  7.8 5.2 %copy-start.4 = (f32[17,8,16,128]{3,2,1,0:T(8,128)S(1)}, f32[17,8,16,128]{3,2,1,0:T(8,128)}, u32[]{:S(2)}) copy-start(f32[17,8,16,128]{3,2,1,0:T(8,128)} %constant.52.clone.refs_3_.fine_ref) | copy-start | bytes 3342340
  7.8 5.2 %copy-start.9 = (bf16[256,256]{1,0:T(8,128)(2,1)S(1)}, bf16[256,256]{1,0:T(8,128)(2,1)}, u32[]{:S(2)}) copy-start(bf16[256,256]{1,0:T(8,128)(2,1)} %constant.48.clone.refs_3_.refs_1_.refs_6_) | copy-start | bytes 393220
  7.8 5.2 %copy-start.12 = (bf16[256,256]{1,0:T(8,128)(2,1)S(1)}, bf16[256,256]{1,0:T(8,128)(2,1)}, u32[]{:S(2)}) copy-start(bf16[256,256]{1,0:T(8,128)(2,1)} %constant.50.clone.refs_2_) | copy-start | bytes 393220
  7.8 41.8 %all-to-all-start = ((f32[8,48,16,128]{3,2,1,0:T(8,128)}), f32[8,48,16,128]{3,2,1,0:T(8,128)}, u32[]{:S(2)}, u32[]{:S(2)}) async-start(f32[8,48,16,128]{3,2,1,0:T(8,128)} %shard_map.158), calls=%async_computation | async-start | bytes 6291456 | tf_op jit(solution)/shard_map/all_to_all | solution.py:381
  13.0 3.4 %copy-start.11 = (f32[4,32,128,128]{3,2,1,0:T(8,128)S(1)}, f32[4,32,128,128]{3,2,1,0:T(8,128)}, u32[]{:S(2)}) copy-start(f32[4,32,128,128]{3,2,1,0:T(8,128)} %refs_0_) | copy-start | bytes 25165828
  27.1 3.4 %copy-start.2 = (f32[4,32,128,128]{3,2,1,0:T(8,128)}, f32[4,32,128,128]{3,2,1,0:T(8,128)S(1)}, u32[]{:S(2)}) copy-start(f32[4,32,128,128]{3,2,1,0:T(8,128)S(1)} %get-tuple-element.45) | copy-start | bytes 25165828
  30.5 1.5 copy-start.7
  49.6 4.9 %copy-start.46 = (f32[128]{0:T(128)S(1)}, f32[128]{0:T(128)}, u32[]{:S(2)}) copy-start(f32[128]{0:T(128)} %constant.51.clone) | copy-start | bytes 1540
  49.6 35.9 %all-to-all-start.1 = ((f32[8,40,16,128]{3,2,1,0:T(8,128)}), f32[8,40,16,128]{3,2,1,0:T(8,128)}, u32[]{:S(2)}, u32[]{:S(2)}) async-start(f32[8,40,16,128]{3,2,1,0:T(8,128)} %copy-done.7), calls=%async_computation.1 | async-start | bytes 5242880 | tf_op jit(solution)/shard_map/all_to_all | solution.py:381
  54.7 2.9 %copy-start.41 = (f32[4,32,128,1,1]{2,1,0,4,3:T(8,128)S(1)}, f32[4,32,128,1,1]{2,1,0,4,3:T(8,128)}, u32[]{:S(2)}) copy-start(f32[4,32,128,1,1]{2,1,0,4,3:T(8,128)} %constant.73) | copy-start | bytes 196612
  58.6 1.3 copy-start.27
  59.9 36.2 %collective-permute-start.2 = (f32[128,16,128]{2,0,1:T(8,128)S(1)}, f32[128,16,128]{2,0,1:T(8,128)}, u32[]{:S(2)}, u32[]{:S(2)}) collective-permute-start(f32[128,16,128]{2,0,1:T(8,128)S(1)} %slice_bitcast_fusion.1), channel_id=1, source_target_pairs={{0,8},{8,16},{16,24},{24,0},{1,9},{9,17},{17,25},{25,1},{2,10},{10... | collective-permute-start | bytes 3145736 | tf_op jit(solution)/shard_map/ppermute | solution.py:402
  86.6 2.0 copy-start.30
  86.6 2.0 copy-start.47
  92.5 3.5 %copy-start.13 = (f32[4,2,128,16,128]{4,2,3,1,0:T(8,128)}, f32[4,2,128,16,128]{4,2,3,1,0:T(8,128)S(1)}, u32[]{:S(2)}) copy-start(f32[4,2,128,16,128]{4,2,3,1,0:T(8,128)S(1)} %bitcast_multiply_fusion) | copy-start | bytes 25165828
  92.5 3.5 %copy-start.28 = (f32[2,128,16,128]{3,1,2,0:T(8,128)S(1)}, f32[2,128,16,128]{3,1,2,0:T(8,128)}, u32[]{:S(2)}) copy-start(f32[2,128,16,128]{3,1,2,0:T(8,128)} %copy-done.27) | copy-start | bytes 6291460
  100.6 43.2 %copy-start.14 = (f32[128,16,128]{2,0,1:T(8,128)}, f32[128,16,128]{2,0,1:T(8,128)S(1)}, u32[]{:S(2)}) copy-start(f32[128,16,128]{2,0,1:T(8,128)S(1)} %get-tuple-element.117) | copy-start | bytes 3145732
  101.7 15.2 %collective-permute-start.1 = (f32[128,8,128]{2,0,1:T(8,128)}, f32[128,8,128]{2,0,1:T(8,128)}, u32[]{:S(2)}, u32[]{:S(2)}) collective-permute-start(f32[128,8,128]{2,0,1:T(8,128)} %get-tuple-element.105), channel_id=1, source_target_pairs={{0,8},{8,16},{16,24},{1,9},{9,17},{17,25},{2,10},{10,18},{18,26},{... | collective-permute-start | bytes 1572872 | tf_op jit(solution)/shard_map/ppermute | solution.py:429
  103.0 3.0 %copy-start.44 = (f32[128,8,128]{2,0,1:T(8,128)S(1)}, f32[128,8,128]{2,0,1:T(8,128)}, u32[]{:S(2)}) copy-start(f32[128,8,128]{2,0,1:T(8,128)} %get-tuple-element.104) | copy-start | bytes 1572868
  103.0 4.6 %copy-start.45 = (f32[4,2,16,128,1]{3,2,0,4,1:T(8,128)S(1)}, f32[4,2,16,128,1]{3,2,0,4,1:T(8,128)}, u32[]{:S(2)}) copy-start(f32[4,2,16,128,1]{3,2,0,4,1:T(8,128)} %constant.72) | copy-start | bytes 196612
  106.0 10.9 %copy-start.20 = (f32[128,16,128]{2,0,1:T(8,128)S(1)}, f32[128,16,128]{2,0,1:T(8,128)}, u32[]{:S(2)}) copy-start(f32[128,16,128]{2,0,1:T(8,128)} %get-tuple-element.68) | copy-start | bytes 3145732
  106.0 10.9 %copy-start.34 = (f32[128,16,128]{2,0,1:T(8,128)S(1)}, f32[128,16,128]{2,0,1:T(8,128)}, u32[]{:S(2)}) copy-start(f32[128,16,128]{2,0,1:T(8,128)} %get-tuple-element.116) | copy-start | bytes 3145732
  106.0 22.0 %collective-permute-start = (f32[128,8,128]{2,0,1:T(8,128)S(1)}, f32[128,8,128]{2,0,1:T(8,128)S(1)}, u32[]{:S(2)}, u32[]{:S(2)}) collective-permute-start(f32[128,8,128]{2,0,1:T(8,128)S(1)} %copy-done.44), channel_id=1, source_target_pairs={{0,8},{8,16},{16,24},{1,9},{9,17},{17,25},{2,10},{10,18},{18,26},{... | collective-permute-start | bytes 1572872 | tf_op jit(solution)/shard_map/ppermute | solution.py:429
  116.9 11.6 %slice-start = ((s8[8388608]{0:T(1024)(128)(4,1)}), s8[4194304]{0:T(1024)(128)(4,1)S(1)}, s32[]{:S(2)}) async-start(s8[8388608]{0:T(1024)(128)(4,1)} %bitcast.164), calls=%async_computation.5 | async-start | bytes 8388608
  118.8 24.9 %copy-start.18 = (f32[128,8,128]{2,0,1:T(8,128)}, f32[128,8,128]{2,0,1:T(8,128)S(1)}, u32[]{:S(2)}) copy-start(f32[128,8,128]{2,0,1:T(8,128)S(1)} %get-tuple-element.38) | copy-start | bytes 1572868
  118.8 24.9 %copy-start.32 = (f32[128,8,128]{2,0,1:T(8,128)}, f32[128,8,128]{2,0,1:T(8,128)S(1)}, u32[]{:S(2)}) copy-start(f32[128,8,128]{2,0,1:T(8,128)S(1)} %get-tuple-element.39) | copy-start | bytes 1572868
  118.8 9.7 %slice-start.1 = ((s8[8388608]{0:T(1024)(128)(4,1)}), s8[4194304]{0:T(1024)(128)(4,1)S(1)}, s32[]{:S(2)}) async-start(s8[8388608]{0:T(1024)(128)(4,1)} %bitcast.164), calls=%async_computation.6 | async-start | bytes 8388608
  128.3 15.5 %copy-start.16 = (f32[128,8,128]{2,0,1:T(8,128)}, f32[128,8,128]{2,0,1:T(8,128)S(1)}, u32[]{:S(2)}) copy-start(f32[128,8,128]{2,0,1:T(8,128)S(1)} %get-tuple-element.35) | copy-start | bytes 1572868
  128.3 1.4 copy-start.23
  129.7 1.5 copy-start.25
  129.7 1.9 copy-start.33
  131.6 2.0 copy-start.31
  131.6 2.0 copy-start.48
  135.9 7.0 %collective-permute-start.5 = (f32[128,8,128]{2,0,1:T(8,128)S(1)}, f32[128,8,128]{2,0,1:T(8,128)S(1)}, u32[]{:S(2)}, u32[]{:S(2)}) collective-permute-start(f32[128,8,128]{2,0,1:T(8,128)S(1)} %get-tuple-element.40), channel_id=1, source_target_pairs={{0,8},{1,9},{2,10},{3,11},{4,12},{5,13},{6,14},{7,15}} | collective-permute-start | bytes 1572872 | tf_op jit(solution)/shard_map/ppermute | solution.py:442
  142.2 1.5 collective-permute-start.3
  143.0 0.7 collective-permute-start.6
  143.7 1.4 copy-start.39
  145.1 6.5 %copy-start.17 = (f32[128,8,128]{2,0,1:T(8,128)S(1)}, f32[128,8,128]{2,0,1:T(8,128)}, u32[]{:S(2)}) copy-start(f32[128,8,128]{2,0,1:T(8,128)} %copy-done.16) | copy-start | bytes 1572868
  145.1 6.5 %collective-permute-start.4 = (f32[128,8,128]{2,0,1:T(8,128)}, f32[128,8,128]{2,0,1:T(8,128)}, u32[]{:S(2)}, u32[]{:S(2)}) collective-permute-start(f32[128,8,128]{2,0,1:T(8,128)} %get-tuple-element.100), channel_id=1, source_target_pairs={{8,16},{9,17},{10,18},{11,19},{12,20},{13,21},{14,22},{15,23}} | collective-permute-start | bytes 1572872 | tf_op jit(solution)/shard_map/ppermute | solution.py:442
  146.7 51.8 %all-to-all-start.2 = ((f32[8,40,16,128]{3,2,1,0:T(8,128)}), f32[8,40,16,128]{3,2,1,0:T(8,128)S(1)}, u32[]{:S(2)}, u32[]{:S(2)}) async-start(f32[8,40,16,128]{3,2,1,0:T(8,128)} %pad_maximum_fusion), calls=%async_computation.2 | async-start | bytes 5242880 | tf_op jit(solution)/shard_map/all_to_all | solution.py:381
  151.6 1.9 copy-start.43
  151.6 4.7 %copy-start.22 = (f32[128,16,128]{2,0,1:T(8,128)S(1)}, f32[128,16,128]{2,0,1:T(8,128)}, u32[]{:S(2)}) copy-start(f32[128,16,128]{2,0,1:T(8,128)} %get-tuple-element.114) | copy-start | bytes 3145732
  151.6 5.6 %copy-start.24 = (f32[128,16,128]{2,0,1:T(8,128)S(1)}, f32[128,16,128]{2,0,1:T(8,128)}, u32[]{:S(2)}) copy-start(f32[128,16,128]{2,0,1:T(8,128)} %get-tuple-element.112) | copy-start | bytes 3145732
  151.6 5.6 %copy-start.26 = (f32[128,16,128]{2,0,1:T(8,128)S(1)}, f32[128,16,128]{2,0,1:T(8,128)}, u32[]{:S(2)}) copy-start(f32[128,16,128]{2,0,1:T(8,128)} %get-tuple-element.113) | copy-start | bytes 3145732
  153.5 28.2 %collective-permute-start.8 = (f32[128,8,128]{2,0,1:T(8,128)S(1)}, f32[128,8,128]{2,0,1:T(8,128)S(1)}, u32[]{:S(2)}, u32[]{:S(2)}) collective-permute-start(f32[128,8,128]{2,0,1:T(8,128)S(1)} %copy-done.43), channel_id=1, source_target_pairs={{16,24},{17,25},{18,26},{19,27},{20,28},{21,29},{22,30},{23,31}} | collective-permute-start | bytes 1572872 | tf_op jit(solution)/shard_map/ppermute | solution.py:442
  154.8 37.9 %collective-permute-start.7 = (f32[128,8,128]{2,0,1:T(8,128)S(1)}, f32[128,8,128]{2,0,1:T(8,128)S(1)}, u32[]{:S(2)}, u32[]{:S(2)}) collective-permute-start(f32[128,8,128]{2,0,1:T(8,128)S(1)} %get-tuple-element.43), channel_id=1, source_target_pairs={{16,24},{17,25},{18,26},{19,27},{20,28},{21,29},{22,30},{23,31}} | collective-permute-start | bytes 1572872 | tf_op jit(solution)/shard_map/ppermute | solution.py:442
  157.2 35.5 %copy-start.15 = (f32[128,16,128]{2,0,1:T(8,128)S(1)}, f32[128,16,128]{2,0,1:T(8,128)}, u32[]{:S(2)}) copy-start(f32[128,16,128]{2,0,1:T(8,128)} %copy-done.14) | copy-start | bytes 3145732
  157.2 35.5 %copy-start.19 = (f32[128,8,128]{2,0,1:T(8,128)S(1)}, f32[128,8,128]{2,0,1:T(8,128)}, u32[]{:S(2)}) copy-start(f32[128,8,128]{2,0,1:T(8,128)} %copy-done.18) | copy-start | bytes 1572868
  157.2 35.5 %copy-start.38 = (f32[128,8,128]{2,0,1:T(8,128)S(1)}, f32[128,8,128]{2,0,1:T(8,128)}, u32[]{:S(2)}) copy-start(f32[128,8,128]{2,0,1:T(8,128)} %get-tuple-element.61) | copy-start | bytes 1572868
  158.4 82.2 %collective-permute-start.9 = (f32[128,16,128]{2,0,1:T(8,128)}, f32[128,16,128]{2,0,1:T(8,128)}, u32[]{:S(2)}, u32[]{:S(2)}) collective-permute-start(f32[128,16,128]{2,0,1:T(8,128)} %get-tuple-element.53), channel_id=1, source_target_pairs={{0,4},{4,0},{1,5},{5,1},{2,6},{6,2},{3,7},{7,3},{8,12},{12,8},{9,1... | collective-permute-start | bytes 3145736 | tf_op jit(solution)/shard_map/ppermute | solution.py:483
  198.5 3.4 %copy-start.3 = (f32[4,32,128,128]{3,2,1,0:T(8,128)S(1)}, f32[4,32,128,128]{3,2,1,0:T(8,128)}, u32[]{:S(2)}) copy-start(f32[4,32,128,128]{3,2,1,0:T(8,128)} %copy-done.2) | copy-start | bytes 25165828
  201.8 1.2 copy-start.5
  206.5 3.4 %copy-start = (f32[4,32,8,16,128]{4,3,2,1,0:T(8,128)}, f32[4,32,8,16,128]{4,3,2,1,0:T(8,128)S(1)}, u32[]{:S(2)}) copy-start(f32[4,32,8,16,128]{4,3,2,1,0:T(8,128)S(1)} %shard_map.160.refs_0_) | copy-start | bytes 25165828
  209.9 9.9 %copy-start.29 = (f32[128,8,128]{2,0,1:T(8,128)S(1)}, f32[128,8,128]{2,0,1:T(8,128)}, u32[]{:S(2)}) copy-start(f32[128,8,128]{2,0,1:T(8,128)} %get-tuple-element.81) | copy-start | bytes 1572868
  209.9 9.9 %copy-start.35 = (f32[1,1,128,8,128]{4,2,3,1,0:T(8,128)S(1)}, f32[1,1,128,8,128]{4,2,3,1,0:T(8,128)}, u32[]{:S(2)}) copy-start(f32[1,1,128,8,128]{4,2,3,1,0:T(8,128)} %get-tuple-element.83) | copy-start | bytes 1572868
  209.9 9.9 %copy-start.36 = (f32[128,8,128]{2,0,1:T(8,128)S(1)}, f32[128,8,128]{2,0,1:T(8,128)}, u32[]{:S(2)}) copy-start(f32[128,8,128]{2,0,1:T(8,128)} %get-tuple-element.84) | copy-start | bytes 1572868
  209.9 9.9 %copy-start.37 = (f32[128,8,128]{2,0,1:T(8,128)S(1)}, f32[128,8,128]{2,0,1:T(8,128)}, u32[]{:S(2)}) copy-start(f32[128,8,128]{2,0,1:T(8,128)} %get-tuple-element.95) | copy-start | bytes 1572868
  209.9 26.8 %all-to-all-start.3 = ((f32[8,40,8,128]{3,2,1,0:T(8,128)}), f32[8,40,8,128]{3,2,1,0:T(8,128)S(1)}, u32[]{:S(2)}, u32[]{:S(2)}) async-start(f32[8,40,8,128]{3,2,1,0:T(8,128)} %pad_maximum_fusion.3), calls=%async_computation.3 | async-start | bytes 2621440 | tf_op jit(solution)/shard_map/all_to_all | solution.py:381
  221.6 1.3 copy-start.40
  221.6 1.3 copy-start.42
  236.7 20.9 %all-to-all-start.4 = ((f32[8,40,8,128]{3,2,1,0:T(8,128)}), f32[8,40,8,128]{3,2,1,0:T(8,128)S(1)}, u32[]{:S(2)}, u32[]{:S(2)}) async-start(f32[8,40,8,128]{3,2,1,0:T(8,128)} %pad_maximum_fusion.2), calls=%async_computation.4 | async-start | bytes 2621440 | tf_op jit(solution)/shard_map/all_to_all | solution.py:381
  242.6 15.0 %copy-start.10 = (bf16[256,256]{1,0:T(8,128)(2,1)S(1)}, bf16[256,256]{1,0:T(8,128)(2,1)}, u32[]{:S(2)}) copy-start(bf16[256,256]{1,0:T(8,128)(2,1)} %constant.49.clone.refs_4_.refs_5_) | copy-start | bytes 393220
  257.5 3.4 %copy-start.1 = (f32[4,32,8,16,128]{4,3,2,1,0:T(8,128)S(1)}, f32[4,32,8,16,128]{4,3,2,1,0:T(8,128)}, u32[]{:S(2)}) copy-start(f32[4,32,8,16,128]{4,3,2,1,0:T(8,128)} %copy-done) | copy-start | bytes 25165828
  262.2 1.2 copy-start.8
  (2 other events, 2.5 us)

commit v2 on v1

--- a/solution.py
+++ b/solution.py
@@ -60,6 +60,27 @@
     return np.stack(pivots).astype(np.float32)
 
 
+def ghost_table(across, steps):
+    count, _, width = across.shape
+    parts = two_parts(across)
+    out = np.zeros((2, count, steps, 2, steps, 2, width), ml_dtypes.bfloat16)
+    for n in range(steps):
+        out[0, :, n, :, n, 0] = parts[0]
+        out[0, :, n, :, n, 1] = parts[0]
+        out[1, :, n, :, n, 0] = parts[1]
+    return out.reshape(2 * count * steps * 2, steps * 2 * width)
+
+
+def kick_table(across, steps):
+    count, _, width = across.shape
+    out = np.zeros((steps, width, 3, count, steps, 2), ml_dtypes.bfloat16)
+    upper, lower = (np.transpose(a, (2, 0, 1)) for a in two_parts(across))
+    for n in range(steps):
+        for i, part in enumerate((upper, upper, lower)):
+            out[n, :, i, :, n, :] = part
+    return out.reshape(steps * width, 3 * count * steps * 2)
+
+
 def split(values):
     upper = values.astype(jnp.bfloat16)
     return upper, (values - upper.astype(jnp.float32)).astype(jnp.bfloat16)
@@ -73,12 +94,190 @@
     return both[:, :width] + both[:, width:]
 
 
-def times_left(table, values):
+def times_left(table, *values):
     both = jnp.dot(
-        table, jnp.concatenate(split(values), axis=0), preferred_element_type=jnp.float32
-    )
-    width = values.shape[0]
+        table,
+        jnp.concatenate([part for value in values for part in split(value)], axis=0),
+        preferred_element_type=jnp.float32,
+    )
+    width = both.shape[0] // 2
     return both[:width] + both[width:]
+
+
+def rates(spectrum):
+    inverse = 1.0 / (1.0 - half * spectrum)
+    return half * inverse, (1.0 + half * spectrum) * inverse
+
+
+def side_by_side(count):
+    return 2 if count % 2 == 0 else 1
+
+
+def modal_kernel(
+    arrived_ref, before_ref, guess_ref, spectrum_ref, x_ref, kick_ref, ghost_ref, *out_refs
+):
+    value_ref, second_ref, beyond_ref = out_refs
+    n_space = arrived_ref.shape[0]
+    own, width_x, width_z = before_ref.shape
+    steps = beyond_ref.shape[2] // 2
+    planes = width_x // n_space
+    interval = pl.program_id(0)
+    step = side_by_side(own)
+    for first in range(0, own, step):
+        each = range(first, first + step)
+
+        def lines(begin, count):
+            rows = [
+                [arrived_ref[s, pl.ds(begin * own + q, count, stride=own), :] for q in each]
+                for s in range(n_space)
+            ]
+            return [jnp.concatenate(row, axis=1) for row in rows]
+
+        edges = lines(planes, 2 * steps)
+        total = times_left(x_ref[...], jnp.concatenate(lines(0, planes), axis=0))
+        upper, lower = split(jnp.concatenate(edges, axis=0))
+        kicks = jnp.dot(
+            kick_ref[...],
+            jnp.concatenate([upper, lower, upper], axis=0),
+            preferred_element_type=jnp.float32,
+        )
+        wide = lambda pieces: jnp.concatenate(list(pieces), axis=1)
+        factor, fine = rates(wide(spectrum_ref[q] for q in each))
+        drift, both = None, []
+        for n in range(steps):
+            kick = kicks[n * width_x : (n + 1) * width_x] * factor
+            fresh = kick if drift is None else fine * drift + kick
+            both.append(fresh if drift is None else fresh + drift)
+            drift = fresh
+        total = total + drift
+        leap = (fine * fine) * (fine * fine) if steps == 4 else fine**steps
+        guess = wide(guess_ref[q] for q in each)
+        start = jnp.where(interval == 0, wide(before_ref[q] for q in each), guess)
+        total = total + leap * start
+        beyond = times_left(ghost_ref[...], *both)
+        left = lax.broadcasted_iota(jnp.int32, edges[0].shape, 0) % 2 == 0
+        blank = jnp.zeros_like(edges[0])
+        for i, q in enumerate(each):
+            lanes = slice(i * width_z, (i + 1) * width_z)
+            value_ref[q] = total[:, lanes]
+        for s in range(n_space):
+            behind = pltpu.roll(edges[s - 1], 2 * steps - 1, 0) if s > 0 else blank
+            ahead = pltpu.roll(edges[s + 1], 1, 0) if s < n_space - 1 else blank
+            seen = beyond[s * 2 * steps : (s + 1) * 2 * steps] + jnp.where(left, behind, ahead)
+            for i, q in enumerate(each):
+                beyond_ref[q, s] = seen[:, i * width_z : (i + 1) * width_z]
+
+        @pl.when(interval == 0)
+        def _():
+            second = leap * (total - guess)
+            for i, q in enumerate(each):
+                second_ref[q] = second[:, i * width_z : (i + 1) * width_z]
+
+
+def modal(arrived, before, guess, spectrum, tables):
+    n_space, _, total, own, width_z = arrived.shape
+    width_x = before.shape[1]
+    steps = (total - width_x // n_space) // 2
+    still = lambda a: pl.BlockSpec(a.shape, lambda b: (0,) * a.ndim)
+    lead = pl.BlockSpec((None, own, width_x, width_z), lambda b: (b, 0, 0, 0))
+    return pl.pallas_call(
+        modal_kernel,
+        grid=(2,),
+        out_shape=(
+            jax.ShapeDtypeStruct((2, own, width_x, width_z), jnp.float32),
+            jax.ShapeDtypeStruct((own, width_x, width_z), jnp.float32),
+            jax.ShapeDtypeStruct((2, own, n_space, 2 * steps, width_z), jnp.float32),
+        ),
+        in_specs=[
+            pl.BlockSpec((n_space, None, total * own, width_z), lambda b: (0, b, 0, 0)),
+            still(before),
+            pl.BlockSpec((None, own, width_x, width_z), lambda b: (0, 0, 0, 0)),
+            still(spectrum),
+            *(still(a) for a in tables),
+        ],
+        out_specs=(
+            lead,
+            still(before),
+            pl.BlockSpec((None, own, n_space, 2 * steps, width_z), lambda b: (b, 0, 0, 0, 0)),
+        ),
+        cost_estimate=cost(arrived, before),
+        compiler_params=room(40),
+    )(arrived.reshape(n_space, 2, total * own, width_z), before, guess, spectrum, *tables)
+
+
+def cells_kernel(wide_weight, lasts, spectrum_ref, x_ref, ghost_ref, *refs):
+    *start_refs, out_ref = refs
+    even_refs, start_refs = start_refs[:lasts], start_refs[lasts:]
+    n_space = out_ref.shape[0]
+    own, width_x, width_z = spectrum_ref.shape
+    planes = width_x // n_space
+    count = out_ref.shape[1] // own - planes
+    steps = count // 2
+    interval = pl.program_id(0)
+    step = side_by_side(own)
+    rows = own // lasts
+    for first in range(0, own, step):
+        each = range(first, first + step)
+        wide = lambda pieces: jnp.concatenate(list(pieces), axis=1)
+        spectrum = wide(spectrum_ref[q] for q in each)
+        _, fine = rates(spectrum)
+        even = wide(even_refs[q // rows][q % rows] for q in each)
+        odd = wide(start_refs[0][q] for q in each)
+        if wide_weight is not None:
+            coarse = (1.0 + wide_weight * spectrum) / (1.0 - wide_weight * spectrum)
+            odd = odd + coarse * even
+        field = jnp.where(interval == 0, even, odd)
+        both, power = [], field
+        for n in range(steps if wide_weight is None else steps - 1):
+            later = fine * power
+            both.append(later + power)
+            power = later
+        if wide_weight is not None:
+            both.append((coarse + 1.0) * field)
+        total = times_left(x_ref[...], field)
+        beyond = times_left(ghost_ref[...], *both)
+        for i, q in enumerate(each):
+            lanes = slice(i * width_z, (i + 1) * width_z)
+            for s in range(n_space):
+                seen = beyond[s * count : (s + 1) * count, lanes]
+                if wide_weight is None:
+                    seen = seen + start_refs[1][q, s]
+                out_ref[s, pl.ds(q, planes, stride=own), :] = total[
+                    s * planes : (s + 1) * planes, lanes
+                ]
+                out_ref[s, pl.ds(planes * own + q, count, stride=own), :] = seen
+
+
+def to_cells(wide_weight, spectrum, tables, n_space, steps, evens, others):
+    own, width_x, width_z = spectrum.shape
+    planes = width_x // n_space
+    total = planes + 2 * steps
+    still = lambda a: pl.BlockSpec(a.shape, lambda b: (0,) * a.ndim)
+
+    def placed(array):
+        if array.shape[0] == 2 and array.ndim > 3:
+            tail = array.shape[1:]
+            pick = (lambda b: (0,) + (0,) * len(tail)) if array.ndim == 4 else (
+                lambda b: (b,) + (0,) * len(tail)
+            )
+            return pl.BlockSpec((None, *tail), pick)
+        return still(array)
+
+    out = pl.pallas_call(
+        lambda *refs: cells_kernel(wide_weight, len(evens), *refs),
+        grid=(2,),
+        out_shape=jax.ShapeDtypeStruct((n_space, 2, total * own, width_z), jnp.float32),
+        in_specs=[
+            still(spectrum),
+            *(still(a) for a in tables),
+            *(still(a) for a in evens),
+            *(placed(a) for a in others),
+        ],
+        out_specs=pl.BlockSpec((n_space, None, total * own, width_z), lambda b: (0, b, 0, 0)),
+        cost_estimate=cost(spectrum, spectrum),
+        compiler_params=room(40),
+    )(spectrum, *tables, *evens, *others)
+    return out.reshape(2 * n_space, total, own, width_z)
 
 
 def solve(planes, right, pivot, work, left_ghost, right_ghost, finish):
@@ -194,7 +393,7 @@
 def opening_fields(guess, initial, z_right, y_left, pair, parts):
     planes, width_y, width_z = guess.shape
     share = planes // 2
-    count = 8 if share % 8 == 0 else 1
+    count = next(c for c in (16, 8, 1) if share % c == 0)
     g_steps, a_steps = planes // count, share // count
     own = width_y // parts
     block = (count, width_y, width_z)
@@ -253,7 +452,7 @@
         out_specs=block,
         scratch_shapes=[pltpu.VMEM((planes, step, own, width_z), jnp.float32)],
         cost_estimate=cost(early),
-        compiler_params=room(24),
+        compiler_params=room(60),
     )(pushed, early, fine_pivots)
 
 
@@ -338,7 +537,7 @@
             pltpu.VMEM((planes, some, own, width_z), jnp.float32),
         ],
         cost_estimate=cost(relaxed),
-        compiler_params=room(28),
+        compiler_params=room(60),
     )(relaxed, *lates, fine_pivots, wide_pivots, y_left, z_right)
 
 
@@ -364,18 +563,16 @@
         jnp.asarray(eigen_values(n).astype(np.float32)) for n in (width_x, width_y, width_z)
     )
     spectrum = (
-        e_x[:, None, None]
-        + lax.dynamic_slice_in_dim(e_y, offset, own)[None, :, None]
+        e_x[None, :, None]
+        + lax.dynamic_slice_in_dim(e_y, offset, own)[:, None, None]
         + e_z[None, None, :]
     )
-    implicit = 1.0 - half * spectrum
-    fine = (1.0 + half * spectrum) / implicit
+    fine = (1.0 + half * spectrum) / (1.0 - half * spectrum)
     wide = steps * half
     coarse = (1.0 + wide * spectrum) / (1.0 - wide * spectrum)
-    power = [jnp.ones_like(fine)]
-    for _ in range(steps):
-        power.append(power[-1] * fine)
-    leap = power[steps]
+    leap = fine
+    for _ in range(steps - 1):
+        leap = leap * fine
 
     def swap(fields):
         return lax.all_to_all(fields, ("space", "pair"), split_axis=0, concat_axis=0, tiled=True)
@@ -386,7 +583,7 @@
     by_device = table_x.reshape(n_space, planes, width_x)
 
     def modes(cells):
-        return jnp.einsum("sbmqr,smp->bpqr", cells, by_device, precision=high)
+        return jnp.einsum("sbmqr,smp->bqpr", cells, by_device, precision=high)
 
     share = planes // 2
     opened = opening_fields(coarse_guess[0], initial, z_right, y_left, pair, parts)
@@ -401,29 +598,24 @@
     guess = modes(opened[:, :, :planes])
     before = lax.ppermute(guess[1], "plane", [(i, (i + 1) % n_plane) for i in range(n_plane)])
     anchor = jnp.einsum(
-        "sbmqr,sbmp->pqr",
+        "sbmqr,sbmp->qpr",
         opened[:, :, planes:],
         table_x.reshape(n_space, 2, share, width_x),
         precision=high,
     )
 
-    edges = arrived[:, :, planes:].reshape(n_space, 2, steps, 2, own, width_z)
     full = np.concatenate([np.zeros((1, width_x)), sine_table(width_x), np.zeros((1, width_x))])
-    across = np.stack([full[0 : width_x : planes], full[planes + 1 :: planes]], axis=1)
-    border = np.stack([full[1 : width_x + 1 : planes], full[planes : width_x + 1 : planes]], axis=1)
-    across = jnp.asarray(across.astype(np.float32))
-    border = jnp.asarray(border.astype(np.float32))
-    kicks = jnp.einsum("sbnkqr,skp->nbpqr", edges, across, precision=high) * (half / implicit)
-    drift = [kicks[0]]
-    for n in range(1, steps):
-        drift.append(fine * drift[-1] + kicks[n])
-    gathered = modes(arrived[:, :, :planes]) + drift[-1]
-
-    value = jnp.stack([leap * before + gathered[0], leap * guess[0] + gathered[1]])
-    second_residual = leap * (value[0] - guess[0])
+    across = np.stack([full[0:width_x:planes], full[planes + 1 :: planes]], axis=1)
+    across = across.astype(np.float32)
+    x_left = jnp.asarray(left_table(sine_table(width_x)))
+    ghost_left = jnp.asarray(ghost_table(across, steps))
+    kick_left = jnp.asarray(kick_table(across, steps))
+    value, second_residual, beyond = modal(
+        arrived, before, guess, spectrum, (x_left, kick_left, ghost_left)
+    )
 
     def chunk_of(array, c):
-        return lax.slice_in_dim(array, c * rows, (c + 1) * rows, axis=array.ndim - 2)
+        return lax.slice_in_dim(array, c * rows, (c + 1) * rows, axis=0)
 
     shifted = [
         lax.ppermute(chunk_of(value[1], c), "plane", [(i, i + 1) for i in range(n_plane - 1)])
@@ -441,69 +633,47 @@
     def hop(c, sent, place):
         return lax.ppermute(sent, "plane", [(place, place + 1)])
 
+    swapped = []
     for c in range(chunks):
         if c > 0:
             sent[c - 1], start[c] = lax.optimization_barrier((sent[c - 1], start[c]))
         lasts.append(jnp.where(level == 0, chunk_of(anchor, c), shifted[c]))
         firsts.append(chunk_of(leap, c) * (lasts[c] - start[c]))
         sent.append(onward(c, carries[c]))
-    sent[-1], lasts, firsts = lax.optimization_barrier((sent[-1], lasts, firsts))
-    last = jnp.concatenate(lasts, axis=1)
-    first_residual = jnp.concatenate(firsts, axis=1)
-
-    def cells(spectra):
-        return jnp.einsum("bpqr,smp->sbmqr", spectra, by_device, precision=high)
-
-    def ghosts(spectra, own_planes=None):
-        rim = jnp.einsum("nbpqr,skp->sbnkqr", spectra, border, precision=high)
-        if own_planes is not None:
-            rim = rim + own_planes
-        blank = jnp.zeros_like(rim[:1, :, :, :1])
-        left = jnp.concatenate([blank, rim[:-1, :, :, 1:]], axis=0)
-        right = jnp.concatenate([rim[1:, :, :, :1], blank], axis=0)
-        both = jnp.concatenate([left, right], axis=3)
-        return both.reshape(n_space, 2, -1, *both.shape[4:])
-
-    def sums(begin, count, c=None):
-        pick = (lambda a: a) if c is None else (lambda a: chunk_of(a, c))
-        return [pick(power[n] + power[n - 1]) * begin for n in range(1, count + 1)]
-
-    def packed(*pieces):
-        joined = jnp.concatenate(pieces, axis=2)
-        return joined.reshape(parts, *joined.shape[2:])
-
-    begin = jnp.stack([last, value[0]])
-    both = sums(begin, steps)
-    for n in range(steps):
-        both[n] = both[n] + drift[n] + (drift[n - 1] if n > 0 else 0.0)
-    early = packed(cells(begin), ghosts(jnp.stack(both), edges))
-    mine = jnp.where(pair == 0, first_residual, second_residual)
-    other = jnp.where(pair == 0, second_residual, first_residual)
-    early, second, other = lax.optimization_barrier((early, second, other))
-    other = lax.ppermute(other, "pair", [(0, 1), (1, 0)])
-    early = swap(early)
+        other = jnp.where(pair == 0, second[c], firsts[c])
+        swapped.append(lax.ppermute(other, "pair", [(0, 1), (1, 0)]))
+    carries[0] = carries[0] + hop(0, sent[0], 0)
+    following = onward(0, carries[0])
+    following, lasts, swapped = lax.optimization_barrier((following, lasts, swapped))
+    tables = (x_left, ghost_left)
+    early = swap(to_cells(None, spectrum, tables, n_space, steps, lasts, (value, beyond)))
     for place in range(n_plane - 1):
         for c in range(chunks):
             if place > 0:
-                sent[c] = onward(c, carries[c])
-        if place == n_plane - 2:
-            sent, pushed = lax.optimization_barrier((sent, pushed))
-        for c in range(chunks):
-            carries[c] = carries[c] + hop(c, sent[c], place)
+                sent[c] = following if place + c == 1 else onward(c, carries[c])
+            if c < chunks - 1:
+                sent[c], second[c + 1] = lax.optimization_barrier((sent[c], second[c + 1]))
+            if c == chunks - 1 and place == n_plane - 2:
+                sent[c], pushed = lax.optimization_barrier((sent[c], pushed))
+            if place + c > 0:
+                carries[c] = carries[c] + hop(c, sent[c], place)
+    mine = jnp.where(pair == 0, jnp.concatenate(firsts, axis=0), second_residual)
+    other = jnp.concatenate(swapped, axis=0)
     fine_pivots, wide_pivots = (
         jnp.asarray(a.reshape(-1, parts, own, width_z)) for a in (fine_pivots, wide_pivots)
     )
     relaxed = relax(pushed.reshape(steps, planes, parts, own, width_z), early, fine_pivots)
+    firsts, relaxed = lax.optimization_barrier((firsts, relaxed))
     lates = []
     for c in range(chunks):
-        error = jnp.stack([carries[c], rate[c] * carries[c] + firsts[c]])
-        spectra = jnp.stack(sums(error, steps - 1, c) + [(rate[c] + 1.0) * error])
-        late = packed(cells(error), ghosts(spectra))
+        late = to_cells(
+            wide, chunk_of(spectrum, c), tables, n_space, steps, carries[c : c + 1], (firsts[c],)
+        )
         late, relaxed, mine = lax.optimization_barrier((late, relaxed, mine))
         lates.append(swap(late))
     residual = jnp.concatenate(
-        [jnp.where(pair == 0, mine, other), jnp.where(pair == 0, other, mine)], axis=1
-    )
+        [jnp.where(pair == 0, mine, other), jnp.where(pair == 0, other, mine)], axis=0
+    ).transpose(1, 0, 2)
     points = finish(relaxed, lates, fine_pivots, wide_pivots, y_left, z_right)
     return (points, residual[None])
 

time: 280 us -> 264 us (0.943); the launches traced: 275 us -> 264 us
  Pallas kernels: 32.7 us -> 57.6 us
  local copies, waits for them, and re-layouts: 45 us -> 25.5 us
  waiting for transfers between devices: 117 us -> 132 us
  other arithmetic: 24.3 us -> 10.6 us
  matrix products: 14.5 us -> 1.66 us
  starting transfers between devices: 39.6 us -> 34.6 us
    all_to_all x5, waiting for transfers between devices: 66.6 us -> 39 us  [swap(): lax.all_to_all(fields, ('space', 'pair'), split_axis=0, concat_axis=0, ti...]
    ppermute x1, waiting for transfers between devices: 0.01 us -> 22.7 us  [per_device(): lax.ppermute(guess[1], 'plane', [(i, (i + 1) % n_plane) for i in range(n_...]
    pallas_call x0 -> x4, Pallas kernels: none -> 18.4 us  [the longest x3 9.32 us: to_cells(): pl.pallas_call(lambda *refs: cells_kernel(wide_weight, len(evens), *refs)...]
    ppermute x1 -> x2, waiting for transfers between devices: 0.01 us -> 13.6 us  [per_device(): swapped.append(lax.ppermute(other, 'pair', [(0, 1), (1, 0)]))]
    dot_general x10 -> x2, matrix products: 14.5 us -> 1.66 us  [the longest x1 1.04 us: modes(): return jnp.einsum('sbmqr,smp->bqpr', cells, by_device, precision=high)]
    unnamed x105 -> x76, local copies, waits for them, and re-layouts: 29.8 us -> 18.5 us
    ppermute x6, waiting for transfers between devices: 32.9 us -> 40 us  [hop(): return lax.ppermute(sent, 'plane', [(place, place + 1)])]
    mul x3 -> x0, other arithmetic: 6.93 us -> none  [the longest x1 4.49 us: per_device(): second_residual = leap * (value[0] - guess[0])]
  transfers between devices with their start and end apart: 15 -> 16, of which waited for: 8 -> 11; matrix products, arithmetic and copies ran while one was open for 16% -> 8% of each run, Pallas kernels for 5% -> 7%
where the time goes in v2:
time: 264 us
  waiting for transfers between devices  132 us (50%)
  Pallas kernels  57.6 us (22%)
  starting transfers between devices  34.6 us (13%)
  local copies, waits for them, and re-layouts  25.5 us (10%)
  other arithmetic  10.6 us (4%)
    ppermute x6, waiting for transfers between devices, hop(): return lax.ppermute(sent, 'plane', [(place, place + 1)])  40 us
    all_to_all x5, waiting for transfers between devices, swap(): lax.all_to_all(fields, ('space', 'pair'), split_axis=0, concat_axis=0, ti...  39 us
    all_to_all x5, starting transfers between devices, swap(): lax.all_to_all(fields, ('space', 'pair'), split_axis=0, concat_axis=0, ti...  25 us
    ppermute x1, waiting for transfers between devices, per_device(): lax.ppermute(guess[1], 'plane', [(i, (i + 1) % n_plane) for i in range(n_...  22.7 us
    unnamed x76, local copies, waits for them, and re-layouts  18.5 us
    ppermute x2, waiting for transfers between devices, per_device(): lax.ppermute(chunk_of(value[1], c), 'plane', [(i, i + 1) for i in range(n...  17.2 us
    pallas_call x1, Pallas kernels, finish(): pl.pallas_call(lambda *refs: finish_kernel(q_steps, *refs), grid=(q_steps...  14.6 us
    ppermute x2, waiting for transfers between devices, per_device(): swapped.append(lax.ppermute(other, 'pair', [(0, 1), (1, 0)]))  13.6 us
  transfers between devices with their start and end apart: 16, of which 11 were waited for; matrix products, arithmetic and copies ran while one was open for 8% of the time, Pallas kernels for 7%

profile of v2, /device:TPU:25, one launch (start us, length us, event | category | flops | bytes accessed | tf_op | source)
XLA Modules:
  0.0 263.5 jit_solution(17935762245001298473)
XLA Ops:
  0.6 5.4 %shard_map.167 = f32[8,48,16,128]{3,2,1,0:T(8,128)} custom-call(s32[1]{0:T(128)} %bitcast.refs_0_, f32[32,128,128]{2,1,0:T(8,128)} %bitcast.40, f32[32,128,128]{2,1,0:T(8,128)} %refs_2_.5, bf16[256,256]{1,0:T(8,128)(2,1)} %constant.45.clone.refs_3_.refs_1_.refs_6_, bf16[256,256]{1,0:T(8,128)(2,1)} %constant.46.clone.refs_4_.x_ref.refs_1_.refs_5_), custom_call_target="tpu_custom_call" | custom-call | flops 838860800 | bytes 4194304 | tf_op jit(solution)/shard_map/pallas_call | solution.py:401
  6.0 5.2 %all-to-all-start = ((f32[8,48,16,128]{3,2,1,0:T(8,128)}), f32[8,48,16,128]{3,2,1,0:T(8,128)}, u32[]{:S(2)}, u32[]{:S(2)}) async-start(f32[8,48,16,128]{3,2,1,0:T(8,128)} %shard_map.167), calls=%async_computation | async-start | bytes 6291456 | tf_op jit(solution)/shard_map/all_to_all | solution.py:578
  11.2 3.4 %copy-done.19 = f32[4,32,128,128]{3,2,1,0:T(8,128)S(1)} copy-done((f32[4,32,128,128]{3,2,1,0:T(8,128)S(1)}, f32[4,32,128,128]{3,2,1,0:T(8,128)}, u32[]{:S(2)}) %copy-start.19) | copy-done | bytes 8388632
  14.6 10.7 %shard_map.168 = (f32[4,32,128,128]{3,2,1,0:T(8,128)S(1)}, f32[8,40,16,128]{3,2,1,0:T(8,128)S(1)}) custom-call(f32[4,32,128,128]{3,2,1,0:T(8,128)S(1)} %copy-done.19, bf16[256,256]{1,0:T(8,128)(2,1)S(1)} %copy-done.15, bf16[256,256]{1,0:T(8,128)(2,1)S(1)} %copy-done.20, f32[17,8,16,128]{3,2,1,0:T(8,128)S(1)} %copy-done.7), custom_call_target="tpu_custom_call" | custom-call | flops 3355443200 | bytes 16777216 | tf_op jit(solution)/shard_map/pallas_call | solution.py:360
  25.3 3.4 %copy-done.3 = f32[4,32,128,128]{3,2,1,0:T(8,128)} copy-done((f32[4,32,128,128]{3,2,1,0:T(8,128)}, f32[4,32,128,128]{3,2,1,0:T(8,128)S(1)}, u32[]{:S(2)}) %copy-start.3) | copy-done | bytes 8388632
  28.7 1.6 copy-done.10
  30.3 17.6 %all-to-all-done = f32[8,48,16,128]{3,2,1,0:T(8,128)} async-done(((f32[8,48,16,128]{3,2,1,0:T(8,128)}), f32[8,48,16,128]{3,2,1,0:T(8,128)}, u32[]{:S(2)}, u32[]{:S(2)}) %all-to-all-start) | async-done | bytes 3145760 | tf_op jit(solution)/shard_map/all_to_all | solution.py:578
  47.8 4.8 %all-to-all-start.1 = ((f32[8,40,16,128]{3,2,1,0:T(8,128)}), f32[8,40,16,128]{3,2,1,0:T(8,128)}, u32[]{:S(2)}, u32[]{:S(2)}) async-start(f32[8,40,16,128]{3,2,1,0:T(8,128)} %copy-done.10), calls=%async_computation.1 | async-start | bytes 5242880 | tf_op jit(solution)/shard_map/all_to_all | solution.py:578
  52.6 2.9 %copy.20 = f32[4,2,48,16,128]{4,2,0,3,1:T(8,128)S(1)} copy(f32[4,2,48,16,128]{4,3,2,1,0:T(8,128)} %bitcast.2) | data formatting | bytes 6291456 | tf_op jit(solution)/shard_map/optimization_barrier | solution.py:595
  55.5 1.0 fusion.2.guess_ref
  56.6 0.1 slice_bitcast_fusion
  56.6 1.3 copy-done
  58.0 0.1 dynamic_slice.3
  58.1 0.1 broadcast_add_fusion.1
  58.1 1.9 fusion.8
  60.0 22.7 %collective-permute-done.before_ref = f32[16,128,128]{2,1,0:T(8,128)S(1)} collective-permute-done((f32[16,128,128]{2,1,0:T(8,128)S(1)}, f32[16,128,128]{2,1,0:T(8,128)S(1)}, u32[]{:S(2)}, u32[]{:S(2)}) %collective-permute-start) | collective-permute-done | bytes 1048608 | tf_op jit(solution)/shard_map/ppermute | solution.py:599
  82.7 1.0 all-to-all-done.1
  83.7 1.6 copy-done.1
  85.3 9.0 %shard_map.169 = (f32[2,16,128,128]{3,2,1,0:T(8,128)S(1)}, f32[16,128,128]{2,1,0:T(8,128)S(1)}, f32[2,16,4,8,128]{4,3,2,1,0:T(8,128)S(1)}) custom-call(f32[4,2,640,128]{3,2,1,0:T(8,128)} %bitcast.7.arrived_ref, f32[16,128,128]{2,1,0:T(8,128)S(1)} %collective-permute-done.before_ref, f32[2,16,128,128]{3,2,1,0:T(8,128)S(1)} %copy-done.1, ...), custom_call_target="tpu_custom_call" | custom-call | flops 1468006400 | bytes 7340032 | tf_op jit(solution)/shard_map/pallas_call | solution.py:183
  94.3 0.1 slice_bitcast_fusion.2
  94.4 0.7 copy-done.16
  95.1 1.3 copy-done.5
  96.4 1.3 collective-permute-start.2
  97.7 2.9 %copy.18 = f32[4,2,48,16,128]{4,2,0,1,3:T(8,128)S(1)} copy(f32[4,2,48,16,128]{4,3,2,1,0:T(8,128)} %bitcast.2) | data formatting | bytes 6291456 | tf_op jit(solution)/shard_map/optimization_barrier | solution.py:595
  100.7 0.6 convolution_bitcast_fusion
  101.3 1.3 collective-permute-start.1
  102.6 8.8 %collective-permute-done.2 = f32[8,128,128]{2,1,0:T(8,128)} collective-permute-done((f32[8,128,128]{2,1,0:T(8,128)S(1)}, f32[8,128,128]{2,1,0:T(8,128)}, u32[]{:S(2)}, u32[]{:S(2)}) %collective-permute-start.2) | collective-permute-done | bytes 524320 | tf_op jit(solution)/shard_map/ppermute | solution.py:621
  111.4 1.4 slice_select_fusion.2
  112.8 0.1 multiply_add_fusion.5
  112.9 0.7 collective-permute-start.4
  113.6 0.5 collective-permute-start.5
  114.1 8.4 %collective-permute-done.1 = f32[8,128,128]{2,1,0:T(8,128)S(1)} collective-permute-done((f32[8,128,128]{2,1,0:T(8,128)S(1)}, f32[8,128,128]{2,1,0:T(8,128)S(1)}, u32[]{:S(2)}, u32[]{:S(2)}) %collective-permute-start.1) | collective-permute-done | bytes 524320 | tf_op jit(solution)/shard_map/ppermute | solution.py:621
  122.5 1.4 broadcast_select_fusion.2
  123.9 0.4 collective-permute-start.6
  124.3 0.4 collective-permute-done.5
  124.8 13.1 %collective-permute-done.6 = f32[8,128,128]{2,1,0:T(8,128)S(1)} collective-permute-done((f32[8,128,128]{2,1,0:T(8,128)S(1)}, f32[8,128,128]{2,1,0:T(8,128)S(1)}, u32[]{:S(2)}, u32[]{:S(2)}) %collective-permute-start.6) | collective-permute-done | bytes 524320 | tf_op jit(solution)/shard_map/ppermute | solution.py:644
  137.9 1.4 collective-permute-start.8
  139.4 3.7 %shard_map.170 = f32[4,2,640,128]{3,2,1,0:T(8,128)S(1)} custom-call(f32[16,128,128]{2,1,0:T(8,128)S(1)} %get-tuple-element.90.spectrum_ref.refs_0_, bf16[256,256]{1,0:T(8,128)(2,1)S(1)} %copy-done.4, bf16[64,1024]{1,0:T(8,128)(2,1)S(1)} %copy-done.11, f32[8,128,128]{2,1,0:T(8,128)S(1)} %get-tuple-element.51.refs_3_, ...), custom_call_target="tpu_custom_call" | custom-call | flops 838860800 | bytes 4194304 | tf_op jit(solution)/shard_map/pallas_call | solution.py:266
  143.1 1.5 copy-done.2
  144.6 5.6 %all-to-all-start.2 = ((f32[8,40,16,128]{3,2,1,0:T(8,128)}), f32[8,40,16,128]{3,2,1,0:T(8,128)}, u32[]{:S(2)}, u32[]{:S(2)}) async-start(f32[8,40,16,128]{3,2,1,0:T(8,128)} %bitcast.38), calls=%async_computation.2 | async-start | bytes 5242880 | tf_op jit(solution)/shard_map/all_to_all | solution.py:578
  150.2 2.0 multiply_add_fusion
  152.2 0.7 collective-permute-start.3
  152.9 1.3 collective-permute-start.10
  154.2 0.2 multiply_add_fusion.3
  154.3 0.7 collective-permute-start.7
  155.1 1.0 fusion.13
  156.1 1.1 maximum_select_fusion
  157.2 15.3 %collective-permute-done.10 = f32[8,128,128]{2,1,0:T(8,128)S(1)} collective-permute-done((f32[8,128,128]{2,1,0:T(8,128)S(1)}, f32[8,128,128]{2,1,0:T(8,128)S(1)}, u32[]{:S(2)}, u32[]{:S(2)}) %collective-permute-start.10) | collective-permute-done | bytes 524320 | tf_op jit(solution)/shard_map/ppermute | solution.py:634
  172.5 0.9 add.116.refs_3_
  173.4 1.2 multiply_add_fusion.1
  174.5 6.7 %all-to-all-done.2.early_ref = f32[8,40,16,128]{3,2,1,0:T(8,128)} async-done(((f32[8,40,16,128]{3,2,1,0:T(8,128)}), f32[8,40,16,128]{3,2,1,0:T(8,128)}, u32[]{:S(2)}, u32[]{:S(2)}) %all-to-all-start.2) | async-done | bytes 2621472 | tf_op jit(solution)/shard_map/all_to_all | solution.py:578
  181.2 8.6 %shard_map.171.refs_0_ = f32[4,32,8,16,128]{4,3,2,1,0:T(8,128)} custom-call(f32[4,32,8,16,128]{4,3,2,1,0:T(8,128)} %bitcast.39, f32[8,40,16,128]{3,2,1,0:T(8,128)} %all-to-all-done.2.early_ref, f32[17,8,16,128]{3,2,1,0:T(8,128)} %constant.49.clone.refs_3_.fine_ref), custom_call_target="tpu_custom_call" | custom-call | flops 1048576000 | bytes 5242880 | tf_op jit(solution)/shard_map/pallas_call | solution.py:443
  189.8 2.8 %shard_map.173 = f32[4,2,320,128]{3,2,1,0:T(8,128)} custom-call(f32[8,128,128]{2,1,0:T(8,128)S(1)} %copy-done.14, bf16[256,256]{1,0:T(8,128)(2,1)S(1)} %copy-done.4, bf16[64,1024]{1,0:T(8,128)(2,1)S(1)} %copy-done.11, f32[8,128,128]{2,1,0:T(8,128)S(1)} %copy-done.12, f32[8,128,128]{2,1,0:T(8,128)S(1)} %get-tuple-element.56.refs_4_), custom_call_target="tpu_custom_call" | custom-call | flops 419430400 | bytes 2097152 | tf_op jit(solution)/shard_map/pallas_call | solution.py:266
  192.6 4.8 %all-to-all-start.3 = ((f32[8,40,8,128]{3,2,1,0:T(8,128)}), f32[8,40,8,128]{3,2,1,0:T(8,128)}, u32[]{:S(2)}, u32[]{:S(2)}) async-start(f32[8,40,8,128]{3,2,1,0:T(8,128)} %bitcast.19), calls=%async_computation.3 | async-start | bytes 2621440 | tf_op jit(solution)/shard_map/all_to_all | solution.py:578
  197.4 1.3 collective-permute-start.9
  198.7 24.7 %collective-permute-done.9 = f32[8,128,128]{2,1,0:T(8,128)S(1)} collective-permute-done((f32[8,128,128]{2,1,0:T(8,128)S(1)}, f32[8,128,128]{2,1,0:T(8,128)S(1)}, u32[]{:S(2)}, u32[]{:S(2)}) %collective-permute-start.9) | collective-permute-done | bytes 524320 | tf_op jit(solution)/shard_map/ppermute | solution.py:634
  223.5 2.8 %shard_map.172 = f32[4,2,320,128]{3,2,1,0:T(8,128)} custom-call(f32[8,128,128]{2,1,0:T(8,128)S(1)} %copy-done.13, bf16[256,256]{1,0:T(8,128)(2,1)S(1)} %copy-done.4, bf16[64,1024]{1,0:T(8,128)(2,1)S(1)} %copy-done.11, f32[8,128,128]{2,1,0:T(8,128)S(1)} %add.115.refs_3_, f32[8,128,128]{2,1,0:T(8,128)S(1)} %get-tuple-element.54.refs_4_), custom_call_target="tpu_custom_call" | custom-call | flops 419430400 | bytes 2097152 | tf_op jit(solution)/shard_map/pallas_call | solution.py:266
  226.3 4.7 %all-to-all-start.4 = ((f32[8,40,8,128]{3,2,1,0:T(8,128)}), f32[8,40,8,128]{3,2,1,0:T(8,128)S(1)}, u32[]{:S(2)}, u32[]{:S(2)}) async-start(f32[8,40,8,128]{3,2,1,0:T(8,128)} %bitcast.18), calls=%async_computation.4 | async-start | bytes 2621440 | tf_op jit(solution)/shard_map/all_to_all | solution.py:578
  231.1 0.2 broadcast_select_fusion.1
  231.3 0.2 maximum_bitcast_fusion
  231.5 2.5 copy.22
  234.0 13.8 %all-to-all-done.4.refs_2_ = f32[8,40,8,128]{3,2,1,0:T(8,128)S(1)} async-done(((f32[8,40,8,128]{3,2,1,0:T(8,128)}), f32[8,40,8,128]{3,2,1,0:T(8,128)S(1)}, u32[]{:S(2)}, u32[]{:S(2)}) %all-to-all-start.4) | async-done | bytes 1310752 | tf_op jit(solution)/shard_map/all_to_all | solution.py:578
  247.9 1.1 copy-done.23
  248.9 14.6 %shard_map.174 = f32[4,32,128,128]{3,2,1,0:T(8,128)} custom-call(f32[4,32,8,16,128]{4,3,2,1,0:T(8,128)} %shard_map.171.refs_0_, f32[8,40,8,128]{3,2,1,0:T(8,128)} %all-to-all-done.3.refs_1_, f32[8,40,8,128]{3,2,1,0:T(8,128)} %copy-done.23, f32[17,8,16,128]{3,2,1,0:T(8,128)} %constant.49.clone.refs_3_.fine_ref, f32[17,8,16,128]{3,2,1,0:T(8,128)} %constant.52.clone.refs_4_, ...), custom_call_target="tpu_custom_call" | custom-call | flops 3355443200 | bytes 16777216 | tf_op jit(solution)/shard_map/pallas_call | solution.py:518
  (74 shorter events, 0.3 us)
Async XLA Ops:
  6.0 5.2 %copy-start.7 = (f32[17,8,16,128]{3,2,1,0:T(8,128)S(1)}, f32[17,8,16,128]{3,2,1,0:T(8,128)}, u32[]{:S(2)}) copy-start(f32[17,8,16,128]{3,2,1,0:T(8,128)} %constant.49.clone.refs_3_.fine_ref) | copy-start | bytes 3342340
  6.0 5.2 %copy-start.15 = (bf16[256,256]{1,0:T(8,128)(2,1)S(1)}, bf16[256,256]{1,0:T(8,128)(2,1)}, u32[]{:S(2)}) copy-start(bf16[256,256]{1,0:T(8,128)(2,1)} %constant.45.clone.refs_3_.refs_1_.refs_6_) | copy-start | bytes 393220
  6.0 5.2 %copy-start.20 = (bf16[256,256]{1,0:T(8,128)(2,1)S(1)}, bf16[256,256]{1,0:T(8,128)(2,1)}, u32[]{:S(2)}) copy-start(bf16[256,256]{1,0:T(8,128)(2,1)} %constant.47.clone.refs_2_) | copy-start | bytes 393220
  6.0 41.8 %all-to-all-start = ((f32[8,48,16,128]{3,2,1,0:T(8,128)}), f32[8,48,16,128]{3,2,1,0:T(8,128)}, u32[]{:S(2)}, u32[]{:S(2)}) async-start(f32[8,48,16,128]{3,2,1,0:T(8,128)} %shard_map.167), calls=%async_computation | async-start | bytes 6291456 | tf_op jit(solution)/shard_map/all_to_all | solution.py:578
  11.2 3.4 %copy-start.19 = (f32[4,32,128,128]{3,2,1,0:T(8,128)S(1)}, f32[4,32,128,128]{3,2,1,0:T(8,128)}, u32[]{:S(2)}) copy-start(f32[4,32,128,128]{3,2,1,0:T(8,128)} %refs_0_) | copy-start | bytes 25165828
  25.3 3.4 %copy-start.3 = (f32[4,32,128,128]{3,2,1,0:T(8,128)}, f32[4,32,128,128]{3,2,1,0:T(8,128)S(1)}, u32[]{:S(2)}) copy-start(f32[4,32,128,128]{3,2,1,0:T(8,128)S(1)} %get-tuple-element.50) | copy-start | bytes 25165828
  28.7 1.6 copy-start.10
  47.8 35.8 %all-to-all-start.1 = ((f32[8,40,16,128]{3,2,1,0:T(8,128)}), f32[8,40,16,128]{3,2,1,0:T(8,128)}, u32[]{:S(2)}, u32[]{:S(2)}) async-start(f32[8,40,16,128]{3,2,1,0:T(8,128)} %copy-done.10), calls=%async_computation.1 | async-start | bytes 5242880 | tf_op jit(solution)/shard_map/all_to_all | solution.py:578
  52.6 2.9 %copy-start.34 = (f32[4,32,128,1,1]{2,1,0,4,3:T(8,128)S(1)}, f32[4,32,128,1,1]{2,1,0,4,3:T(8,128)}, u32[]{:S(2)}) copy-start(f32[4,32,128,1,1]{2,1,0,4,3:T(8,128)} %constant.58) | copy-start | bytes 196612
  56.5 1.4 copy-start.36
  56.6 1.3 copy-start
  58.0 25.7 %copy-start.4 = (bf16[256,256]{1,0:T(8,128)(2,1)S(1)}, bf16[256,256]{1,0:T(8,128)(2,1)}, u32[]{:S(2)}) copy-start(bf16[256,256]{1,0:T(8,128)(2,1)} %constant.46.clone.refs_4_.x_ref.refs_1_.refs_5_) | copy-start | bytes 393220
  58.0 25.7 %copy-start.11 = (bf16[64,1024]{1,0:T(8,128)(2,1)S(1)}, bf16[64,1024]{1,0:T(8,128)(2,1)}, u32[]{:S(2)}) copy-start(bf16[64,1024]{1,0:T(8,128)(2,1)} %constant.50.clone.ghost_ref.refs_2_) | copy-start | bytes 393220
  58.0 25.7 %copy-start.18 = (bf16[512,96]{1,0:T(8,128)(2,1)S(1)}, bf16[512,96]{1,0:T(8,128)(2,1)}, u32[]{:S(2)}) copy-start(bf16[512,96]{1,0:T(8,128)(2,1)} %constant.51.clone.kick_ref) | copy-start | bytes 294916
  58.0 24.7 %collective-permute-start = (f32[16,128,128]{2,1,0:T(8,128)S(1)}, f32[16,128,128]{2,1,0:T(8,128)S(1)}, u32[]{:S(2)}, u32[]{:S(2)}) collective-permute-start(f32[16,128,128]{2,1,0:T(8,128)S(1)} %slice_bitcast_fusion), channel_id=1, source_target_pairs={{0,8},{8,16},{16,24},{24,0},{1,9},{9,17},{17,25},{25,1},{2,10},{10... | collective-permute-start | bytes 3145736 | tf_op jit(solution)/shard_map/ppermute | solution.py:599
  82.7 11.6 %copy-start.8 = (f32[16,128,128]{2,1,0:T(8,128)}, f32[16,128,128]{2,1,0:T(8,128)S(1)}, u32[]{:S(2)}) copy-start(f32[16,128,128]{2,1,0:T(8,128)S(1)} %collective-permute-done.before_ref) | copy-start | bytes 3145732
  83.7 1.6 copy-start.1
  94.3 0.8 copy-start.16
  95.1 1.3 copy-start.5
  96.4 15.0 %collective-permute-start.2 = (f32[8,128,128]{2,1,0:T(8,128)S(1)}, f32[8,128,128]{2,1,0:T(8,128)}, u32[]{:S(2)}, u32[]{:S(2)}) collective-permute-start(f32[8,128,128]{2,1,0:T(8,128)S(1)} %get-tuple-element.82), channel_id=1, source_target_pairs={{0,8},{8,16},{16,24},{1,9},{9,17},{17,25},{2,10},{10,18},{18,26},{... | collective-permute-start | bytes 1572872 | tf_op jit(solution)/shard_map/ppermute | solution.py:621
  97.7 3.0 %copy-start.35 = (f32[4,2,16,128,1]{3,2,0,4,1:T(8,128)S(1)}, f32[4,2,16,128,1]{3,2,0,4,1:T(8,128)}, u32[]{:S(2)}) copy-start(f32[4,2,16,128,1]{3,2,0,4,1:T(8,128)} %constant.57) | copy-start | bytes 196612
  100.7 10.7 %copy-start.9 = (f32[16,128,128]{2,1,0:T(8,128)S(1)}, f32[16,128,128]{2,1,0:T(8,128)}, u32[]{:S(2)}) copy-start(f32[16,128,128]{2,1,0:T(8,128)} %copy-done.8) | copy-start | bytes 3145732
  100.7 10.7 %copy-start.26 = (f32[16,128,128]{2,1,0:T(8,128)S(1)}, f32[16,128,128]{2,1,0:T(8,128)}, u32[]{:S(2)}) copy-start(f32[16,128,128]{2,1,0:T(8,128)} %get-tuple-element.89) | copy-start | bytes 3145732
  101.3 21.2 %collective-permute-start.1 = (f32[8,128,128]{2,1,0:T(8,128)S(1)}, f32[8,128,128]{2,1,0:T(8,128)S(1)}, u32[]{:S(2)}, u32[]{:S(2)}) collective-permute-start(f32[8,128,128]{2,1,0:T(8,128)S(1)} %get-tuple-element.81), channel_id=1, source_target_pairs={{0,8},{8,16},{16,24},{1,9},{9,17},{17,25},{2,10},{10,18},{18,26},{... | collective-permute-start | bytes 1572872 | tf_op jit(solution)/shard_map/ppermute | solution.py:621
  111.4 1.4 copy-start.21
  112.9 9.6 %collective-permute-start.4 = (f32[8,128,128]{2,1,0:T(8,128)S(1)}, f32[8,128,128]{2,1,0:T(8,128)S(1)}, u32[]{:S(2)}, u32[]{:S(2)}) collective-permute-start(f32[8,128,128]{2,1,0:T(8,128)S(1)} %multiply_add_fusion.5), channel_id=1, source_target_pairs={{0,8},{1,9},{2,10},{3,11},{4,12},{5,13},{6,14},{7,15}} | collective-permute-start | bytes 1572872 | tf_op jit(solution)/shard_map/ppermute | solution.py:634
  113.6 25.8 %copy-start.6 = (f32[2,16,128,128]{3,2,1,0:T(8,128)S(1)}, f32[2,16,128,128]{3,2,1,0:T(8,128)}, u32[]{:S(2)}) copy-start(f32[2,16,128,128]{3,2,1,0:T(8,128)} %copy-done.5) | copy-start | bytes 6291460
  113.6 25.8 %copy-start.17 = (f32[2,16,4,8,128]{4,3,2,1,0:T(8,128)S(1)}, f32[2,16,4,8,128]{4,3,2,1,0:T(8,128)}, u32[]{:S(2)}) copy-start(f32[2,16,4,8,128]{4,3,2,1,0:T(8,128)} %copy-done.16) | copy-start | bytes 1572868
  113.6 11.2 %collective-permute-start.5 = (f32[8,128,128]{2,1,0:T(8,128)S(1)}, f32[8,128,128]{2,1,0:T(8,128)S(1)}, u32[]{:S(2)}, u32[]{:S(2)}) collective-permute-start(f32[8,128,128]{2,1,0:T(8,128)S(1)} %get-tuple-element.75), channel_id=1, source_target_pairs={{0,4},{4,0},{1,5},{5,1},{2,6},{6,2},{3,7},{7,3},{8,12},{12,8},{9,1... | collective-permute-start | bytes 1572872 | tf_op jit(solution)/shard_map/ppermute | solution.py:644
  122.5 1.4 copy-start.28
  123.9 14.0 %collective-permute-start.6 = (f32[8,128,128]{2,1,0:T(8,128)S(1)}, f32[8,128,128]{2,1,0:T(8,128)S(1)}, u32[]{:S(2)}, u32[]{:S(2)}) collective-permute-start(f32[8,128,128]{2,1,0:T(8,128)S(1)} %get-tuple-element.72), channel_id=1, source_target_pairs={{0,4},{4,0},{1,5},{5,1},{2,6},{6,2},{3,7},{7,3},{8,12},{12,8},{9,1... | collective-permute-start | bytes 1572872 | tf_op jit(solution)/shard_map/ppermute | solution.py:644
  124.8 14.6 %copy-start.30 = (f32[8,128,128]{2,1,0:T(8,128)}, f32[8,128,128]{2,1,0:T(8,128)S(1)}, u32[]{:S(2)}) copy-start(f32[8,128,128]{2,1,0:T(8,128)S(1)} %collective-permute-done.5) | copy-start | bytes 1572868
  137.9 1.5 copy-start.32
  137.9 12.2 %collective-permute-start.8 = (f32[8,128,128]{2,1,0:T(8,128)}, f32[8,128,128]{2,1,0:T(8,128)}, u32[]{:S(2)}, u32[]{:S(2)}) collective-permute-start(f32[8,128,128]{2,1,0:T(8,128)} %get-tuple-element.46), channel_id=1, source_target_pairs={{8,16},{9,17},{10,18},{11,19},{12,20},{13,21},{14,22},{15,23}} | collective-permute-start | bytes 1572872 | tf_op jit(solution)/shard_map/ppermute | solution.py:634
  143.1 1.5 copy-start.2
  144.6 36.6 %all-to-all-start.2 = ((f32[8,40,16,128]{3,2,1,0:T(8,128)}), f32[8,40,16,128]{3,2,1,0:T(8,128)}, u32[]{:S(2)}, u32[]{:S(2)}) async-start(f32[8,40,16,128]{3,2,1,0:T(8,128)} %bitcast.38), calls=%async_computation.2 | async-start | bytes 5242880 | tf_op jit(solution)/shard_map/all_to_all | solution.py:578
  150.2 4.0 %copy-start.22 = (f32[16,128,128]{2,1,0:T(8,128)S(1)}, f32[16,128,128]{2,1,0:T(8,128)}, u32[]{:S(2)}) copy-start(f32[16,128,128]{2,1,0:T(8,128)} %get-tuple-element.88) | copy-start | bytes 3145732
  150.2 4.0 %copy-start.24 = (f32[8,128,128]{2,1,0:T(8,128)S(1)}, f32[8,128,128]{2,1,0:T(8,128)}, u32[]{:S(2)}) copy-start(f32[8,128,128]{2,1,0:T(8,128)} %get-tuple-element.47) | copy-start | bytes 1572868
  152.2 2.0 collective-permute-start.3
  152.9 19.6 %collective-permute-start.10 = (f32[8,128,128]{2,1,0:T(8,128)S(1)}, f32[8,128,128]{2,1,0:T(8,128)S(1)}, u32[]{:S(2)}, u32[]{:S(2)}) collective-permute-start(f32[8,128,128]{2,1,0:T(8,128)S(1)} %get-tuple-element.55), channel_id=1, source_target_pairs={{16,24},{17,25},{18,26},{19,27},{20,28},{21,29},{22,30},{23,31}} | collective-permute-start | bytes 1572872 | tf_op jit(solution)/shard_map/ppermute | solution.py:634
  154.3 19.0 %collective-permute-start.7 = (f32[8,128,128]{2,1,0:T(8,128)S(1)}, f32[8,128,128]{2,1,0:T(8,128)S(1)}, u32[]{:S(2)}, u32[]{:S(2)}) collective-permute-start(f32[8,128,128]{2,1,0:T(8,128)S(1)} %multiply_add_fusion.3), channel_id=1, source_target_pairs={{8,16},{9,17},{10,18},{11,19},{12,20},{13,21},{14,22},{15,23}} | collective-permute-start | bytes 1572872 | tf_op jit(solution)/shard_map/ppermute | solution.py:634
  181.2 8.6 %copy-start.12 = (f32[8,128,128]{2,1,0:T(8,128)S(1)}, f32[8,128,128]{2,1,0:T(8,128)}, u32[]{:S(2)}) copy-start(f32[8,128,128]{2,1,0:T(8,128)} %add.116.refs_3_) | copy-start | bytes 1572868
  181.2 8.6 %copy-start.14 = (f32[8,128,128]{2,1,0:T(8,128)S(1)}, f32[8,128,128]{2,1,0:T(8,128)}, u32[]{:S(2)}) copy-start(f32[8,128,128]{2,1,0:T(8,128)} %get-tuple-element.83.refs_0_) | copy-start | bytes 1572868
  192.6 4.8 %copy-start.29 = (f32[8,128,128]{2,1,0:T(8,128)S(1)}, f32[8,128,128]{2,1,0:T(8,128)}, u32[]{:S(2)}) copy-start(f32[8,128,128]{2,1,0:T(8,128)} %get-tuple-element.49) | copy-start | bytes 1572868
  192.6 30.8 %copy-start.27 = (f32[8,128,128]{2,1,0:T(8,128)S(1)}, f32[8,128,128]{2,1,0:T(8,128)}, u32[]{:S(2)}) copy-start(f32[8,128,128]{2,1,0:T(8,128)} %get-tuple-element.69) | copy-start | bytes 1572868
  192.6 30.9 %copy-start.13 = (f32[8,128,128]{2,1,0:T(8,128)S(1)}, f32[8,128,128]{2,1,0:T(8,128)}, u32[]{:S(2)}) copy-start(f32[8,128,128]{2,1,0:T(8,128)} %get-tuple-element.84.refs_0_) | copy-start | bytes 1572868
  192.6 33.7 %all-to-all-start.3 = ((f32[8,40,8,128]{3,2,1,0:T(8,128)}), f32[8,40,8,128]{3,2,1,0:T(8,128)}, u32[]{:S(2)}, u32[]{:S(2)}) async-start(f32[8,40,8,128]{3,2,1,0:T(8,128)} %bitcast.19), calls=%async_computation.3 | async-start | bytes 2621440 | tf_op jit(solution)/shard_map/all_to_all | solution.py:578
  197.4 26.0 %collective-permute-start.9 = (f32[8,128,128]{2,1,0:T(8,128)S(1)}, f32[8,128,128]{2,1,0:T(8,128)S(1)}, u32[]{:S(2)}, u32[]{:S(2)}) collective-permute-start(f32[8,128,128]{2,1,0:T(8,128)S(1)} %copy-done.29), channel_id=1, source_target_pairs={{16,24},{17,25},{18,26},{19,27},{20,28},{21,29},{22,30},{23,31}} | collective-permute-start | bytes 1572872 | tf_op jit(solution)/shard_map/ppermute | solution.py:634
  226.3 4.7 %copy-start.31 = (f32[8,128,128]{2,1,0:T(8,128)S(1)}, f32[8,128,128]{2,1,0:T(8,128)}, u32[]{:S(2)}) copy-start(f32[8,128,128]{2,1,0:T(8,128)} %copy-done.30) | copy-start | bytes 1572868
  226.3 4.8 %copy-start.33 = (f32[8,128,128]{2,1,0:T(8,128)S(1)}, f32[8,128,128]{2,1,0:T(8,128)}, u32[]{:S(2)}) copy-start(f32[8,128,128]{2,1,0:T(8,128)} %copy-done.32) | copy-start | bytes 1572868
  226.3 4.8 %copy-start.25 = (f32[16,128,128]{2,1,0:T(8,128)S(1)}, f32[16,128,128]{2,1,0:T(8,128)}, u32[]{:S(2)}) copy-start(f32[16,128,128]{2,1,0:T(8,128)} %maximum_select_fusion) | copy-start | bytes 3145732
  226.3 21.6 %all-to-all-start.4 = ((f32[8,40,8,128]{3,2,1,0:T(8,128)}), f32[8,40,8,128]{3,2,1,0:T(8,128)S(1)}, u32[]{:S(2)}, u32[]{:S(2)}) async-start(f32[8,40,8,128]{3,2,1,0:T(8,128)} %bitcast.18), calls=%async_computation.4 | async-start | bytes 2621440 | tf_op jit(solution)/shard_map/all_to_all | solution.py:578
  247.9 1.1 copy-start.23

commit v3 on v2

--- a/solution.py
+++ b/solution.py
@@ -419,44 +419,7 @@
     )(pair[None], guess, initial, z_right, y_left)
 
 
-def relax_kernel(pushed_ref, early_ref, fine_ref, out_ref, work):
-    steps, planes = out_ref.shape[:2]
-    for n in range(steps):
-
-        def old(k):
-            return early_ref[:, k] if n == 0 else out_ref[n - 1, k]
-
-        def right(k):
-            return pushed_ref[n, k] + (2.0 / half) * old(k)
-
-        def keep(k, solved):
-            out_ref[n, k] = solved - old(k)
-
-        ghosts = [early_ref[:, planes + 2 * n + i] for i in (0, 1)]
-        solve(planes, right, lambda k: fine_ref[k], work, *ghosts, keep)
-
-
-def relax(pushed, early, fine_pivots):
-    steps, planes, parts, own, width_z = pushed.shape
-    step = 2 if parts % 2 == 0 else 1
-    block = pl.BlockSpec((steps, planes, step, own, width_z), lambda i: (0, 0, i, 0, 0))
-    return pl.pallas_call(
-        relax_kernel,
-        grid=(parts // step,),
-        out_shape=jax.ShapeDtypeStruct(pushed.shape, jnp.float32),
-        in_specs=[
-            block,
-            pl.BlockSpec((step, early.shape[1], own, width_z), lambda i: (i, 0, 0, 0)),
-            pl.BlockSpec((planes // 2 + 1, step, own, width_z), lambda i: (0, i, 0, 0)),
-        ],
-        out_specs=block,
-        scratch_shapes=[pltpu.VMEM((planes, step, own, width_z), jnp.float32)],
-        cost_estimate=cost(early),
-        compiler_params=room(60),
-    )(pushed, early, fine_pivots)
-
-
-def finish_kernel(q_steps, relaxed_ref, *refs):
+def finish_kernel(q_steps, pushed_ref, early_ref, *refs):
     *late_refs, fine_ref, wide_ref, y_ref, z_ref, out_ref, points, state, work = refs
     steps, count, width_y, width_z = out_ref.shape
     planes = points.shape[1]
@@ -470,9 +433,22 @@
     @pl.when(turn < q_steps)
     def _():
         place = pl.ds(turn * some, some)
+        for n in range(steps):
+
+            def old(k):
+                return early_ref[:, k] if n == 0 else points[n - 1, k, place]
+
+            def right(k):
+                return pushed_ref[n, k] + (2.0 / half) * old(k)
+
+            def keep(k, solved):
+                points[n, k, place] = solved - old(k)
+
+            ghosts = [early_ref[:, planes + 2 * n + i] for i in (0, 1)]
+            solve(planes, right, lambda k: fine_ref[k], work, *ghosts, keep)
 
         def sent(k, solved):
-            points[steps - 1, k, place] = relaxed_ref[steps - 1, k] + (solved - late(k))
+            points[steps - 1, k, place] = points[steps - 1, k, place] + (solved - late(k))
 
         ghosts = [late(planes + 2 * (steps - 1) + i) for i in (0, 1)]
         solve(planes, lambda k: (2.0 / wide) * late(k), lambda k: wide_ref[k], work, *ghosts, sent)
@@ -487,7 +463,7 @@
             def keep(k, solved):
                 fresh = solved - old(k)
                 state[k] = fresh
-                points[n, k, place] = relaxed_ref[n, k] + fresh
+                points[n, k, place] = points[n, k, place] + fresh
 
             ghosts = [late(planes + 2 * n + i) for i in (0, 1)]
             solve(planes, right, lambda k: fine_ref[k], work, *ghosts, keep)
@@ -506,8 +482,8 @@
             out_ref[n] = block.reshape(count, width_y, width_z)
 
 
-def finish(relaxed, lates, fine_pivots, wide_pivots, y_left, z_right):
-    steps, planes, parts, own, width_z = relaxed.shape
+def finish(pushed, early, lates, fine_pivots, wide_pivots, y_left, z_right):
+    steps, planes, parts, own, width_z = pushed.shape
     width_y = parts * own
     some = 2 if parts % 2 == 0 else 1
     count = 4 if planes % 4 == 0 else 1
@@ -523,7 +499,7 @@
             pl.BlockSpec((steps, planes, some, own, width_z), lambda i: (0, 0, ahead(i), 0, 0)),
             *(
                 pl.BlockSpec((some, *late.shape[1:]), lambda i: (ahead(i), 0, 0, 0))
-                for late in lates
+                for late in (early, *lates)
             ),
             pivots,
             pivots,
@@ -532,13 +508,13 @@
         ],
         out_specs=pl.BlockSpec((steps, count, width_y, width_z), lambda i: (0, after(i), 0, 0)),
         scratch_shapes=[
-            pltpu.VMEM(relaxed.shape, jnp.float32),
+            pltpu.VMEM(pushed.shape, jnp.float32),
             pltpu.VMEM((planes, some, own, width_z), jnp.float32),
             pltpu.VMEM((planes, some, own, width_z), jnp.float32),
         ],
-        cost_estimate=cost(relaxed),
+        cost_estimate=cost(pushed),
         compiler_params=room(60),
-    )(relaxed, *lates, fine_pivots, wide_pivots, y_left, z_right)
+    )(pushed, early, *lates, fine_pivots, wide_pivots, y_left, z_right)
 
 
 def per_device(forcing, coarse_guess, initial):
@@ -662,19 +638,19 @@
     fine_pivots, wide_pivots = (
         jnp.asarray(a.reshape(-1, parts, own, width_z)) for a in (fine_pivots, wide_pivots)
     )
-    relaxed = relax(pushed.reshape(steps, planes, parts, own, width_z), early, fine_pivots)
-    firsts, relaxed = lax.optimization_barrier((firsts, relaxed))
+    early, firsts = lax.optimization_barrier((early, firsts))
     lates = []
     for c in range(chunks):
         late = to_cells(
             wide, chunk_of(spectrum, c), tables, n_space, steps, carries[c : c + 1], (firsts[c],)
         )
-        late, relaxed, mine = lax.optimization_barrier((late, relaxed, mine))
+        late, mine = lax.optimization_barrier((late, mine))
         lates.append(swap(late))
     residual = jnp.concatenate(
         [jnp.where(pair == 0, mine, other), jnp.where(pair == 0, other, mine)], axis=0
     ).transpose(1, 0, 2)
-    points = finish(relaxed, lates, fine_pivots, wide_pivots, y_left, z_right)
+    pushed = pushed.reshape(steps, planes, parts, own, width_z)
+    points = finish(pushed, early, lates, fine_pivots, wide_pivots, y_left, z_right)
     return (points, residual[None])
 
 

time: 264 us -> 259 us (0.981)
  Pallas kernels: 57.6 us -> 51.9 us
    pallas_call x1 -> x0, Pallas kernels: 8.59 us -> none  [relax(): pl.pallas_call(relax_kernel, grid=(parts // step,), out_shape=jax.ShapeDt...]
    all_to_all x5, waiting for transfers between devices: 39 us -> 31.8 us  [swap(): lax.all_to_all(fields, ('space', 'pair'), split_axis=0, concat_axis=0, ti...]
    ppermute x6, waiting for transfers between devices: 40 us -> 46.1 us  [hop(): return lax.ppermute(sent, 'plane', [(place, place + 1)])]
    unnamed x76 -> x70, local copies, waits for them, and re-layouts: 18.5 us -> 17.7 us
  transfers between devices with their start and end apart: 16 -> 16, of which waited for: 11 -> 10; matrix products, arithmetic and copies ran while one was open for 8% -> 9% of each run, Pallas kernels for 7% -> 7%
where the time goes in v3:
time: 259 us; the launch traced here: 258 us
  waiting for transfers between devices  131 us (51%)
  Pallas kernels  51.9 us (20%)
  starting transfers between devices  35.8 us (14%)
  local copies, waits for them, and re-layouts  25.8 us (10%)
  other arithmetic  10.6 us (4%)
    ppermute x6, waiting for transfers between devices, hop(): return lax.ppermute(sent, 'plane', [(place, place + 1)])  46.1 us
    all_to_all x5, waiting for transfers between devices, swap(): lax.all_to_all(fields, ('space', 'pair'), split_axis=0, concat_axis=0, ti...  31.8 us
    all_to_all x5, starting transfers between devices, swap(): lax.all_to_all(fields, ('space', 'pair'), split_axis=0, concat_axis=0, ti...  25.8 us
    ppermute x1, waiting for transfers between devices, per_device(): lax.ppermute(guess[1], 'plane', [(i, (i + 1) % n_plane) for i in range(n_...  22.7 us
    unnamed x70, local copies, waits for them, and re-layouts  17.7 us
    ppermute x2, waiting for transfers between devices, per_device(): lax.ppermute(chunk_of(value[1], c), 'plane', [(i, i + 1) for i in range(n...  17 us
    pallas_call x1, Pallas kernels, finish(): pl.pallas_call(lambda *refs: finish_kernel(q_steps, *refs), grid=(q_steps...  16.3 us
    ppermute x2, waiting for transfers between devices, per_device(): swapped.append(lax.ppermute(other, 'pair', [(0, 1), (1, 0)]))  13.6 us
  transfers between devices with their start and end apart: 16, of which 10 were waited for; matrix products, arithmetic and copies ran while one was open for 9% of the time, Pallas kernels for 7%

profile of v3, /device:TPU:25, one launch (start us, length us, event | category | flops | bytes accessed | tf_op | source)
XLA Modules:
  0.0 258.0 jit_solution(13358945602490732455)
XLA Ops:
  0.6 5.3 %shard_map.167 = f32[8,48,16,128]{3,2,1,0:T(8,128)} custom-call(s32[1]{0:T(128)} %bitcast.refs_0_, f32[32,128,128]{2,1,0:T(8,128)} %bitcast.40, f32[32,128,128]{2,1,0:T(8,128)} %refs_2_.5, bf16[256,256]{1,0:T(8,128)(2,1)} %constant.45.clone.refs_3_.refs_1_.refs_7_, bf16[256,256]{1,0:T(8,128)(2,1)} %constant.46.clone.refs_4_.x_ref.refs_1_.refs_6_), custom_call_target="tpu_custom_call" | custom-call | flops 838860800 | bytes 4194304 | tf_op jit(solution)/shard_map/pallas_call | solution.py:401
  6.0 5.1 %all-to-all-start = ((f32[8,48,16,128]{3,2,1,0:T(8,128)}), f32[8,48,16,128]{3,2,1,0:T(8,128)}, u32[]{:S(2)}, u32[]{:S(2)}) async-start(f32[8,48,16,128]{3,2,1,0:T(8,128)} %shard_map.167), calls=%async_computation | async-start | bytes 6291456 | tf_op jit(solution)/shard_map/all_to_all | solution.py:554
  11.2 3.4 %copy-done.17 = f32[4,32,128,128]{3,2,1,0:T(8,128)S(1)} copy-done((f32[4,32,128,128]{3,2,1,0:T(8,128)S(1)}, f32[4,32,128,128]{3,2,1,0:T(8,128)}, u32[]{:S(2)}) %copy-start.17) | copy-done | bytes 8388632
  14.5 11.9 %shard_map.168 = (f32[4,32,128,128]{3,2,1,0:T(8,128)S(1)}, f32[8,40,16,128]{3,2,1,0:T(8,128)}) custom-call(f32[4,32,128,128]{3,2,1,0:T(8,128)S(1)} %copy-done.17, bf16[256,256]{1,0:T(8,128)(2,1)S(1)} %copy-done.13, bf16[256,256]{1,0:T(8,128)(2,1)S(1)} %copy-done.18, f32[17,8,16,128]{3,2,1,0:T(8,128)S(1)} %copy-done.12), custom_call_target="tpu_custom_call" | custom-call | flops 3355443200 | bytes 16777216 | tf_op jit(solution)/shard_map/pallas_call | solution.py:360
  26.5 3.3 %copy-done.3 = f32[4,32,128,128]{3,2,1,0:T(8,128)} copy-done((f32[4,32,128,128]{3,2,1,0:T(8,128)}, f32[4,32,128,128]{3,2,1,0:T(8,128)S(1)}, u32[]{:S(2)}) %copy-start.3) | copy-done | bytes 8388632
  29.8 18.0 %all-to-all-done = f32[8,48,16,128]{3,2,1,0:T(8,128)} async-done(((f32[8,48,16,128]{3,2,1,0:T(8,128)}), f32[8,48,16,128]{3,2,1,0:T(8,128)}, u32[]{:S(2)}, u32[]{:S(2)}) %all-to-all-start) | async-done | bytes 3145760 | tf_op jit(solution)/shard_map/all_to_all | solution.py:554
  47.8 4.8 %all-to-all-start.1 = ((f32[8,40,16,128]{3,2,1,0:T(8,128)}), f32[8,40,16,128]{3,2,1,0:T(8,128)}, u32[]{:S(2)}, u32[]{:S(2)}) async-start(f32[8,40,16,128]{3,2,1,0:T(8,128)} %get-tuple-element.36), calls=%async_computation.1 | async-start | bytes 5242880 | tf_op jit(solution)/shard_map/all_to_all | solution.py:554
  52.6 2.9 %copy.20 = f32[4,2,48,16,128]{4,2,0,3,1:T(8,128)S(1)} copy(f32[4,2,48,16,128]{4,3,2,1,0:T(8,128)} %bitcast.2) | data formatting | bytes 6291456 | tf_op jit(solution)/shard_map/optimization_barrier | solution.py:571
  55.4 1.0 fusion.2.guess_ref
  56.5 0.1 slice_bitcast_fusion
  56.6 1.3 copy-done
  57.9 0.1 dynamic_slice.3
  58.0 0.1 broadcast_add_fusion.1
  58.1 1.9 fusion.8
  59.9 22.7 %collective-permute-done.before_ref = f32[16,128,128]{2,1,0:T(8,128)S(1)} collective-permute-done((f32[16,128,128]{2,1,0:T(8,128)S(1)}, f32[16,128,128]{2,1,0:T(8,128)S(1)}, u32[]{:S(2)}, u32[]{:S(2)}) %collective-permute-start) | collective-permute-done | bytes 1048608 | tf_op jit(solution)/shard_map/ppermute | solution.py:575
  82.6 1.0 all-to-all-done.1
  83.6 1.6 copy-done.1
  85.2 9.0 %shard_map.169 = (f32[2,16,128,128]{3,2,1,0:T(8,128)S(1)}, f32[16,128,128]{2,1,0:T(8,128)S(1)}, f32[2,16,4,8,128]{4,3,2,1,0:T(8,128)S(1)}) custom-call(f32[4,2,640,128]{3,2,1,0:T(8,128)} %bitcast.7.arrived_ref, f32[16,128,128]{2,1,0:T(8,128)S(1)} %collective-permute-done.before_ref, f32[2,16,128,128]{3,2,1,0:T(8,128)S(1)} %copy-done.1, ...), custom_call_target="tpu_custom_call" | custom-call | flops 1468006400 | bytes 7340032 | tf_op jit(solution)/shard_map/pallas_call | solution.py:183
  94.3 0.1 slice_bitcast_fusion.2
  94.3 0.7 copy-done.14
  95.1 1.3 copy-done.5
  96.4 1.3 collective-permute-start.2
  97.7 2.9 %copy.18 = f32[4,2,48,16,128]{4,2,0,1,3:T(8,128)S(1)} copy(f32[4,2,48,16,128]{4,3,2,1,0:T(8,128)} %bitcast.2) | data formatting | bytes 6291456 | tf_op jit(solution)/shard_map/optimization_barrier | solution.py:571
  100.7 0.6 convolution_bitcast_fusion
  101.3 1.3 collective-permute-start.1
  102.6 8.8 %collective-permute-done.2 = f32[8,128,128]{2,1,0:T(8,128)} collective-permute-done((f32[8,128,128]{2,1,0:T(8,128)S(1)}, f32[8,128,128]{2,1,0:T(8,128)}, u32[]{:S(2)}, u32[]{:S(2)}) %collective-permute-start.2) | collective-permute-done | bytes 524320 | tf_op jit(solution)/shard_map/ppermute | solution.py:597
  111.4 1.4 slice_select_fusion.2
  112.8 0.1 multiply_add_fusion.5
  112.9 0.9 collective-permute-start.4
  113.8 0.5 collective-permute-start.5
  114.2 8.3 %collective-permute-done.1 = f32[8,128,128]{2,1,0:T(8,128)S(1)} collective-permute-done((f32[8,128,128]{2,1,0:T(8,128)S(1)}, f32[8,128,128]{2,1,0:T(8,128)S(1)}, u32[]{:S(2)}, u32[]{:S(2)}) %collective-permute-start.1) | collective-permute-done | bytes 524320 | tf_op jit(solution)/shard_map/ppermute | solution.py:597
  122.5 1.4 multiply_add_fusion.4
  123.9 0.1 broadcast_select_fusion.2
  124.0 0.5 collective-permute-start.6
  124.5 0.5 collective-permute-done.5
  125.0 13.1 %collective-permute-done.6 = f32[8,128,128]{2,1,0:T(8,128)S(1)} collective-permute-done((f32[8,128,128]{2,1,0:T(8,128)S(1)}, f32[8,128,128]{2,1,0:T(8,128)S(1)}, u32[]{:S(2)}, u32[]{:S(2)}) %collective-permute-start.6) | collective-permute-done | bytes 524320 | tf_op jit(solution)/shard_map/ppermute | solution.py:620
  138.1 0.8 copy-done.30
  138.9 3.7 %shard_map.170 = f32[4,2,640,128]{3,2,1,0:T(8,128)S(1)} custom-call(f32[16,128,128]{2,1,0:T(8,128)S(1)} %get-tuple-element.86.spectrum_ref.refs_0_, bf16[256,256]{1,0:T(8,128)(2,1)S(1)} %copy-done.4, bf16[64,1024]{1,0:T(8,128)(2,1)S(1)} %copy-done.9, f32[8,128,128]{2,1,0:T(8,128)S(1)} %get-tuple-element.48.refs_3_, ...), custom_call_target="tpu_custom_call" | custom-call | flops 838860800 | bytes 4194304 | tf_op jit(solution)/shard_map/pallas_call | solution.py:266
  142.6 1.5 copy-done.2
  144.1 5.6 %all-to-all-start.2 = ((f32[8,40,16,128]{3,2,1,0:T(8,128)}), f32[8,40,16,128]{3,2,1,0:T(8,128)}, u32[]{:S(2)}, u32[]{:S(2)}) async-start(f32[8,40,16,128]{3,2,1,0:T(8,128)} %bitcast.38), calls=%async_computation.2 | async-start | bytes 5242880 | tf_op jit(solution)/shard_map/all_to_all | solution.py:554
  149.7 0.7 collective-permute-start.3
  150.4 0.7 collective-permute-start.8
  151.1 2.8 %multiply_add_fusion = (f32[8,128,128]{2,1,0:T(8,128)S(1)}, f32[8,128,128]{2,1,0:T(8,128)S(1)}, f32[8,128,128]{2,1,0:T(8,128)}) fusion(f32[8,128,128]{2,1,0:T(8,128)S(1)} %get-tuple-element.53.refs_4_, f32[16,128,128]{2,1,0:T(8,128)} %get-tuple-element.84, f32[16,128,128]{2,1,0:T(8,128)S(1)} %get-tuple-element.38, f32[8,128,128]{2,1,0:T(8,128)} %copy-done.25, ...), kind=kLoop, calls=%fused_computation.21 | loop fusion | flops 1179648 | bytes 6291456 | tf_op jit(solution)/shard_map/add | solution.py:607
  154.0 1.3 collective-permute-start.9
  155.3 1.0 fusion.13
  156.3 1.6 collective-permute-start.7
  157.9 1.1 maximum_select_fusion
  159.0 32.0 %collective-permute-done.9 = f32[8,128,128]{2,1,0:T(8,128)S(1)} collective-permute-done((f32[8,128,128]{2,1,0:T(8,128)S(1)}, f32[8,128,128]{2,1,0:T(8,128)S(1)}, u32[]{:S(2)}, u32[]{:S(2)}) %collective-permute-start.9) | collective-permute-done | bytes 524320 | tf_op jit(solution)/shard_map/ppermute | solution.py:610
  191.0 0.1 add.115.refs_3_
  191.1 2.8 %shard_map.171 = f32[4,2,320,128]{3,2,1,0:T(8,128)} custom-call(f32[8,128,128]{2,1,0:T(8,128)S(1)} %copy-done.11, bf16[256,256]{1,0:T(8,128)(2,1)S(1)} %copy-done.4, bf16[64,1024]{1,0:T(8,128)(2,1)S(1)} %copy-done.9, f32[8,128,128]{2,1,0:T(8,128)S(1)} %add.115.refs_3_, f32[8,128,128]{2,1,0:T(8,128)S(1)} %get-tuple-element.53.refs_4_), custom_call_target="tpu_custom_call" | custom-call | flops 419430400 | bytes 2097152 | tf_op jit(solution)/shard_map/pallas_call | solution.py:266
  193.9 5.4 %all-to-all-start.3 = ((f32[8,40,8,128]{3,2,1,0:T(8,128)}), f32[8,40,8,128]{3,2,1,0:T(8,128)}, u32[]{:S(2)}, u32[]{:S(2)}) async-start(f32[8,40,8,128]{3,2,1,0:T(8,128)} %bitcast.18), calls=%async_computation.3 | async-start | bytes 2621440 | tf_op jit(solution)/shard_map/all_to_all | solution.py:554
  199.4 1.2 multiply_add_fusion.1
  200.6 1.3 collective-permute-start.10
  201.9 14.1 %collective-permute-done.10 = f32[8,128,128]{2,1,0:T(8,128)S(1)} collective-permute-done((f32[8,128,128]{2,1,0:T(8,128)S(1)}, f32[8,128,128]{2,1,0:T(8,128)S(1)}, u32[]{:S(2)}, u32[]{:S(2)}) %collective-permute-start.10) | collective-permute-done | bytes 524320 | tf_op jit(solution)/shard_map/ppermute | solution.py:610
  216.0 0.1 add.116.refs_3_
  216.1 2.8 %shard_map.172 = f32[4,2,320,128]{3,2,1,0:T(8,128)} custom-call(f32[8,128,128]{2,1,0:T(8,128)S(1)} %copy-done.10, bf16[256,256]{1,0:T(8,128)(2,1)S(1)} %copy-done.4, bf16[64,1024]{1,0:T(8,128)(2,1)S(1)} %copy-done.9, f32[8,128,128]{2,1,0:T(8,128)S(1)} %add.116.refs_3_, f32[8,128,128]{2,1,0:T(8,128)S(1)} %get-tuple-element.56.refs_4_), custom_call_target="tpu_custom_call" | custom-call | flops 419430400 | bytes 2097152 | tf_op jit(solution)/shard_map/pallas_call | solution.py:266
  218.9 4.8 %all-to-all-start.4 = ((f32[8,40,8,128]{3,2,1,0:T(8,128)}), f32[8,40,8,128]{3,2,1,0:T(8,128)S(1)}, u32[]{:S(2)}, u32[]{:S(2)}) async-start(f32[8,40,8,128]{3,2,1,0:T(8,128)} %bitcast.19), calls=%async_computation.4 | async-start | bytes 2621440 | tf_op jit(solution)/shard_map/all_to_all | solution.py:554
  223.7 1.1 constant_dynamic-update-slice_fusion
  224.8 0.2 broadcast_select_fusion.1
  225.0 0.2 maximum_bitcast_fusion
  225.2 2.5 copy.22
  227.8 12.8 %all-to-all-done.4.refs_3_ = f32[8,40,8,128]{3,2,1,0:T(8,128)S(1)} async-done(((f32[8,40,8,128]{3,2,1,0:T(8,128)}), f32[8,40,8,128]{3,2,1,0:T(8,128)S(1)}, u32[]{:S(2)}, u32[]{:S(2)}) %all-to-all-start.4) | async-done | bytes 1310752 | tf_op jit(solution)/shard_map/all_to_all | solution.py:554
  240.6 1.1 copy-done.21
  241.6 16.3 %shard_map.173 = f32[4,32,128,128]{3,2,1,0:T(8,128)} custom-call(f32[4,32,8,16,128]{4,3,2,1,0:T(8,128)} %bitcast.39, f32[8,40,16,128]{3,2,1,0:T(8,128)} %all-to-all-done.2.refs_1_, f32[8,40,8,128]{3,2,1,0:T(8,128)} %all-to-all-done.3.refs_2_, f32[8,40,8,128]{3,2,1,0:T(8,128)} %copy-done.21, f32[17,8,16,128]{3,2,1,0:T(8,128)} %constant.49.clone.refs_3_.refs_4_, ...), custom_call_target="tpu_custom_call" | custom-call | flops 3355443200 | bytes 16777216 | tf_op jit(solution)/shard_map/pallas_call | solution.py:494
  (67 shorter events, 0.2 us)
Async XLA Ops:
  6.0 5.2 %copy-start.12 = (f32[17,8,16,128]{3,2,1,0:T(8,128)S(1)}, f32[17,8,16,128]{3,2,1,0:T(8,128)}, u32[]{:S(2)}) copy-start(f32[17,8,16,128]{3,2,1,0:T(8,128)} %constant.49.clone.refs_3_.refs_4_) | copy-start | bytes 3342340
  6.0 5.2 %copy-start.13 = (bf16[256,256]{1,0:T(8,128)(2,1)S(1)}, bf16[256,256]{1,0:T(8,128)(2,1)}, u32[]{:S(2)}) copy-start(bf16[256,256]{1,0:T(8,128)(2,1)} %constant.45.clone.refs_3_.refs_1_.refs_7_) | copy-start | bytes 393220
  6.0 5.2 %copy-start.18 = (bf16[256,256]{1,0:T(8,128)(2,1)S(1)}, bf16[256,256]{1,0:T(8,128)(2,1)}, u32[]{:S(2)}) copy-start(bf16[256,256]{1,0:T(8,128)(2,1)} %constant.47.clone.refs_2_) | copy-start | bytes 393220
  6.0 41.8 %all-to-all-start = ((f32[8,48,16,128]{3,2,1,0:T(8,128)}), f32[8,48,16,128]{3,2,1,0:T(8,128)}, u32[]{:S(2)}, u32[]{:S(2)}) async-start(f32[8,48,16,128]{3,2,1,0:T(8,128)} %shard_map.167), calls=%async_computation | async-start | bytes 6291456 | tf_op jit(solution)/shard_map/all_to_all | solution.py:554
  11.2 3.4 %copy-start.17 = (f32[4,32,128,128]{3,2,1,0:T(8,128)S(1)}, f32[4,32,128,128]{3,2,1,0:T(8,128)}, u32[]{:S(2)}) copy-start(f32[4,32,128,128]{3,2,1,0:T(8,128)} %refs_0_) | copy-start | bytes 25165828
  26.5 3.3 %copy-start.3 = (f32[4,32,128,128]{3,2,1,0:T(8,128)}, f32[4,32,128,128]{3,2,1,0:T(8,128)S(1)}, u32[]{:S(2)}) copy-start(f32[4,32,128,128]{3,2,1,0:T(8,128)S(1)} %get-tuple-element.47) | copy-start | bytes 25165828
  47.8 35.8 %all-to-all-start.1 = ((f32[8,40,16,128]{3,2,1,0:T(8,128)}), f32[8,40,16,128]{3,2,1,0:T(8,128)}, u32[]{:S(2)}, u32[]{:S(2)}) async-start(f32[8,40,16,128]{3,2,1,0:T(8,128)} %get-tuple-element.36), calls=%async_computation.1 | async-start | bytes 5242880 | tf_op jit(solution)/shard_map/all_to_all | solution.py:554
  52.6 2.9 %copy-start.31 = (f32[4,32,128,1,1]{2,1,0,4,3:T(8,128)S(1)}, f32[4,32,128,1,1]{2,1,0,4,3:T(8,128)}, u32[]{:S(2)}) copy-start(f32[4,32,128,1,1]{2,1,0,4,3:T(8,128)} %constant.58) | copy-start | bytes 196612
  56.5 1.4 copy-start.33
  56.6 1.3 copy-start
  57.9 25.7 %copy-start.4 = (bf16[256,256]{1,0:T(8,128)(2,1)S(1)}, bf16[256,256]{1,0:T(8,128)(2,1)}, u32[]{:S(2)}) copy-start(bf16[256,256]{1,0:T(8,128)(2,1)} %constant.46.clone.refs_4_.x_ref.refs_1_.refs_6_) | copy-start | bytes 393220
  57.9 25.7 %copy-start.9 = (bf16[64,1024]{1,0:T(8,128)(2,1)S(1)}, bf16[64,1024]{1,0:T(8,128)(2,1)}, u32[]{:S(2)}) copy-start(bf16[64,1024]{1,0:T(8,128)(2,1)} %constant.50.clone.ghost_ref.refs_2_) | copy-start | bytes 393220
  57.9 25.7 %copy-start.16 = (bf16[512,96]{1,0:T(8,128)(2,1)S(1)}, bf16[512,96]{1,0:T(8,128)(2,1)}, u32[]{:S(2)}) copy-start(bf16[512,96]{1,0:T(8,128)(2,1)} %constant.51.clone.kick_ref) | copy-start | bytes 294916
  57.9 24.7 %collective-permute-start = (f32[16,128,128]{2,1,0:T(8,128)S(1)}, f32[16,128,128]{2,1,0:T(8,128)S(1)}, u32[]{:S(2)}, u32[]{:S(2)}) collective-permute-start(f32[16,128,128]{2,1,0:T(8,128)S(1)} %slice_bitcast_fusion), channel_id=1, source_target_pairs={{0,8},{8,16},{16,24},{24,0},{1,9},{9,17},{17,25},{25,1},{2,10},{10... | collective-permute-start | bytes 3145736 | tf_op jit(solution)/shard_map/ppermute | solution.py:575
  82.6 11.6 %copy-start.7 = (f32[16,128,128]{2,1,0:T(8,128)}, f32[16,128,128]{2,1,0:T(8,128)S(1)}, u32[]{:S(2)}) copy-start(f32[16,128,128]{2,1,0:T(8,128)S(1)} %collective-permute-done.before_ref) | copy-start | bytes 3145732
  83.6 1.6 copy-start.1
  94.3 0.8 copy-start.14
  95.1 1.3 copy-start.5
  96.4 15.0 %collective-permute-start.2 = (f32[8,128,128]{2,1,0:T(8,128)S(1)}, f32[8,128,128]{2,1,0:T(8,128)}, u32[]{:S(2)}, u32[]{:S(2)}) collective-permute-start(f32[8,128,128]{2,1,0:T(8,128)S(1)} %get-tuple-element.78), channel_id=1, source_target_pairs={{0,8},{8,16},{16,24},{1,9},{9,17},{17,25},{2,10},{10,18},{18,26},{... | collective-permute-start | bytes 1572872 | tf_op jit(solution)/shard_map/ppermute | solution.py:597
  97.7 3.0 %copy-start.32 = (f32[4,2,16,128,1]{3,2,0,4,1:T(8,128)S(1)}, f32[4,2,16,128,1]{3,2,0,4,1:T(8,128)}, u32[]{:S(2)}) copy-start(f32[4,2,16,128,1]{3,2,0,4,1:T(8,128)} %constant.57) | copy-start | bytes 196612
  100.7 10.7 %copy-start.8 = (f32[16,128,128]{2,1,0:T(8,128)S(1)}, f32[16,128,128]{2,1,0:T(8,128)}, u32[]{:S(2)}) copy-start(f32[16,128,128]{2,1,0:T(8,128)} %copy-done.7) | copy-start | bytes 3145732
  100.7 10.7 %copy-start.24 = (f32[16,128,128]{2,1,0:T(8,128)S(1)}, f32[16,128,128]{2,1,0:T(8,128)}, u32[]{:S(2)}) copy-start(f32[16,128,128]{2,1,0:T(8,128)} %get-tuple-element.85) | copy-start | bytes 3145732
  101.3 21.2 %collective-permute-start.1 = (f32[8,128,128]{2,1,0:T(8,128)S(1)}, f32[8,128,128]{2,1,0:T(8,128)S(1)}, u32[]{:S(2)}, u32[]{:S(2)}) collective-permute-start(f32[8,128,128]{2,1,0:T(8,128)S(1)} %get-tuple-element.77), channel_id=1, source_target_pairs={{0,8},{8,16},{16,24},{1,9},{9,17},{17,25},{2,10},{10,18},{18,26},{... | collective-permute-start | bytes 1572872 | tf_op jit(solution)/shard_map/ppermute | solution.py:597
  111.4 1.4 copy-start.19
  112.9 9.6 %collective-permute-start.4 = (f32[8,128,128]{2,1,0:T(8,128)S(1)}, f32[8,128,128]{2,1,0:T(8,128)S(1)}, u32[]{:S(2)}, u32[]{:S(2)}) collective-permute-start(f32[8,128,128]{2,1,0:T(8,128)S(1)} %multiply_add_fusion.5), channel_id=1, source_target_pairs={{0,8},{1,9},{2,10},{3,11},{4,12},{5,13},{6,14},{7,15}} | collective-permute-start | bytes 1572872 | tf_op jit(solution)/shard_map/ppermute | solution.py:610
  113.8 25.1 %copy-start.15 = (f32[2,16,4,8,128]{4,3,2,1,0:T(8,128)S(1)}, f32[2,16,4,8,128]{4,3,2,1,0:T(8,128)}, u32[]{:S(2)}) copy-start(f32[2,16,4,8,128]{4,3,2,1,0:T(8,128)} %copy-done.14) | copy-start | bytes 1572868
  113.8 11.2 %collective-permute-start.5 = (f32[8,128,128]{2,1,0:T(8,128)S(1)}, f32[8,128,128]{2,1,0:T(8,128)S(1)}, u32[]{:S(2)}, u32[]{:S(2)}) collective-permute-start(f32[8,128,128]{2,1,0:T(8,128)S(1)} %get-tuple-element.71), channel_id=1, source_target_pairs={{0,4},{4,0},{1,5},{5,1},{2,6},{6,2},{3,7},{7,3},{8,12},{12,8},{9,1... | collective-permute-start | bytes 1572872 | tf_op jit(solution)/shard_map/ppermute | solution.py:620
  122.5 1.4 copy-start.25
  122.5 16.4 %copy-start.6 = (f32[2,16,128,128]{3,2,1,0:T(8,128)S(1)}, f32[2,16,128,128]{3,2,1,0:T(8,128)}, u32[]{:S(2)}) copy-start(f32[2,16,128,128]{3,2,1,0:T(8,128)} %copy-done.5) | copy-start | bytes 6291460
  124.0 14.1 %collective-permute-start.6 = (f32[8,128,128]{2,1,0:T(8,128)S(1)}, f32[8,128,128]{2,1,0:T(8,128)S(1)}, u32[]{:S(2)}, u32[]{:S(2)}) collective-permute-start(f32[8,128,128]{2,1,0:T(8,128)S(1)} %broadcast_select_fusion.2), channel_id=1, source_target_pairs={{0,4},{4,0},{1,5},{5,1},{2,6},{6,2},{3,7},{7,3},{8,12},{12,8},{9,1... | collective-permute-start | bytes 1572872 | tf_op jit(solution)/shard_map/ppermute | solution.py:620
  125.0 13.1 %copy-start.28 = (f32[8,128,128]{2,1,0:T(8,128)}, f32[8,128,128]{2,1,0:T(8,128)S(1)}, u32[]{:S(2)}) copy-start(f32[8,128,128]{2,1,0:T(8,128)S(1)} %collective-permute-done.5) | copy-start | bytes 1572868
  138.1 0.8 copy-start.30
  142.6 1.5 copy-start.2
  144.1 47.0 %all-to-all-start.2 = ((f32[8,40,16,128]{3,2,1,0:T(8,128)}), f32[8,40,16,128]{3,2,1,0:T(8,128)}, u32[]{:S(2)}, u32[]{:S(2)}) async-start(f32[8,40,16,128]{3,2,1,0:T(8,128)} %bitcast.38), calls=%async_computation.2 | async-start | bytes 5242880 | tf_op jit(solution)/shard_map/all_to_all | solution.py:554
  149.7 1.4 collective-permute-start.3
  150.4 0.7 collective-permute-start.8
  151.1 2.9 %copy-start.26 = (f32[8,128,128]{2,1,0:T(8,128)}, f32[8,128,128]{2,1,0:T(8,128)S(1)}, u32[]{:S(2)}) copy-start(f32[8,128,128]{2,1,0:T(8,128)S(1)} %collective-permute-done.3) | copy-start | bytes 1572868
  154.0 37.0 %collective-permute-start.9 = (f32[8,128,128]{2,1,0:T(8,128)S(1)}, f32[8,128,128]{2,1,0:T(8,128)S(1)}, u32[]{:S(2)}, u32[]{:S(2)}) collective-permute-start(f32[8,128,128]{2,1,0:T(8,128)S(1)} %get-tuple-element.52), channel_id=1, source_target_pairs={{16,24},{17,25},{18,26},{19,27},{20,28},{21,29},{22,30},{23,31}} | collective-permute-start | bytes 1572872 | tf_op jit(solution)/shard_map/ppermute | solution.py:610
  156.3 34.7 %copy-start.11 = (f32[8,128,128]{2,1,0:T(8,128)S(1)}, f32[8,128,128]{2,1,0:T(8,128)}, u32[]{:S(2)}) copy-start(f32[8,128,128]{2,1,0:T(8,128)} %get-tuple-element.80.refs_0_) | copy-start | bytes 1572868
  156.3 43.0 %collective-permute-start.7 = (f32[8,128,128]{2,1,0:T(8,128)}, f32[8,128,128]{2,1,0:T(8,128)}, u32[]{:S(2)}, u32[]{:S(2)}) collective-permute-start(f32[8,128,128]{2,1,0:T(8,128)} %get-tuple-element.81), channel_id=1, source_target_pairs={{8,16},{9,17},{10,18},{11,19},{12,20},{13,21},{14,22},{15,23}} | collective-permute-start | bytes 1572872 | tf_op jit(solution)/shard_map/ppermute | solution.py:610
  193.9 5.5 %copy-start.20 = (f32[16,128,128]{2,1,0:T(8,128)S(1)}, f32[16,128,128]{2,1,0:T(8,128)}, u32[]{:S(2)}) copy-start(f32[16,128,128]{2,1,0:T(8,128)} %get-tuple-element.84) | copy-start | bytes 3145732
  193.9 5.5 %copy-start.22 = (f32[8,128,128]{2,1,0:T(8,128)S(1)}, f32[8,128,128]{2,1,0:T(8,128)}, u32[]{:S(2)}) copy-start(f32[8,128,128]{2,1,0:T(8,128)} %get-tuple-element.45) | copy-start | bytes 1572868
  193.9 5.5 %copy-start.27 = (f32[8,128,128]{2,1,0:T(8,128)S(1)}, f32[8,128,128]{2,1,0:T(8,128)}, u32[]{:S(2)}) copy-start(f32[8,128,128]{2,1,0:T(8,128)} %copy-done.26) | copy-start | bytes 1572868
  193.9 25.0 %all-to-all-start.3 = ((f32[8,40,8,128]{3,2,1,0:T(8,128)}), f32[8,40,8,128]{3,2,1,0:T(8,128)}, u32[]{:S(2)}, u32[]{:S(2)}) async-start(f32[8,40,8,128]{3,2,1,0:T(8,128)} %bitcast.18), calls=%async_computation.3 | async-start | bytes 2621440 | tf_op jit(solution)/shard_map/all_to_all | solution.py:554
  199.3 16.7 %copy-start.10 = (f32[8,128,128]{2,1,0:T(8,128)S(1)}, f32[8,128,128]{2,1,0:T(8,128)}, u32[]{:S(2)}) copy-start(f32[8,128,128]{2,1,0:T(8,128)} %get-tuple-element.79.refs_0_) | copy-start | bytes 1572868
  200.6 15.4 %collective-permute-start.10 = (f32[8,128,128]{2,1,0:T(8,128)S(1)}, f32[8,128,128]{2,1,0:T(8,128)S(1)}, u32[]{:S(2)}, u32[]{:S(2)}) collective-permute-start(f32[8,128,128]{2,1,0:T(8,128)S(1)} %get-tuple-element.55), channel_id=1, source_target_pairs={{16,24},{17,25},{18,26},{19,27},{20,28},{21,29},{22,30},{23,31}} | collective-permute-start | bytes 1572872 | tf_op jit(solution)/shard_map/ppermute | solution.py:610
  218.9 4.8 %copy-start.29 = (f32[8,128,128]{2,1,0:T(8,128)S(1)}, f32[8,128,128]{2,1,0:T(8,128)}, u32[]{:S(2)}) copy-start(f32[8,128,128]{2,1,0:T(8,128)} %copy-done.28) | copy-start | bytes 1572868
  218.9 6.0 %copy-start.23 = (f32[16,128,128]{2,1,0:T(8,128)S(1)}, f32[16,128,128]{2,1,0:T(8,128)}, u32[]{:S(2)}) copy-start(f32[16,128,128]{2,1,0:T(8,128)} %maximum_select_fusion) | copy-start | bytes 3145732
  218.9 21.7 %all-to-all-start.4 = ((f32[8,40,8,128]{3,2,1,0:T(8,128)}), f32[8,40,8,128]{3,2,1,0:T(8,128)S(1)}, u32[]{:S(2)}, u32[]{:S(2)}) async-start(f32[8,40,8,128]{3,2,1,0:T(8,128)} %bitcast.19), calls=%async_computation.4 | async-start | bytes 2621440 | tf_op jit(solution)/shard_map/all_to_all | solution.py:554
  240.6 1.1 copy-start.21

commit v4 on v3

--- a/solution.py
+++ b/solution.py
@@ -485,8 +485,8 @@
 def finish(pushed, early, lates, fine_pivots, wide_pivots, y_left, z_right):
     steps, planes, parts, own, width_z = pushed.shape
     width_y = parts * own
-    some = 2 if parts % 2 == 0 else 1
-    count = 4 if planes % 4 == 0 else 1
+    some = next(c for c in (4, 2, 1) if parts % c == 0)
+    count = next(c for c in (8, 4, 1) if planes % c == 0)
     q_steps, x_steps = parts // some, planes // count
     ahead = lambda i: jnp.minimum(i, q_steps - 1)
     after = lambda i: jnp.maximum(i - q_steps, 0)

time: 259 us -> 258 us (level)
  no operation moved by 1% of the time
where the time goes in v4:
time: 258 us; the launch traced here: 257 us
  waiting for transfers between devices  131 us (51%)
  Pallas kernels  51.1 us (20%)
  starting transfers between devices  35.8 us (14%)
  local copies, waits for them, and re-layouts  25.8 us (10%)
  other arithmetic  10.6 us (4%)
    ppermute x6, waiting for transfers between devices, hop(): return lax.ppermute(sent, 'plane', [(place, place + 1)])  46.1 us
    all_to_all x5, waiting for transfers between devices, swap(): lax.all_to_all(fields, ('space', 'pair'), split_axis=0, concat_axis=0, ti...  31.8 us
    all_to_all x5, starting transfers between devices, swap(): lax.all_to_all(fields, ('space', 'pair'), split_axis=0, concat_axis=0, ti...  25.8 us
    ppermute x1, waiting for transfers between devices, per_device(): lax.ppermute(guess[1], 'plane', [(i, (i + 1) % n_plane) for i in range(n_...  22.7 us
    unnamed x70, local copies, waits for them, and re-layouts  17.7 us
    ppermute x2, waiting for transfers between devices, per_device(): lax.ppermute(chunk_of(value[1], c), 'plane', [(i, i + 1) for i in range(n...  17 us
    pallas_call x1, Pallas kernels, finish(): pl.pallas_call(lambda *refs: finish_kernel(q_steps, *refs), grid=(q_steps...  15.6 us
    ppermute x2, waiting for transfers between devices, per_device(): swapped.append(lax.ppermute(other, 'pair', [(0, 1), (1, 0)]))  13.6 us
  transfers between devices with their start and end apart: 16, of which 10 were waited for; matrix products, arithmetic and copies ran while one was open for 9% of the time, Pallas kernels for 7%

profile of v4, /device:TPU:25, one launch (start us, length us, event | category | flops | bytes accessed | tf_op | source)
XLA Modules:
  0.0 257.2 jit_solution(18086175816656786270)
XLA Ops:
  0.6 5.3 %shard_map.167 = f32[8,48,16,128]{3,2,1,0:T(8,128)} custom-call(s32[1]{0:T(128)} %bitcast.refs_0_, f32[32,128,128]{2,1,0:T(8,128)} %bitcast.40, f32[32,128,128]{2,1,0:T(8,128)} %refs_2_.5, bf16[256,256]{1,0:T(8,128)(2,1)} %constant.45.clone.refs_3_.refs_1_.refs_7_, bf16[256,256]{1,0:T(8,128)(2,1)} %constant.46.clone.refs_4_.x_ref.refs_1_.refs_6_), custom_call_target="tpu_custom_call" | custom-call | flops 838860800 | bytes 4194304 | tf_op jit(solution)/shard_map/pallas_call | solution.py:401
  6.0 5.1 %all-to-all-start = ((f32[8,48,16,128]{3,2,1,0:T(8,128)}), f32[8,48,16,128]{3,2,1,0:T(8,128)}, u32[]{:S(2)}, u32[]{:S(2)}) async-start(f32[8,48,16,128]{3,2,1,0:T(8,128)} %shard_map.167), calls=%async_computation | async-start | bytes 6291456 | tf_op jit(solution)/shard_map/all_to_all | solution.py:554
  11.2 3.4 %copy-done.17 = f32[4,32,128,128]{3,2,1,0:T(8,128)S(1)} copy-done((f32[4,32,128,128]{3,2,1,0:T(8,128)S(1)}, f32[4,32,128,128]{3,2,1,0:T(8,128)}, u32[]{:S(2)}) %copy-start.17) | copy-done | bytes 8388632
  14.5 11.9 %shard_map.168 = (f32[4,32,128,128]{3,2,1,0:T(8,128)S(1)}, f32[8,40,16,128]{3,2,1,0:T(8,128)}) custom-call(f32[4,32,128,128]{3,2,1,0:T(8,128)S(1)} %copy-done.17, bf16[256,256]{1,0:T(8,128)(2,1)S(1)} %copy-done.13, bf16[256,256]{1,0:T(8,128)(2,1)S(1)} %copy-done.18, f32[17,8,16,128]{3,2,1,0:T(8,128)S(1)} %copy-done.12), custom_call_target="tpu_custom_call" | custom-call | flops 3355443200 | bytes 16777216 | tf_op jit(solution)/shard_map/pallas_call | solution.py:360
  26.5 3.3 %copy-done.3 = f32[4,32,128,128]{3,2,1,0:T(8,128)} copy-done((f32[4,32,128,128]{3,2,1,0:T(8,128)}, f32[4,32,128,128]{3,2,1,0:T(8,128)S(1)}, u32[]{:S(2)}) %copy-start.3) | copy-done | bytes 8388632
  29.8 18.0 %all-to-all-done = f32[8,48,16,128]{3,2,1,0:T(8,128)} async-done(((f32[8,48,16,128]{3,2,1,0:T(8,128)}), f32[8,48,16,128]{3,2,1,0:T(8,128)}, u32[]{:S(2)}, u32[]{:S(2)}) %all-to-all-start) | async-done | bytes 3145760 | tf_op jit(solution)/shard_map/all_to_all | solution.py:554
  47.8 4.8 %all-to-all-start.1 = ((f32[8,40,16,128]{3,2,1,0:T(8,128)}), f32[8,40,16,128]{3,2,1,0:T(8,128)}, u32[]{:S(2)}, u32[]{:S(2)}) async-start(f32[8,40,16,128]{3,2,1,0:T(8,128)} %get-tuple-element.36), calls=%async_computation.1 | async-start | bytes 5242880 | tf_op jit(solution)/shard_map/all_to_all | solution.py:554
  52.6 2.9 %copy.20 = f32[4,2,48,16,128]{4,2,0,3,1:T(8,128)S(1)} copy(f32[4,2,48,16,128]{4,3,2,1,0:T(8,128)} %bitcast.2) | data formatting | bytes 6291456 | tf_op jit(solution)/shard_map/optimization_barrier | solution.py:571
  55.4 1.0 fusion.2.guess_ref
  56.5 0.1 slice_bitcast_fusion
  56.6 1.3 copy-done
  57.9 0.1 dynamic_slice.3
  58.0 0.1 broadcast_add_fusion.1
  58.1 1.9 fusion.8
  59.9 22.7 %collective-permute-done.before_ref = f32[16,128,128]{2,1,0:T(8,128)S(1)} collective-permute-done((f32[16,128,128]{2,1,0:T(8,128)S(1)}, f32[16,128,128]{2,1,0:T(8,128)S(1)}, u32[]{:S(2)}, u32[]{:S(2)}) %collective-permute-start) | collective-permute-done | bytes 1048608 | tf_op jit(solution)/shard_map/ppermute | solution.py:575
  82.6 1.0 all-to-all-done.1
  83.6 1.6 copy-done.1
  85.2 9.0 %shard_map.169 = (f32[2,16,128,128]{3,2,1,0:T(8,128)S(1)}, f32[16,128,128]{2,1,0:T(8,128)S(1)}, f32[2,16,4,8,128]{4,3,2,1,0:T(8,128)S(1)}) custom-call(f32[4,2,640,128]{3,2,1,0:T(8,128)} %bitcast.7.arrived_ref, f32[16,128,128]{2,1,0:T(8,128)S(1)} %collective-permute-done.before_ref, f32[2,16,128,128]{3,2,1,0:T(8,128)S(1)} %copy-done.1, ...), custom_call_target="tpu_custom_call" | custom-call | flops 1468006400 | bytes 7340032 | tf_op jit(solution)/shard_map/pallas_call | solution.py:183
  94.3 0.1 slice_bitcast_fusion.2
  94.3 0.7 copy-done.14
  95.1 1.3 copy-done.5
  96.4 1.3 collective-permute-start.2
  97.7 2.9 %copy.18 = f32[4,2,48,16,128]{4,2,0,1,3:T(8,128)S(1)} copy(f32[4,2,48,16,128]{4,3,2,1,0:T(8,128)} %bitcast.2) | data formatting | bytes 6291456 | tf_op jit(solution)/shard_map/optimization_barrier | solution.py:571
  100.7 0.6 convolution_bitcast_fusion
  101.3 1.3 collective-permute-start.1
  102.6 8.8 %collective-permute-done.2 = f32[8,128,128]{2,1,0:T(8,128)} collective-permute-done((f32[8,128,128]{2,1,0:T(8,128)S(1)}, f32[8,128,128]{2,1,0:T(8,128)}, u32[]{:S(2)}, u32[]{:S(2)}) %collective-permute-start.2) | collective-permute-done | bytes 524320 | tf_op jit(solution)/shard_map/ppermute | solution.py:597
  111.4 1.4 slice_select_fusion.2
  112.8 0.1 multiply_add_fusion.5
  112.9 0.9 collective-permute-start.4
  113.8 0.5 collective-permute-start.5
  114.2 8.3 %collective-permute-done.1 = f32[8,128,128]{2,1,0:T(8,128)S(1)} collective-permute-done((f32[8,128,128]{2,1,0:T(8,128)S(1)}, f32[8,128,128]{2,1,0:T(8,128)S(1)}, u32[]{:S(2)}, u32[]{:S(2)}) %collective-permute-start.1) | collective-permute-done | bytes 524320 | tf_op jit(solution)/shard_map/ppermute | solution.py:597
  122.5 1.4 multiply_add_fusion.4
  123.9 0.1 broadcast_select_fusion.2
  124.0 0.5 collective-permute-start.6
  124.5 0.5 collective-permute-done.5
  125.0 13.1 %collective-permute-done.6 = f32[8,128,128]{2,1,0:T(8,128)S(1)} collective-permute-done((f32[8,128,128]{2,1,0:T(8,128)S(1)}, f32[8,128,128]{2,1,0:T(8,128)S(1)}, u32[]{:S(2)}, u32[]{:S(2)}) %collective-permute-start.6) | collective-permute-done | bytes 524320 | tf_op jit(solution)/shard_map/ppermute | solution.py:620
  138.1 0.8 copy-done.30
  138.9 3.7 %shard_map.170 = f32[4,2,640,128]{3,2,1,0:T(8,128)S(1)} custom-call(f32[16,128,128]{2,1,0:T(8,128)S(1)} %get-tuple-element.86.spectrum_ref.refs_0_, bf16[256,256]{1,0:T(8,128)(2,1)S(1)} %copy-done.4, bf16[64,1024]{1,0:T(8,128)(2,1)S(1)} %copy-done.9, f32[8,128,128]{2,1,0:T(8,128)S(1)} %get-tuple-element.48.refs_3_, ...), custom_call_target="tpu_custom_call" | custom-call | flops 838860800 | bytes 4194304 | tf_op jit(solution)/shard_map/pallas_call | solution.py:266
  142.6 1.5 copy-done.2
  144.1 5.6 %all-to-all-start.2 = ((f32[8,40,16,128]{3,2,1,0:T(8,128)}), f32[8,40,16,128]{3,2,1,0:T(8,128)}, u32[]{:S(2)}, u32[]{:S(2)}) async-start(f32[8,40,16,128]{3,2,1,0:T(8,128)} %bitcast.38), calls=%async_computation.2 | async-start | bytes 5242880 | tf_op jit(solution)/shard_map/all_to_all | solution.py:554
  149.7 0.7 collective-permute-start.3
  150.4 0.7 collective-permute-start.8
  151.1 2.8 %multiply_add_fusion = (f32[8,128,128]{2,1,0:T(8,128)S(1)}, f32[8,128,128]{2,1,0:T(8,128)S(1)}, f32[8,128,128]{2,1,0:T(8,128)}) fusion(f32[8,128,128]{2,1,0:T(8,128)S(1)} %get-tuple-element.53.refs_4_, f32[16,128,128]{2,1,0:T(8,128)} %get-tuple-element.84, f32[16,128,128]{2,1,0:T(8,128)S(1)} %get-tuple-element.38, f32[8,128,128]{2,1,0:T(8,128)} %copy-done.25, ...), kind=kLoop, calls=%fused_computation.21 | loop fusion | flops 1179648 | bytes 6291456 | tf_op jit(solution)/shard_map/add | solution.py:607
  154.0 1.3 collective-permute-start.9
  155.3 1.0 fusion.13
  156.3 1.6 collective-permute-start.7
  157.9 1.1 maximum_select_fusion
  159.0 32.0 %collective-permute-done.9 = f32[8,128,128]{2,1,0:T(8,128)S(1)} collective-permute-done((f32[8,128,128]{2,1,0:T(8,128)S(1)}, f32[8,128,128]{2,1,0:T(8,128)S(1)}, u32[]{:S(2)}, u32[]{:S(2)}) %collective-permute-start.9) | collective-permute-done | bytes 524320 | tf_op jit(solution)/shard_map/ppermute | solution.py:610
  191.0 0.1 add.115.refs_3_
  191.1 2.8 %shard_map.171 = f32[4,2,320,128]{3,2,1,0:T(8,128)} custom-call(f32[8,128,128]{2,1,0:T(8,128)S(1)} %copy-done.11, bf16[256,256]{1,0:T(8,128)(2,1)S(1)} %copy-done.4, bf16[64,1024]{1,0:T(8,128)(2,1)S(1)} %copy-done.9, f32[8,128,128]{2,1,0:T(8,128)S(1)} %add.115.refs_3_, f32[8,128,128]{2,1,0:T(8,128)S(1)} %get-tuple-element.53.refs_4_), custom_call_target="tpu_custom_call" | custom-call | flops 419430400 | bytes 2097152 | tf_op jit(solution)/shard_map/pallas_call | solution.py:266
  193.9 5.4 %all-to-all-start.3 = ((f32[8,40,8,128]{3,2,1,0:T(8,128)}), f32[8,40,8,128]{3,2,1,0:T(8,128)}, u32[]{:S(2)}, u32[]{:S(2)}) async-start(f32[8,40,8,128]{3,2,1,0:T(8,128)} %bitcast.18), calls=%async_computation.3 | async-start | bytes 2621440 | tf_op jit(solution)/shard_map/all_to_all | solution.py:554
  199.4 1.2 multiply_add_fusion.1
  200.6 1.3 collective-permute-start.10
  201.9 14.1 %collective-permute-done.10 = f32[8,128,128]{2,1,0:T(8,128)S(1)} collective-permute-done((f32[8,128,128]{2,1,0:T(8,128)S(1)}, f32[8,128,128]{2,1,0:T(8,128)S(1)}, u32[]{:S(2)}, u32[]{:S(2)}) %collective-permute-start.10) | collective-permute-done | bytes 524320 | tf_op jit(solution)/shard_map/ppermute | solution.py:610
  216.0 0.1 add.116.refs_3_
  216.1 2.8 %shard_map.172 = f32[4,2,320,128]{3,2,1,0:T(8,128)} custom-call(f32[8,128,128]{2,1,0:T(8,128)S(1)} %copy-done.10, bf16[256,256]{1,0:T(8,128)(2,1)S(1)} %copy-done.4, bf16[64,1024]{1,0:T(8,128)(2,1)S(1)} %copy-done.9, f32[8,128,128]{2,1,0:T(8,128)S(1)} %add.116.refs_3_, f32[8,128,128]{2,1,0:T(8,128)S(1)} %get-tuple-element.56.refs_4_), custom_call_target="tpu_custom_call" | custom-call | flops 419430400 | bytes 2097152 | tf_op jit(solution)/shard_map/pallas_call | solution.py:266
  218.9 4.8 %all-to-all-start.4 = ((f32[8,40,8,128]{3,2,1,0:T(8,128)}), f32[8,40,8,128]{3,2,1,0:T(8,128)S(1)}, u32[]{:S(2)}, u32[]{:S(2)}) async-start(f32[8,40,8,128]{3,2,1,0:T(8,128)} %bitcast.19), calls=%async_computation.4 | async-start | bytes 2621440 | tf_op jit(solution)/shard_map/all_to_all | solution.py:554
  223.7 1.1 constant_dynamic-update-slice_fusion
  224.8 0.2 broadcast_select_fusion.1
  225.0 0.2 maximum_bitcast_fusion
  225.2 2.5 copy.22
  227.8 12.8 %all-to-all-done.4.refs_3_ = f32[8,40,8,128]{3,2,1,0:T(8,128)S(1)} async-done(((f32[8,40,8,128]{3,2,1,0:T(8,128)}), f32[8,40,8,128]{3,2,1,0:T(8,128)S(1)}, u32[]{:S(2)}, u32[]{:S(2)}) %all-to-all-start.4) | async-done | bytes 1310752 | tf_op jit(solution)/shard_map/all_to_all | solution.py:554
  240.6 1.1 copy-done.21
  241.6 15.6 %shard_map.173 = f32[4,32,128,128]{3,2,1,0:T(8,128)} custom-call(f32[4,32,8,16,128]{4,3,2,1,0:T(8,128)} %bitcast.39, f32[8,40,16,128]{3,2,1,0:T(8,128)} %all-to-all-done.2.refs_1_, f32[8,40,8,128]{3,2,1,0:T(8,128)} %all-to-all-done.3.refs_2_, f32[8,40,8,128]{3,2,1,0:T(8,128)} %copy-done.21, f32[17,8,16,128]{3,2,1,0:T(8,128)} %constant.49.clone.refs_3_.refs_4_, ...), custom_call_target="tpu_custom_call" | custom-call | flops 3355443200 | bytes 16777216 | tf_op jit(solution)/shard_map/pallas_call | solution.py:494
  (67 shorter events, 0.2 us)
Async XLA Ops:
  6.0 5.2 %copy-start.12 = (f32[17,8,16,128]{3,2,1,0:T(8,128)S(1)}, f32[17,8,16,128]{3,2,1,0:T(8,128)}, u32[]{:S(2)}) copy-start(f32[17,8,16,128]{3,2,1,0:T(8,128)} %constant.49.clone.refs_3_.refs_4_) | copy-start | bytes 3342340
  6.0 5.2 %copy-start.13 = (bf16[256,256]{1,0:T(8,128)(2,1)S(1)}, bf16[256,256]{1,0:T(8,128)(2,1)}, u32[]{:S(2)}) copy-start(bf16[256,256]{1,0:T(8,128)(2,1)} %constant.45.clone.refs_3_.refs_1_.refs_7_) | copy-start | bytes 393220
  6.0 5.2 %copy-start.18 = (bf16[256,256]{1,0:T(8,128)(2,1)S(1)}, bf16[256,256]{1,0:T(8,128)(2,1)}, u32[]{:S(2)}) copy-start(bf16[256,256]{1,0:T(8,128)(2,1)} %constant.47.clone.refs_2_) | copy-start | bytes 393220
  6.0 41.8 %all-to-all-start = ((f32[8,48,16,128]{3,2,1,0:T(8,128)}), f32[8,48,16,128]{3,2,1,0:T(8,128)}, u32[]{:S(2)}, u32[]{:S(2)}) async-start(f32[8,48,16,128]{3,2,1,0:T(8,128)} %shard_map.167), calls=%async_computation | async-start | bytes 6291456 | tf_op jit(solution)/shard_map/all_to_all | solution.py:554
  11.2 3.4 %copy-start.17 = (f32[4,32,128,128]{3,2,1,0:T(8,128)S(1)}, f32[4,32,128,128]{3,2,1,0:T(8,128)}, u32[]{:S(2)}) copy-start(f32[4,32,128,128]{3,2,1,0:T(8,128)} %refs_0_) | copy-start | bytes 25165828
  26.5 3.3 %copy-start.3 = (f32[4,32,128,128]{3,2,1,0:T(8,128)}, f32[4,32,128,128]{3,2,1,0:T(8,128)S(1)}, u32[]{:S(2)}) copy-start(f32[4,32,128,128]{3,2,1,0:T(8,128)S(1)} %get-tuple-element.47) | copy-start | bytes 25165828
  47.8 35.8 %all-to-all-start.1 = ((f32[8,40,16,128]{3,2,1,0:T(8,128)}), f32[8,40,16,128]{3,2,1,0:T(8,128)}, u32[]{:S(2)}, u32[]{:S(2)}) async-start(f32[8,40,16,128]{3,2,1,0:T(8,128)} %get-tuple-element.36), calls=%async_computation.1 | async-start | bytes 5242880 | tf_op jit(solution)/shard_map/all_to_all | solution.py:554
  52.6 2.9 %copy-start.31 = (f32[4,32,128,1,1]{2,1,0,4,3:T(8,128)S(1)}, f32[4,32,128,1,1]{2,1,0,4,3:T(8,128)}, u32[]{:S(2)}) copy-start(f32[4,32,128,1,1]{2,1,0,4,3:T(8,128)} %constant.58) | copy-start | bytes 196612
  56.5 1.4 copy-start.33
  56.6 1.3 copy-start
  57.9 25.7 %copy-start.4 = (bf16[256,256]{1,0:T(8,128)(2,1)S(1)}, bf16[256,256]{1,0:T(8,128)(2,1)}, u32[]{:S(2)}) copy-start(bf16[256,256]{1,0:T(8,128)(2,1)} %constant.46.clone.refs_4_.x_ref.refs_1_.refs_6_) | copy-start | bytes 393220
  57.9 25.7 %copy-start.9 = (bf16[64,1024]{1,0:T(8,128)(2,1)S(1)}, bf16[64,1024]{1,0:T(8,128)(2,1)}, u32[]{:S(2)}) copy-start(bf16[64,1024]{1,0:T(8,128)(2,1)} %constant.50.clone.ghost_ref.refs_2_) | copy-start | bytes 393220
  57.9 25.7 %copy-start.16 = (bf16[512,96]{1,0:T(8,128)(2,1)S(1)}, bf16[512,96]{1,0:T(8,128)(2,1)}, u32[]{:S(2)}) copy-start(bf16[512,96]{1,0:T(8,128)(2,1)} %constant.51.clone.kick_ref) | copy-start | bytes 294916
  57.9 24.7 %collective-permute-start = (f32[16,128,128]{2,1,0:T(8,128)S(1)}, f32[16,128,128]{2,1,0:T(8,128)S(1)}, u32[]{:S(2)}, u32[]{:S(2)}) collective-permute-start(f32[16,128,128]{2,1,0:T(8,128)S(1)} %slice_bitcast_fusion), channel_id=1, source_target_pairs={{0,8},{8,16},{16,24},{24,0},{1,9},{9,17},{17,25},{25,1},{2,10},{10... | collective-permute-start | bytes 3145736 | tf_op jit(solution)/shard_map/ppermute | solution.py:575
  82.6 11.6 %copy-start.7 = (f32[16,128,128]{2,1,0:T(8,128)}, f32[16,128,128]{2,1,0:T(8,128)S(1)}, u32[]{:S(2)}) copy-start(f32[16,128,128]{2,1,0:T(8,128)S(1)} %collective-permute-done.before_ref) | copy-start | bytes 3145732
  83.6 1.6 copy-start.1
  94.3 0.8 copy-start.14
  95.1 1.3 copy-start.5
  96.4 15.0 %collective-permute-start.2 = (f32[8,128,128]{2,1,0:T(8,128)S(1)}, f32[8,128,128]{2,1,0:T(8,128)}, u32[]{:S(2)}, u32[]{:S(2)}) collective-permute-start(f32[8,128,128]{2,1,0:T(8,128)S(1)} %get-tuple-element.78), channel_id=1, source_target_pairs={{0,8},{8,16},{16,24},{1,9},{9,17},{17,25},{2,10},{10,18},{18,26},{... | collective-permute-start | bytes 1572872 | tf_op jit(solution)/shard_map/ppermute | solution.py:597
  97.7 3.0 %copy-start.32 = (f32[4,2,16,128,1]{3,2,0,4,1:T(8,128)S(1)}, f32[4,2,16,128,1]{3,2,0,4,1:T(8,128)}, u32[]{:S(2)}) copy-start(f32[4,2,16,128,1]{3,2,0,4,1:T(8,128)} %constant.57) | copy-start | bytes 196612
  100.7 10.7 %copy-start.8 = (f32[16,128,128]{2,1,0:T(8,128)S(1)}, f32[16,128,128]{2,1,0:T(8,128)}, u32[]{:S(2)}) copy-start(f32[16,128,128]{2,1,0:T(8,128)} %copy-done.7) | copy-start | bytes 3145732
  100.7 10.7 %copy-start.24 = (f32[16,128,128]{2,1,0:T(8,128)S(1)}, f32[16,128,128]{2,1,0:T(8,128)}, u32[]{:S(2)}) copy-start(f32[16,128,128]{2,1,0:T(8,128)} %get-tuple-element.85) | copy-start | bytes 3145732
  101.3 21.2 %collective-permute-start.1 = (f32[8,128,128]{2,1,0:T(8,128)S(1)}, f32[8,128,128]{2,1,0:T(8,128)S(1)}, u32[]{:S(2)}, u32[]{:S(2)}) collective-permute-start(f32[8,128,128]{2,1,0:T(8,128)S(1)} %get-tuple-element.77), channel_id=1, source_target_pairs={{0,8},{8,16},{16,24},{1,9},{9,17},{17,25},{2,10},{10,18},{18,26},{... | collective-permute-start | bytes 1572872 | tf_op jit(solution)/shard_map/ppermute | solution.py:597
  111.4 1.4 copy-start.19
  112.9 9.6 %collective-permute-start.4 = (f32[8,128,128]{2,1,0:T(8,128)S(1)}, f32[8,128,128]{2,1,0:T(8,128)S(1)}, u32[]{:S(2)}, u32[]{:S(2)}) collective-permute-start(f32[8,128,128]{2,1,0:T(8,128)S(1)} %multiply_add_fusion.5), channel_id=1, source_target_pairs={{0,8},{1,9},{2,10},{3,11},{4,12},{5,13},{6,14},{7,15}} | collective-permute-start | bytes 1572872 | tf_op jit(solution)/shard_map/ppermute | solution.py:610
  113.8 25.1 %copy-start.15 = (f32[2,16,4,8,128]{4,3,2,1,0:T(8,128)S(1)}, f32[2,16,4,8,128]{4,3,2,1,0:T(8,128)}, u32[]{:S(2)}) copy-start(f32[2,16,4,8,128]{4,3,2,1,0:T(8,128)} %copy-done.14) | copy-start | bytes 1572868
  113.8 11.2 %collective-permute-start.5 = (f32[8,128,128]{2,1,0:T(8,128)S(1)}, f32[8,128,128]{2,1,0:T(8,128)S(1)}, u32[]{:S(2)}, u32[]{:S(2)}) collective-permute-start(f32[8,128,128]{2,1,0:T(8,128)S(1)} %get-tuple-element.71), channel_id=1, source_target_pairs={{0,4},{4,0},{1,5},{5,1},{2,6},{6,2},{3,7},{7,3},{8,12},{12,8},{9,1... | collective-permute-start | bytes 1572872 | tf_op jit(solution)/shard_map/ppermute | solution.py:620
  122.5 1.4 copy-start.25
  122.5 16.4 %copy-start.6 = (f32[2,16,128,128]{3,2,1,0:T(8,128)S(1)}, f32[2,16,128,128]{3,2,1,0:T(8,128)}, u32[]{:S(2)}) copy-start(f32[2,16,128,128]{3,2,1,0:T(8,128)} %copy-done.5) | copy-start | bytes 6291460
  124.0 14.1 %collective-permute-start.6 = (f32[8,128,128]{2,1,0:T(8,128)S(1)}, f32[8,128,128]{2,1,0:T(8,128)S(1)}, u32[]{:S(2)}, u32[]{:S(2)}) collective-permute-start(f32[8,128,128]{2,1,0:T(8,128)S(1)} %broadcast_select_fusion.2), channel_id=1, source_target_pairs={{0,4},{4,0},{1,5},{5,1},{2,6},{6,2},{3,7},{7,3},{8,12},{12,8},{9,1... | collective-permute-start | bytes 1572872 | tf_op jit(solution)/shard_map/ppermute | solution.py:620
  125.0 13.1 %copy-start.28 = (f32[8,128,128]{2,1,0:T(8,128)}, f32[8,128,128]{2,1,0:T(8,128)S(1)}, u32[]{:S(2)}) copy-start(f32[8,128,128]{2,1,0:T(8,128)S(1)} %collective-permute-done.5) | copy-start | bytes 1572868
  138.1 0.8 copy-start.30
  142.6 1.5 copy-start.2
  144.1 47.0 %all-to-all-start.2 = ((f32[8,40,16,128]{3,2,1,0:T(8,128)}), f32[8,40,16,128]{3,2,1,0:T(8,128)}, u32[]{:S(2)}, u32[]{:S(2)}) async-start(f32[8,40,16,128]{3,2,1,0:T(8,128)} %bitcast.38), calls=%async_computation.2 | async-start | bytes 5242880 | tf_op jit(solution)/shard_map/all_to_all | solution.py:554
  149.7 1.4 collective-permute-start.3
  150.4 0.7 collective-permute-start.8
  151.1 2.9 %copy-start.26 = (f32[8,128,128]{2,1,0:T(8,128)}, f32[8,128,128]{2,1,0:T(8,128)S(1)}, u32[]{:S(2)}) copy-start(f32[8,128,128]{2,1,0:T(8,128)S(1)} %collective-permute-done.3) | copy-start | bytes 1572868
  154.0 37.0 %collective-permute-start.9 = (f32[8,128,128]{2,1,0:T(8,128)S(1)}, f32[8,128,128]{2,1,0:T(8,128)S(1)}, u32[]{:S(2)}, u32[]{:S(2)}) collective-permute-start(f32[8,128,128]{2,1,0:T(8,128)S(1)} %get-tuple-element.52), channel_id=1, source_target_pairs={{16,24},{17,25},{18,26},{19,27},{20,28},{21,29},{22,30},{23,31}} | collective-permute-start | bytes 1572872 | tf_op jit(solution)/shard_map/ppermute | solution.py:610
  156.3 34.7 %copy-start.11 = (f32[8,128,128]{2,1,0:T(8,128)S(1)}, f32[8,128,128]{2,1,0:T(8,128)}, u32[]{:S(2)}) copy-start(f32[8,128,128]{2,1,0:T(8,128)} %get-tuple-element.80.refs_0_) | copy-start | bytes 1572868
  156.3 43.0 %collective-permute-start.7 = (f32[8,128,128]{2,1,0:T(8,128)}, f32[8,128,128]{2,1,0:T(8,128)}, u32[]{:S(2)}, u32[]{:S(2)}) collective-permute-start(f32[8,128,128]{2,1,0:T(8,128)} %get-tuple-element.81), channel_id=1, source_target_pairs={{8,16},{9,17},{10,18},{11,19},{12,20},{13,21},{14,22},{15,23}} | collective-permute-start | bytes 1572872 | tf_op jit(solution)/shard_map/ppermute | solution.py:610
  193.9 5.5 %copy-start.20 = (f32[16,128,128]{2,1,0:T(8,128)S(1)}, f32[16,128,128]{2,1,0:T(8,128)}, u32[]{:S(2)}) copy-start(f32[16,128,128]{2,1,0:T(8,128)} %get-tuple-element.84) | copy-start | bytes 3145732
  193.9 5.5 %copy-start.22 = (f32[8,128,128]{2,1,0:T(8,128)S(1)}, f32[8,128,128]{2,1,0:T(8,128)}, u32[]{:S(2)}) copy-start(f32[8,128,128]{2,1,0:T(8,128)} %get-tuple-element.45) | copy-start | bytes 1572868
  193.9 5.5 %copy-start.27 = (f32[8,128,128]{2,1,0:T(8,128)S(1)}, f32[8,128,128]{2,1,0:T(8,128)}, u32[]{:S(2)}) copy-start(f32[8,128,128]{2,1,0:T(8,128)} %copy-done.26) | copy-start | bytes 1572868
  193.9 25.0 %all-to-all-start.3 = ((f32[8,40,8,128]{3,2,1,0:T(8,128)}), f32[8,40,8,128]{3,2,1,0:T(8,128)}, u32[]{:S(2)}, u32[]{:S(2)}) async-start(f32[8,40,8,128]{3,2,1,0:T(8,128)} %bitcast.18), calls=%async_computation.3 | async-start | bytes 2621440 | tf_op jit(solution)/shard_map/all_to_all | solution.py:554
  199.3 16.7 %copy-start.10 = (f32[8,128,128]{2,1,0:T(8,128)S(1)}, f32[8,128,128]{2,1,0:T(8,128)}, u32[]{:S(2)}) copy-start(f32[8,128,128]{2,1,0:T(8,128)} %get-tuple-element.79.refs_0_) | copy-start | bytes 1572868
  200.6 15.4 %collective-permute-start.10 = (f32[8,128,128]{2,1,0:T(8,128)S(1)}, f32[8,128,128]{2,1,0:T(8,128)S(1)}, u32[]{:S(2)}, u32[]{:S(2)}) collective-permute-start(f32[8,128,128]{2,1,0:T(8,128)S(1)} %get-tuple-element.55), channel_id=1, source_target_pairs={{16,24},{17,25},{18,26},{19,27},{20,28},{21,29},{22,30},{23,31}} | collective-permute-start | bytes 1572872 | tf_op jit(solution)/shard_map/ppermute | solution.py:610
  218.9 4.8 %copy-start.29 = (f32[8,128,128]{2,1,0:T(8,128)S(1)}, f32[8,128,128]{2,1,0:T(8,128)}, u32[]{:S(2)}) copy-start(f32[8,128,128]{2,1,0:T(8,128)} %copy-done.28) | copy-start | bytes 1572868
  218.9 6.0 %copy-start.23 = (f32[16,128,128]{2,1,0:T(8,128)S(1)}, f32[16,128,128]{2,1,0:T(8,128)}, u32[]{:S(2)}) copy-start(f32[16,128,128]{2,1,0:T(8,128)} %maximum_select_fusion) | copy-start | bytes 3145732
  218.9 21.7 %all-to-all-start.4 = ((f32[8,40,8,128]{3,2,1,0:T(8,128)}), f32[8,40,8,128]{3,2,1,0:T(8,128)S(1)}, u32[]{:S(2)}, u32[]{:S(2)}) async-start(f32[8,40,8,128]{3,2,1,0:T(8,128)} %bitcast.19), calls=%async_computation.4 | async-start | bytes 2621440 | tf_op jit(solution)/shard_map/all_to_all | solution.py:554
  240.6 1.1 copy-start.21

commit v5 on v4

--- a/solution.py
+++ b/solution.py
@@ -201,7 +201,7 @@
             pl.BlockSpec((None, own, n_space, 2 * steps, width_z), lambda b: (b, 0, 0, 0, 0)),
         ),
         cost_estimate=cost(arrived, before),
-        compiler_params=room(40),
+        compiler_params=room(60),
     )(arrived.reshape(n_space, 2, total * own, width_z), before, guess, spectrum, *tables)
 
 
@@ -275,7 +275,7 @@
         ],
         out_specs=pl.BlockSpec((n_space, None, total * own, width_z), lambda b: (0, b, 0, 0)),
         cost_estimate=cost(spectrum, spectrum),
-        compiler_params=room(40),
+        compiler_params=room(60),
     )(spectrum, *tables, *evens, *others)
     return out.reshape(2 * n_space, total, own, width_z)
 

time: 258 us -> 263 us (1.019)
  Pallas kernels: 51.1 us -> 59.4 us
  local copies, waits for them, and re-layouts: 25.8 us -> 22.7 us
  waiting for transfers between devices: 131 us -> 128 us
    pallas_call x3, Pallas kernels: 9.31 us -> 15.2 us  [to_cells(): pl.pallas_call(lambda *refs: cells_kernel(wide_weight, len(evens), *refs)...]
    unnamed x70 -> x46, local copies, waits for them, and re-layouts: 17.7 us -> 13.3 us
  transfers between devices with their start and end apart: 16 -> 16, of which waited for: 10 -> 9; matrix products, arithmetic and copies ran while one was open for 9% -> 10% of each run, Pallas kernels for 7% -> 8%
where the time goes in v5:
time: 263 us; the launch traced here: 262 us
  waiting for transfers between devices  128 us (49%)
  Pallas kernels  59.4 us (23%)
  starting transfers between devices  37.1 us (14%)
  local copies, waits for them, and re-layouts  22.7 us (9%)
  other arithmetic  12.8 us (5%)
    ppermute x6, waiting for transfers between devices, hop(): return lax.ppermute(sent, 'plane', [(place, place + 1)])  45.9 us
    all_to_all x5, waiting for transfers between devices, swap(): lax.all_to_all(fields, ('space', 'pair'), split_axis=0, concat_axis=0, ti...  30.8 us
    all_to_all x5, starting transfers between devices, swap(): lax.all_to_all(fields, ('space', 'pair'), split_axis=0, concat_axis=0, ti...  26.2 us
    ppermute x1, waiting for transfers between devices, per_device(): lax.ppermute(guess[1], 'plane', [(i, (i + 1) % n_plane) for i in range(n_...  22.2 us
    ppermute x2, waiting for transfers between devices, per_device(): lax.ppermute(chunk_of(value[1], c), 'plane', [(i, i + 1) for i in range(n...  15.5 us
    pallas_call x1, Pallas kernels, finish(): pl.pallas_call(lambda *refs: finish_kernel(q_steps, *refs), grid=(q_steps...  15.5 us
    pallas_call x3, Pallas kernels, to_cells(): pl.pallas_call(lambda *refs: cells_kernel(wide_weight, len(evens), *refs)...  15.2 us
    unnamed x46, local copies, waits for them, and re-layouts  13.3 us
  transfers between devices with their start and end apart: 16, of which 9 were waited for; matrix products, arithmetic and copies ran while one was open for 10% of the time, Pallas kernels for 8%

profile of v5, /device:TPU:25, one launch (start us, length us, event | category | flops | bytes accessed | tf_op | source)
XLA Modules:
  0.0 262.2 jit_solution(17829259561242028147)
XLA Ops:
  0.6 5.3 %shard_map.167 = f32[8,48,16,128]{3,2,1,0:T(8,128)} custom-call(s32[1]{0:T(128)} %bitcast.refs_0_, f32[32,128,128]{2,1,0:T(8,128)} %bitcast.42, f32[32,128,128]{2,1,0:T(8,128)} %refs_2_.5, bf16[256,256]{1,0:T(8,128)(2,1)} %constant.45.clone.refs_3_.refs_1_.refs_7_, bf16[256,256]{1,0:T(8,128)(2,1)} %constant.46.clone.refs_4_.x_ref.refs_1_.refs_6_), custom_call_target="tpu_custom_call" | custom-call | flops 838860800 | bytes 4194304 | tf_op jit(solution)/shard_map/pallas_call | solution.py:401
  6.0 5.2 %all-to-all-start = ((f32[8,48,16,128]{3,2,1,0:T(8,128)}), f32[8,48,16,128]{3,2,1,0:T(8,128)}, u32[]{:S(2)}, u32[]{:S(2)}) async-start(f32[8,48,16,128]{3,2,1,0:T(8,128)} %shard_map.167), calls=%async_computation | async-start | bytes 6291456 | tf_op jit(solution)/shard_map/all_to_all | solution.py:554
  11.2 3.4 %copy-done.3 = f32[4,32,128,128]{3,2,1,0:T(8,128)S(1)} copy-done((f32[4,32,128,128]{3,2,1,0:T(8,128)S(1)}, f32[4,32,128,128]{3,2,1,0:T(8,128)}, u32[]{:S(2)}) %copy-start.3) | copy-done | bytes 8388632
  14.6 11.9 %shard_map.168 = (f32[4,32,128,128]{3,2,1,0:T(8,128)S(1)}, f32[8,40,16,128]{3,2,1,0:T(8,128)}) custom-call(f32[4,32,128,128]{3,2,1,0:T(8,128)S(1)} %copy-done.3, bf16[256,256]{1,0:T(8,128)(2,1)S(1)} %copy-done.2, bf16[256,256]{1,0:T(8,128)(2,1)S(1)} %copy-done.4, f32[17,8,16,128]{3,2,1,0:T(8,128)S(1)} %copy-done.1), custom_call_target="tpu_custom_call" | custom-call | flops 3355443200 | bytes 16777216 | tf_op jit(solution)/shard_map/pallas_call | solution.py:360
  26.5 3.3 %copy-done = f32[4,32,128,128]{3,2,1,0:T(8,128)} copy-done((f32[4,32,128,128]{3,2,1,0:T(8,128)}, f32[4,32,128,128]{3,2,1,0:T(8,128)S(1)}, u32[]{:S(2)}) %copy-start) | copy-done | bytes 8388632
  29.7 18.1 %all-to-all-done = f32[8,48,16,128]{3,2,1,0:T(8,128)} async-done(((f32[8,48,16,128]{3,2,1,0:T(8,128)}), f32[8,48,16,128]{3,2,1,0:T(8,128)}, u32[]{:S(2)}, u32[]{:S(2)}) %all-to-all-start) | async-done | bytes 3145760 | tf_op jit(solution)/shard_map/all_to_all | solution.py:554
  47.8 4.8 %all-to-all-start.1 = ((f32[8,40,16,128]{3,2,1,0:T(8,128)}), f32[8,40,16,128]{3,2,1,0:T(8,128)}, u32[]{:S(2)}, u32[]{:S(2)}) async-start(f32[8,40,16,128]{3,2,1,0:T(8,128)} %get-tuple-element.36), calls=%async_computation.1 | async-start | bytes 5242880 | tf_op jit(solution)/shard_map/all_to_all | solution.py:554
  52.6 2.9 %copy.20 = f32[4,2,48,16,128]{4,2,0,3,1:T(8,128)S(1)} copy(f32[4,2,48,16,128]{4,3,2,1,0:T(8,128)} %bitcast.2) | data formatting | bytes 6291456 | tf_op jit(solution)/shard_map/optimization_barrier | solution.py:571
  55.4 1.0 fusion.2.guess_ref
  56.5 0.0 copy-start.9
  56.5 1.3 copy-done.9
  57.8 0.1 slice_bitcast_fusion
  57.9 0.1 collective-permute-start
  58.0 0.5 copy-done.21
  58.5 0.1 dynamic_slice.3
  58.5 0.1 broadcast_add_fusion.1
  58.6 1.8 fusion.8
  60.5 22.2 %collective-permute-done.before_ref = f32[16,128,128]{2,1,0:T(8,128)S(1)} collective-permute-done((f32[16,128,128]{2,1,0:T(8,128)S(1)}, f32[16,128,128]{2,1,0:T(8,128)S(1)}, u32[]{:S(2)}, u32[]{:S(2)}) %collective-permute-start) | collective-permute-done | bytes 1048608 | tf_op jit(solution)/shard_map/ppermute | solution.py:575
  82.7 0.9 all-to-all-done.1
  83.6 0.1 copy-done.13
  83.7 11.5 %shard_map.169 = (f32[2,16,128,128]{3,2,1,0:T(8,128)}, f32[16,128,128]{2,1,0:T(8,128)}, f32[2,16,4,8,128]{4,3,2,1,0:T(8,128)}) custom-call(f32[4,2,640,128]{3,2,1,0:T(8,128)} %bitcast.7.arrived_ref, f32[16,128,128]{2,1,0:T(8,128)} %copy-done.13, f32[2,16,128,128]{3,2,1,0:T(8,128)} %copy-done.9, f32[16,128,128]{2,1,0:T(8,128)} %get-tuple-element.86.spectrum_ref.refs_0_, ...), custom_call_target="tpu_custom_call" | custom-call | flops 1468006400 | bytes 7340032 | tf_op jit(solution)/shard_map/pallas_call | solution.py:183
  95.2 1.3 slice_bitcast_fusion.2
  96.4 1.3 collective-permute-start.2
  97.8 0.0 copy-start.20
  97.8 3.0 %copy.18 = f32[4,2,48,16,128]{4,2,0,1,3:T(8,128)S(1)} copy(f32[4,2,48,16,128]{4,3,2,1,0:T(8,128)} %bitcast.2) | data formatting | bytes 6291456 | tf_op jit(solution)/shard_map/optimization_barrier | solution.py:571
  100.8 0.6 convolution_bitcast_fusion
  101.4 1.3 collective-permute-start.1
  102.7 8.3 %collective-permute-done.2 = f32[8,128,128]{2,1,0:T(8,128)} collective-permute-done((f32[8,128,128]{2,1,0:T(8,128)S(1)}, f32[8,128,128]{2,1,0:T(8,128)}, u32[]{:S(2)}, u32[]{:S(2)}) %collective-permute-start.2) | collective-permute-done | bytes 524320 | tf_op jit(solution)/shard_map/ppermute | solution.py:597
  111.1 2.1 slice_select_fusion.2
  113.1 0.1 multiply_add_fusion.5
  113.2 0.9 collective-permute-start.4
  114.1 0.9 collective-permute-start.5
  115.0 7.2 %collective-permute-done.1 = f32[8,128,128]{2,1,0:T(8,128)S(1)} collective-permute-done((f32[8,128,128]{2,1,0:T(8,128)S(1)}, f32[8,128,128]{2,1,0:T(8,128)S(1)}, u32[]{:S(2)}, u32[]{:S(2)}) %collective-permute-start.1) | collective-permute-done | bytes 524320 | tf_op jit(solution)/shard_map/ppermute | solution.py:597
  122.3 1.7 multiply_add_fusion.4
  124.0 0.1 broadcast_select_fusion.2
  124.0 0.9 collective-permute-start.6
  125.0 13.2 %collective-permute-done.6 = f32[8,128,128]{2,1,0:T(8,128)} collective-permute-done((f32[8,128,128]{2,1,0:T(8,128)S(1)}, f32[8,128,128]{2,1,0:T(8,128)}, u32[]{:S(2)}, u32[]{:S(2)}) %collective-permute-start.6) | collective-permute-done | bytes 524320 | tf_op jit(solution)/shard_map/ppermute | solution.py:620
  138.2 6.7 %shard_map.170 = f32[4,2,640,128]{3,2,1,0:T(8,128)} custom-call(f32[16,128,128]{2,1,0:T(8,128)} %get-tuple-element.86.spectrum_ref.refs_0_, bf16[256,256]{1,0:T(8,128)(2,1)} %constant.46.clone.refs_4_.x_ref.refs_1_.refs_6_, bf16[64,1024]{1,0:T(8,128)(2,1)} %constant.50.clone.ghost_ref.refs_2_, f32[8,128,128]{2,1,0:T(8,128)} %get-tuple-element.48.refs_3_, ...), custom_call_target="tpu_custom_call" | custom-call | flops 838860800 | bytes 4194304 | tf_op jit(solution)/shard_map/pallas_call | solution.py:266
  144.9 6.0 %all-to-all-start.2 = ((f32[8,40,16,128]{3,2,1,0:T(8,128)}), f32[8,40,16,128]{3,2,1,0:T(8,128)}, u32[]{:S(2)}, u32[]{:S(2)}) async-start(f32[8,40,16,128]{3,2,1,0:T(8,128)} %bitcast.39), calls=%async_computation.2 | async-start | bytes 5242880 | tf_op jit(solution)/shard_map/all_to_all | solution.py:554
  150.8 0.8 collective-permute-start.3
  151.7 0.7 collective-permute-start.8
  152.4 2.5 multiply_add_fusion
  154.9 1.3 collective-permute-start.9
  156.2 1.0 fusion.13
  157.3 1.4 collective-permute-start.7
  158.7 1.1 maximum_select_fusion
  159.8 31.8 %collective-permute-done.9 = f32[8,128,128]{2,1,0:T(8,128)S(1)} collective-permute-done((f32[8,128,128]{2,1,0:T(8,128)S(1)}, f32[8,128,128]{2,1,0:T(8,128)S(1)}, u32[]{:S(2)}, u32[]{:S(2)}) %collective-permute-start.9) | collective-permute-done | bytes 524320 | tf_op jit(solution)/shard_map/ppermute | solution.py:610
  191.6 0.9 add.115.refs_3_
  192.5 4.2 %shard_map.171 = f32[4,2,320,128]{3,2,1,0:T(8,128)} custom-call(f32[8,128,128]{2,1,0:T(8,128)} %get-tuple-element.80.refs_0_, bf16[256,256]{1,0:T(8,128)(2,1)} %constant.46.clone.refs_4_.x_ref.refs_1_.refs_6_, bf16[64,1024]{1,0:T(8,128)(2,1)} %constant.50.clone.ghost_ref.refs_2_, f32[8,128,128]{2,1,0:T(8,128)} %add.115.refs_3_, f32[8,128,128]{2,1,0:T(8,128)} %copy-done.6), custom_call_target="tpu_custom_call" | custom-call | flops 419430400 | bytes 2097152 | tf_op jit(solution)/shard_map/pallas_call | solution.py:266
  196.7 5.4 %all-to-all-start.3 = ((f32[8,40,8,128]{3,2,1,0:T(8,128)}), f32[8,40,8,128]{3,2,1,0:T(8,128)}, u32[]{:S(2)}, u32[]{:S(2)}) async-start(f32[8,40,8,128]{3,2,1,0:T(8,128)} %bitcast.40), calls=%async_computation.3 | async-start | bytes 2621440 | tf_op jit(solution)/shard_map/all_to_all | solution.py:554
  202.2 1.2 multiply_add_fusion.1
  203.4 1.3 collective-permute-start.10
  204.7 14.1 %collective-permute-done.10 = f32[8,128,128]{2,1,0:T(8,128)S(1)} collective-permute-done((f32[8,128,128]{2,1,0:T(8,128)S(1)}, f32[8,128,128]{2,1,0:T(8,128)S(1)}, u32[]{:S(2)}, u32[]{:S(2)}) %collective-permute-start.10) | collective-permute-done | bytes 524320 | tf_op jit(solution)/shard_map/ppermute | solution.py:610
  218.8 0.9 add.116.refs_3_
  219.7 4.2 %shard_map.172 = f32[4,2,320,128]{3,2,1,0:T(8,128)} custom-call(f32[8,128,128]{2,1,0:T(8,128)} %get-tuple-element.79.refs_0_, bf16[256,256]{1,0:T(8,128)(2,1)} %constant.46.clone.refs_4_.x_ref.refs_1_.refs_6_, bf16[64,1024]{1,0:T(8,128)(2,1)} %constant.50.clone.ghost_ref.refs_2_, f32[8,128,128]{2,1,0:T(8,128)} %add.116.refs_3_, f32[8,128,128]{2,1,0:T(8,128)} %copy-done.5), custom_call_target="tpu_custom_call" | custom-call | flops 419430400 | bytes 2097152 | tf_op jit(solution)/shard_map/pallas_call | solution.py:266
  223.9 4.8 %all-to-all-start.4 = ((f32[8,40,8,128]{3,2,1,0:T(8,128)}), f32[8,40,8,128]{3,2,1,0:T(8,128)S(1)}, u32[]{:S(2)}, u32[]{:S(2)}) async-start(f32[8,40,8,128]{3,2,1,0:T(8,128)} %bitcast.41), calls=%async_computation.4 | async-start | bytes 2621440 | tf_op jit(solution)/shard_map/all_to_all | solution.py:554
  228.8 1.1 constant_dynamic-update-slice_fusion.1
  229.8 1.1 constant_dynamic-update-slice_fusion
  230.9 0.2 broadcast_select_fusion.1
  231.1 0.2 maximum_bitcast_fusion
  231.3 2.5 copy.22
  233.9 11.8 %all-to-all-done.4.refs_3_ = f32[8,40,8,128]{3,2,1,0:T(8,128)S(1)} async-done(((f32[8,40,8,128]{3,2,1,0:T(8,128)}), f32[8,40,8,128]{3,2,1,0:T(8,128)S(1)}, u32[]{:S(2)}, u32[]{:S(2)}) %all-to-all-start.4) | async-done | bytes 1310752 | tf_op jit(solution)/shard_map/all_to_all | solution.py:554
  245.6 1.0 copy-done.10
  246.7 15.5 %shard_map.173 = f32[4,32,128,128]{3,2,1,0:T(8,128)} custom-call(f32[4,32,8,16,128]{4,3,2,1,0:T(8,128)} %bitcast.38, f32[8,40,16,128]{3,2,1,0:T(8,128)} %all-to-all-done.2.refs_1_, f32[8,40,8,128]{3,2,1,0:T(8,128)} %all-to-all-done.3.refs_2_, f32[8,40,8,128]{3,2,1,0:T(8,128)} %copy-done.10, f32[17,8,16,128]{3,2,1,0:T(8,128)} %constant.49.clone.refs_3_.refs_4_, ...), custom_call_target="tpu_custom_call" | custom-call | flops 3355443200 | bytes 16777216 | tf_op jit(solution)/shard_map/pallas_call | solution.py:494
  (43 shorter events, 0.1 us)
Async XLA Ops:
  6.0 5.2 %copy-start.1 = (f32[17,8,16,128]{3,2,1,0:T(8,128)S(1)}, f32[17,8,16,128]{3,2,1,0:T(8,128)}, u32[]{:S(2)}) copy-start(f32[17,8,16,128]{3,2,1,0:T(8,128)} %constant.49.clone.refs_3_.refs_4_) | copy-start | bytes 3342340
  6.0 5.2 %copy-start.2 = (bf16[256,256]{1,0:T(8,128)(2,1)S(1)}, bf16[256,256]{1,0:T(8,128)(2,1)}, u32[]{:S(2)}) copy-start(bf16[256,256]{1,0:T(8,128)(2,1)} %constant.45.clone.refs_3_.refs_1_.refs_7_) | copy-start | bytes 393220
  6.0 5.2 %copy-start.4 = (bf16[256,256]{1,0:T(8,128)(2,1)S(1)}, bf16[256,256]{1,0:T(8,128)(2,1)}, u32[]{:S(2)}) copy-start(bf16[256,256]{1,0:T(8,128)(2,1)} %constant.47.clone.refs_2_) | copy-start | bytes 393220
  6.0 41.8 %all-to-all-start = ((f32[8,48,16,128]{3,2,1,0:T(8,128)}), f32[8,48,16,128]{3,2,1,0:T(8,128)}, u32[]{:S(2)}, u32[]{:S(2)}) async-start(f32[8,48,16,128]{3,2,1,0:T(8,128)} %shard_map.167), calls=%async_computation | async-start | bytes 6291456 | tf_op jit(solution)/shard_map/all_to_all | solution.py:554
  11.2 3.4 %copy-start.3 = (f32[4,32,128,128]{3,2,1,0:T(8,128)S(1)}, f32[4,32,128,128]{3,2,1,0:T(8,128)}, u32[]{:S(2)}) copy-start(f32[4,32,128,128]{3,2,1,0:T(8,128)} %refs_0_) | copy-start | bytes 25165828
  26.5 3.3 %copy-start = (f32[4,32,128,128]{3,2,1,0:T(8,128)}, f32[4,32,128,128]{3,2,1,0:T(8,128)S(1)}, u32[]{:S(2)}) copy-start(f32[4,32,128,128]{3,2,1,0:T(8,128)S(1)} %get-tuple-element.47) | copy-start | bytes 25165828
  47.8 35.8 %all-to-all-start.1 = ((f32[8,40,16,128]{3,2,1,0:T(8,128)}), f32[8,40,16,128]{3,2,1,0:T(8,128)}, u32[]{:S(2)}, u32[]{:S(2)}) async-start(f32[8,40,16,128]{3,2,1,0:T(8,128)} %get-tuple-element.36), calls=%async_computation.1 | async-start | bytes 5242880 | tf_op jit(solution)/shard_map/all_to_all | solution.py:554
  52.6 2.9 %copy-start.19 = (f32[4,32,128,1,1]{2,1,0,4,3:T(8,128)S(1)}, f32[4,32,128,1,1]{2,1,0,4,3:T(8,128)}, u32[]{:S(2)}) copy-start(f32[4,32,128,1,1]{2,1,0,4,3:T(8,128)} %constant.58) | copy-start | bytes 196612
  56.5 1.3 copy-start.9
  57.8 0.7 copy-start.21
  57.9 24.8 %collective-permute-start = (f32[16,128,128]{2,1,0:T(8,128)S(1)}, f32[16,128,128]{2,1,0:T(8,128)S(1)}, u32[]{:S(2)}, u32[]{:S(2)}) collective-permute-start(f32[16,128,128]{2,1,0:T(8,128)S(1)} %slice_bitcast_fusion), channel_id=1, source_target_pairs={{0,8},{8,16},{16,24},{24,0},{1,9},{9,17},{17,25},{25,1},{2,10},{10... | collective-permute-start | bytes 3145736 | tf_op jit(solution)/shard_map/ppermute | solution.py:575
  82.7 1.0 copy-start.13
  96.4 14.6 %collective-permute-start.2 = (f32[8,128,128]{2,1,0:T(8,128)S(1)}, f32[8,128,128]{2,1,0:T(8,128)}, u32[]{:S(2)}, u32[]{:S(2)}) collective-permute-start(f32[8,128,128]{2,1,0:T(8,128)S(1)} %get-tuple-element.78), channel_id=1, source_target_pairs={{0,8},{8,16},{16,24},{1,9},{9,17},{17,25},{2,10},{10,18},{18,26},{... | collective-permute-start | bytes 1572872 | tf_op jit(solution)/shard_map/ppermute | solution.py:597
  97.8 3.0 %copy-start.20 = (f32[4,2,16,128,1]{3,2,0,4,1:T(8,128)S(1)}, f32[4,2,16,128,1]{3,2,0,4,1:T(8,128)}, u32[]{:S(2)}) copy-start(f32[4,2,16,128,1]{3,2,0,4,1:T(8,128)} %constant.57) | copy-start | bytes 196612
  97.8 13.3 %copy-start.15 = (f32[16,128,128]{2,1,0:T(8,128)S(1)}, f32[16,128,128]{2,1,0:T(8,128)}, u32[]{:S(2)}) copy-start(f32[16,128,128]{2,1,0:T(8,128)} %get-tuple-element.85) | copy-start | bytes 3145732
  100.8 10.3 %copy-start.7 = (f32[16,128,128]{2,1,0:T(8,128)S(1)}, f32[16,128,128]{2,1,0:T(8,128)}, u32[]{:S(2)}) copy-start(f32[16,128,128]{2,1,0:T(8,128)} %get-tuple-element.38) | copy-start | bytes 3145732
  100.8 10.3 %copy-start.14 = (f32[16,128,128]{2,1,0:T(8,128)S(1)}, f32[16,128,128]{2,1,0:T(8,128)}, u32[]{:S(2)}) copy-start(f32[16,128,128]{2,1,0:T(8,128)} %copy-done.13) | copy-start | bytes 3145732
  101.4 20.8 %collective-permute-start.1 = (f32[8,128,128]{2,1,0:T(8,128)S(1)}, f32[8,128,128]{2,1,0:T(8,128)S(1)}, u32[]{:S(2)}, u32[]{:S(2)}) collective-permute-start(f32[8,128,128]{2,1,0:T(8,128)S(1)} %get-tuple-element.77), channel_id=1, source_target_pairs={{0,8},{8,16},{16,24},{1,9},{9,17},{17,25},{2,10},{10,18},{18,26},{... | collective-permute-start | bytes 1572872 | tf_op jit(solution)/shard_map/ppermute | solution.py:597
  113.1 45.6 %copy-start.6 = (f32[8,128,128]{2,1,0:T(8,128)}, f32[8,128,128]{2,1,0:T(8,128)S(1)}, u32[]{:S(2)}) copy-start(f32[8,128,128]{2,1,0:T(8,128)S(1)} %get-tuple-element.53.refs_4_) | copy-start | bytes 1572868
  113.2 9.1 %collective-permute-start.4 = (f32[8,128,128]{2,1,0:T(8,128)S(1)}, f32[8,128,128]{2,1,0:T(8,128)S(1)}, u32[]{:S(2)}, u32[]{:S(2)}) collective-permute-start(f32[8,128,128]{2,1,0:T(8,128)S(1)} %multiply_add_fusion.5), channel_id=1, source_target_pairs={{0,8},{1,9},{2,10},{3,11},{4,12},{5,13},{6,14},{7,15}} | collective-permute-start | bytes 1572872 | tf_op jit(solution)/shard_map/ppermute | solution.py:610
  114.1 10.8 %collective-permute-start.5 = (f32[8,128,128]{2,1,0:T(8,128)S(1)}, f32[8,128,128]{2,1,0:T(8,128)}, u32[]{:S(2)}, u32[]{:S(2)}) collective-permute-start(f32[8,128,128]{2,1,0:T(8,128)S(1)} %get-tuple-element.71), channel_id=1, source_target_pairs={{0,4},{4,0},{1,5},{5,1},{2,6},{6,2},{3,7},{7,3},{8,12},{12,8},{9,1... | collective-permute-start | bytes 1572872 | tf_op jit(solution)/shard_map/ppermute | solution.py:620
  122.3 1.7 copy-start.16
  124.0 78.2 %copy-start.5 = (f32[8,128,128]{2,1,0:T(8,128)}, f32[8,128,128]{2,1,0:T(8,128)S(1)}, u32[]{:S(2)}) copy-start(f32[8,128,128]{2,1,0:T(8,128)S(1)} %get-tuple-element.56.refs_4_) | copy-start | bytes 1572868
  124.0 14.2 %collective-permute-start.6 = (f32[8,128,128]{2,1,0:T(8,128)S(1)}, f32[8,128,128]{2,1,0:T(8,128)}, u32[]{:S(2)}, u32[]{:S(2)}) collective-permute-start(f32[8,128,128]{2,1,0:T(8,128)S(1)} %broadcast_select_fusion.2), channel_id=1, source_target_pairs={{0,4},{4,0},{1,5},{5,1},{2,6},{6,2},{3,7},{7,3},{8,12},{12,8},{9,1... | collective-permute-start | bytes 1572872 | tf_op jit(solution)/shard_map/ppermute | solution.py:620
  144.9 47.6 %all-to-all-start.2 = ((f32[8,40,16,128]{3,2,1,0:T(8,128)}), f32[8,40,16,128]{3,2,1,0:T(8,128)}, u32[]{:S(2)}, u32[]{:S(2)}) async-start(f32[8,40,16,128]{3,2,1,0:T(8,128)} %bitcast.39), calls=%async_computation.2 | async-start | bytes 5242880 | tf_op jit(solution)/shard_map/all_to_all | solution.py:554
  150.8 5.4 %copy-start.8 = (f32[16,128,128]{2,1,0:T(8,128)S(1)}, f32[16,128,128]{2,1,0:T(8,128)}, u32[]{:S(2)}) copy-start(f32[16,128,128]{2,1,0:T(8,128)} %get-tuple-element.86.spectrum_ref.refs_0_) | copy-start | bytes 3145732
  150.8 1.5 collective-permute-start.3
  151.7 0.7 collective-permute-start.8
  152.4 2.6 copy-start.17
  154.9 36.7 %collective-permute-start.9 = (f32[8,128,128]{2,1,0:T(8,128)S(1)}, f32[8,128,128]{2,1,0:T(8,128)S(1)}, u32[]{:S(2)}, u32[]{:S(2)}) collective-permute-start(f32[8,128,128]{2,1,0:T(8,128)S(1)} %get-tuple-element.52), channel_id=1, source_target_pairs={{16,24},{17,25},{18,26},{19,27},{20,28},{21,29},{22,30},{23,31}} | collective-permute-start | bytes 1572872 | tf_op jit(solution)/shard_map/ppermute | solution.py:610
  157.3 44.9 %collective-permute-start.7 = (f32[8,128,128]{2,1,0:T(8,128)}, f32[8,128,128]{2,1,0:T(8,128)}, u32[]{:S(2)}, u32[]{:S(2)}) collective-permute-start(f32[8,128,128]{2,1,0:T(8,128)} %get-tuple-element.81), channel_id=1, source_target_pairs={{8,16},{9,17},{10,18},{11,19},{12,20},{13,21},{14,22},{15,23}} | collective-permute-start | bytes 1572872 | tf_op jit(solution)/shard_map/ppermute | solution.py:610
  196.7 5.5 %copy-start.11 = (f32[8,128,128]{2,1,0:T(8,128)S(1)}, f32[8,128,128]{2,1,0:T(8,128)}, u32[]{:S(2)}) copy-start(f32[8,128,128]{2,1,0:T(8,128)} %get-tuple-element.45) | copy-start | bytes 1572868
  196.7 5.5 %copy-start.18 = (f32[8,128,128]{2,1,0:T(8,128)S(1)}, f32[8,128,128]{2,1,0:T(8,128)}, u32[]{:S(2)}) copy-start(f32[8,128,128]{2,1,0:T(8,128)} %copy-done.17) | copy-start | bytes 1572868
  196.7 27.2 %all-to-all-start.3 = ((f32[8,40,8,128]{3,2,1,0:T(8,128)}), f32[8,40,8,128]{3,2,1,0:T(8,128)}, u32[]{:S(2)}, u32[]{:S(2)}) async-start(f32[8,40,8,128]{3,2,1,0:T(8,128)} %bitcast.40), calls=%async_computation.3 | async-start | bytes 2621440 | tf_op jit(solution)/shard_map/all_to_all | solution.py:554
  203.4 15.4 %collective-permute-start.10 = (f32[8,128,128]{2,1,0:T(8,128)S(1)}, f32[8,128,128]{2,1,0:T(8,128)S(1)}, u32[]{:S(2)}, u32[]{:S(2)}) collective-permute-start(f32[8,128,128]{2,1,0:T(8,128)S(1)} %get-tuple-element.55), channel_id=1, source_target_pairs={{16,24},{17,25},{18,26},{19,27},{20,28},{21,29},{22,30},{23,31}} | collective-permute-start | bytes 1572872 | tf_op jit(solution)/shard_map/ppermute | solution.py:610
  223.9 7.0 %copy-start.12 = (f32[16,128,128]{2,1,0:T(8,128)S(1)}, f32[16,128,128]{2,1,0:T(8,128)}, u32[]{:S(2)}) copy-start(f32[16,128,128]{2,1,0:T(8,128)} %maximum_select_fusion) | copy-start | bytes 3145732
  223.9 21.7 %all-to-all-start.4 = ((f32[8,40,8,128]{3,2,1,0:T(8,128)}), f32[8,40,8,128]{3,2,1,0:T(8,128)S(1)}, u32[]{:S(2)}, u32[]{:S(2)}) async-start(f32[8,40,8,128]{3,2,1,0:T(8,128)} %bitcast.41), calls=%async_computation.4 | async-start | bytes 2621440 | tf_op jit(solution)/shard_map/all_to_all | solution.py:554
  245.6 1.0 copy-start.10
